TPU v7x, 32 devices: a whole 2x2x4 slice. The times are simulated.
32 devices in a mesh: groups: 2 (over y), seq: 4 (over z), head: 2 (over x), fsdp: 2 (over core).
Axes of the slice: x: 2, y: 2, z: 4, core: 2. Of those that a mesh axis runs over, the one named last changes fastest.
Arguments:
- residual_in: bfloat16 [16384, 2048], P(('groups', 'seq', 'fsdp'), 'head'), parts along dimension 0, may hold values from -6 to 6
- query_rows: bfloat16 [16384, 2048], P(('groups', 'seq', 'fsdp'), 'head'), parts along dimension 0, may hold values from -7 to 7
- key_rows: bfloat16 [16384, 2048], P(('groups', 'seq', 'fsdp'), 'head'), parts along dimension 0, may hold values from -7 to 7
- value_rows: bfloat16 [16384, 2048], P(('groups', 'seq', 'fsdp'), 'head'), parts along dimension 0, may hold values from -6 to 6
- bc_weight: bfloat16 [2048, 256], P(('head', 'fsdp')), may hold values from -0.125 to 0.125
- decay_rate: float32 [16384, 32], P(('groups', 'seq', 'fsdp'), 'head'), parts along dimension 0, may hold values from 0 to 0.8
- level_codes: int32 [16384, 18], P(('groups', 'seq', 'fsdp')), parts along dimension 0, may hold values from 0 to 255
- level_scale: float32 [18], replicated, may hold values from 0.05 to 1
- positions: int32 [16384], P(('groups', 'seq', 'fsdp')), parts along dimension 0, may hold values from 0 to 2047, as said below
- ssm_gain: float32 [2048], P('head'), may hold values from 0.25 to 1.75
Outputs:
- mixed_out: bfloat16 [16384, 2048], P(('groups', 'seq', 'fsdp'), 'head'), parts along dimension 0
There are 2 independent parts, one for each index of `groups`. A program takes and returns all parts, laid end to end along the dimension named above; an argument that names none is the same for every part. Nothing has to cross between parts.
Inputs may be any that keep to these rules, and one draw needn't show every extreme that they name: positions[t] is 0 where a document begins (always at t = 0) and positions[t - 1] + 1 elsewhere.
All inputs are finite; a program needn't handle non-finite values.
Results may differ from a plain program's by a relative error of at most 0.008.
Values may be sent and summed in bfloat16 or wider, within the bound.
No kernel may reach another device: no remote copies, remote signals or barrier semaphores. Data moves between devices by JAX's collectives and lax.ppermute only.
A program may use at most 64 MiB of HBM per device.

v0:
```python
import math

import jax
import jax.numpy as jnp
from jax import lax
from jax.sharding import PartitionSpec as P

HEAD_DIM = 128
HEAD_VALUES = 64
STATES = 128
WINDOW = 128


def from_behind(x, axis, by):
    length = lax.axis_size(axis)
    pairs = [(i, i + by) for i in range(length) if 0 <= i + by < length]
    return lax.ppermute(x, axis, pairs)


def partner(x, axis, distance):
    return lax.ppermute(x, axis, [(i, i ^ 1 << distance) for i in range(lax.axis_size(axis))])


def widen(vector, repeat_count):
    return jnp.repeat(vector, repeat_count, axis=-1)


def window_attention(query_rows, key_rows, value_rows, edge_keys, edge_values, positions):
    row_count, local_width = query_rows.shape
    head_count = local_width // HEAD_DIM
    block_total = row_count // WINDOW
    key_blocks = jnp.concatenate([edge_keys, key_rows], axis=0).reshape(
        block_total + 1, WINDOW, head_count, HEAD_DIM
    )
    value_blocks = jnp.concatenate([edge_values, value_rows], axis=0).reshape(
        block_total + 1, WINDOW, head_count, HEAD_DIM
    )
    key_pairs = jnp.concatenate([key_blocks[:block_total], key_blocks[1:]], axis=1)
    value_pairs = jnp.concatenate([value_blocks[:block_total], value_blocks[1:]], axis=1)
    query_blocks = query_rows.reshape(block_total, WINDOW, head_count, HEAD_DIM)
    scores = jnp.einsum(
        "bqhd,bkhd->bhqk", query_blocks, key_pairs, preferred_element_type=jnp.float32
    ) / math.sqrt(HEAD_DIM)
    query_idx = jnp.arange(WINDOW, dtype=jnp.int32)[:, None]
    key_idx = jnp.arange(2 * WINDOW, dtype=jnp.int32)[None, :]
    distance = query_idx + WINDOW - key_idx
    doc_pos = positions.reshape(block_total, 1, WINDOW, 1)
    visible = (
        (distance >= 0)[None, None]
        & (distance < WINDOW)[None, None]
        & (distance[None, None] <= doc_pos)
    )
    masked = jnp.where(visible, scores, -jnp.inf)
    top_score = jnp.max(masked, axis=3, keepdims=True)
    weights = jnp.exp(masked - top_score)
    probabilities = (weights / jnp.sum(weights, axis=3, keepdims=True)).astype(jnp.bfloat16)
    attended = jnp.einsum(
        "bhqk,bkhd->bqhd", probabilities, value_pairs, preferred_element_type=jnp.float32
    )
    return attended.reshape(row_count, local_width)


def body(
    residual_in,
    query_rows,
    key_rows,
    value_rows,
    bc_weight,
    decay_rate,
    level_codes,
    level_scale,
    positions,
    ssm_gain,
):
    row_count, local_width = residual_in.shape
    edge_rows = from_behind(
        (key_rows[row_count - WINDOW :], value_rows[row_count - WINDOW :]), ("seq", "fsdp"), 1
    )
    attended = window_attention(
        query_rows, key_rows, value_rows, edge_rows[0], edge_rows[1], positions
    )
    hidden = (residual_in.astype(jnp.float32) + attended).astype(jnp.bfloat16)
    partial_value = jnp.dot(
        hidden,
        lax.all_gather(bc_weight, "fsdp", axis=0, tiled=True),
        preferred_element_type=jnp.float32,
    )
    bc_full = lax.psum(partial_value, "head").astype(jnp.bfloat16)
    b_mat = bc_full[:, :STATES]
    c_mat = bc_full[:, STATES:]
    ssm_count = decay_rate.shape[1]
    values_h = hidden.reshape(row_count, ssm_count, HEAD_VALUES)
    log_cum = -jnp.cumsum(decay_rate, axis=0)
    log_end = log_cum[row_count - 1]
    scaled = (
        jnp.exp(log_end[None, :] - log_cum)[:, :, None] * values_h.astype(jnp.float32)
    ).astype(jnp.bfloat16)
    block_state = lax.dot_general(
        b_mat,
        scaled.reshape(row_count, local_width),
        (((0,), (0,)), ((), ())),
        preferred_element_type=jnp.float32,
    )
    lambdas = level_codes.astype(jnp.float32) * level_scale[None, :]
    local_bits = row_count.bit_length() - 1
    token_index = jnp.arange(row_count, dtype=jnp.int32)
    xor_idx = jnp.bitwise_xor(token_index[:, None], token_index[None, :])
    causal = token_index[None, :] <= token_index[:, None]
    level_weight = jnp.zeros((row_count, row_count), jnp.float32)
    for level_idx in range(local_bits + 1):
        low_edge = 0 if level_idx == 0 else 1 << level_idx - 1
        high_edge = 1 << level_idx
        inside = (xor_idx >= low_edge) & (xor_idx < high_edge)
        level_weight = level_weight + jnp.where(inside, lambdas[:, level_idx : level_idx + 1], 0.0)
    gram_mat = lax.dot_general(
        c_mat, b_mat, (((1,), (1,)), ((), ())), preferred_element_type=jnp.float32
    )
    shared = jnp.where(causal, gram_mat * level_weight, 0.0)

    def head_term(operands):
        cum_head, values_head = operands
        decay_mat = jnp.exp(jnp.where(causal, cum_head[:, None] - cum_head[None, :], -jnp.inf))
        mixing = (shared * decay_mat).astype(jnp.bfloat16)
        return jnp.dot(mixing, values_head, preferred_element_type=jnp.float32)

    intra_term = lax.map(head_term, (log_cum.T, jnp.transpose(values_h, (1, 0, 2))))
    shard_count = lax.axis_size(("seq", "fsdp"))
    shard_pos = lax.axis_index(("seq", "fsdp"))
    cross_count = shard_count.bit_length() - 1
    carry_state = block_state
    carry_end = log_end
    before = jnp.zeros_like(log_end)
    carried_list = []
    for bit_pos in range(cross_count):
        other_state, other_end = partner((carry_state, carry_end), ("seq", "fsdp"), bit_pos)
        upper_half = jnp.bitwise_and(jnp.right_shift(shard_pos, bit_pos), 1) == 1
        carried_list.append(
            jnp.where(upper_half, other_state * widen(jnp.exp(before), HEAD_VALUES)[None, :], 0.0)
        )
        joined_upper = other_state * widen(jnp.exp(carry_end), HEAD_VALUES)[None, :] + carry_state
        joined_lower = carry_state * widen(jnp.exp(other_end), HEAD_VALUES)[None, :] + other_state
        carry_state = jnp.where(upper_half, joined_upper, joined_lower)
        before = jnp.where(upper_half, before + other_end, before)
        carry_end = carry_end + other_end
    levels_state = jnp.stack(carried_list, axis=0)
    stacked = jnp.transpose(levels_state.astype(jnp.bfloat16), (1, 0, 2)).reshape(
        STATES, cross_count * local_width
    )
    level_reads = jnp.dot(c_mat, stacked, preferred_element_type=jnp.float32).reshape(
        row_count, cross_count, ssm_count, HEAD_VALUES
    )
    lam_cross = lambdas[:, local_bits + 1 : local_bits + 1 + cross_count]
    cross_term = jnp.einsum("rl,rlhp->rhp", lam_cross, level_reads) * jnp.exp(log_cum)[:, :, None]
    ssm_out = jnp.transpose(intra_term, (1, 0, 2)) + cross_term
    inv_rms = lax.rsqrt(jnp.mean(ssm_out * ssm_out, axis=2, keepdims=True) + 1e-05)
    result = (
        hidden.astype(jnp.float32)
        + (ssm_out * inv_rms).reshape(row_count, local_width) * ssm_gain[None, :]
    )
    return result.astype(jnp.bfloat16)


def solution(mesh):
    in_specs = (
        P(("groups", "seq", "fsdp"), "head"),
        P(("groups", "seq", "fsdp"), "head"),
        P(("groups", "seq", "fsdp"), "head"),
        P(("groups", "seq", "fsdp"), "head"),
        P(("head", "fsdp"), None),
        P(("groups", "seq", "fsdp"), "head"),
        P(("groups", "seq", "fsdp"), None),
        P(),
        P(("groups", "seq", "fsdp")),
        P("head"),
    )
    out_specs = P(("groups", "seq", "fsdp"), "head")
    return jax.shard_map(body, mesh=mesh, in_specs=in_specs, out_specs=out_specs, check_vma=False)
```

profile of v0, /device:TPU:0, one launch (start us, length us, event | category | flops | bytes accessed | tf_op | source)
XLA Modules:
  0.0 232.8 jit_solution(9729053218725581105)
XLA Ops:
  0.9 4.5 %reduce-window.6 = f32[16,8,128]{2,1,0:T(8,128)S(1)} reduce-window(f32[16,8,128]{2,1,0:T(8,128)S(1)} %bitcast.138, f32[]{:T(128)} %constant.32.clone.1), window={size=1x1x128 pad=0_0x0_0x127_0}, to_apply=%region_2.3 | reduce-window | flops 2080768 | bytes 131076 | tf_op jit(solution)/shard_map/reduce-window
  8.7 2.0 collective-permute-start.1
  12.3 4.5 %collective-permute-start = (bf16[128,1024]{1,0:T(8,128)(2,1)}, bf16[128,1024]{1,0:T(8,128)(2,1)S(1)}, u32[]{:S(2)}, u32[]{:S(2)}) collective-permute-start(bf16[128,1024]{1,0:T(8,128)(2,1)} %slice.77), channel_id=1, source_target_pairs={{0,1},{1,4},{4,5},{5,8},{8,9},{9,12},{12,13},{2,3},{3,6},{6,7},{7,... | collective-permute-start | bytes 786440 | tf_op jit(solution)/shard_map/ppermute | solution.py:17
  17.7 2.4 %copy.58 = bf16[128,8,8,128]{3,2,1,0:T(8,128)(2,1)S(1)} copy(bf16[128,8,8,128]{3,1,2,0:T(8,128)(2,1)} %bitcast.126) | data formatting | bytes 4194304
  20.1 1.9 copy.35
  22.0 1.9 copy.59
  24.0 2.0 copy.56
  25.9 4.1 %copy.33 = bf16[8,128,8,128]{1,3,2,0:T(8,128)(2,1)} copy(bf16[8,128,8,128]{3,2,1,0:T(8,128)(2,1)} %bitcast.132) | data formatting | bytes 4194304 | tf_op jit(solution)/shard_map/slice | solution.py:39
  30.0 2.5 %mul.119 = f32[1024,16,64]{0,2,1:T(8,128)} broadcast(f32[1024,16]{0,1:T(8,128)S(1)} %get-tuple-element.85), dimensions={0,1} | broadcast | bytes 4259840 | tf_op jit(solution)/shard_map/mul | solution.py:96
  32.5 5.5 %copy.43 = f32[1024,1024]{1,0:T(8,128)} copy(f32[1024,1024]{0,1:T(8,128)} %bitcast.124) | data formatting | bytes 8388608 | tf_op jit(solution)/shard_map/mul | solution.py:96
  39.7 2.3 all_gather.3
  42.8 1.9 copy.34
  44.9 2.0 copy.55
  46.9 4.1 %copy.32 = bf16[8,128,8,128]{1,3,2,0:T(8,128)(2,1)} copy(bf16[8,128,8,128]{3,2,1,0:T(8,128)(2,1)} %bitcast.130) | data formatting | bytes 4194304 | tf_op jit(solution)/shard_map/slice | solution.py:39
  51.0 3.5 %fusion.19 = f32[8,8,256,128]{3,2,1,0:T(8,128)S(1)} fusion(bf16[8,128,8,128]{3,1,2,0:T(8,128)(2,1)S(1)} %copy-done.4, bf16[8,128,8,128]{3,1,2,0:T(8,128)(2,1)} %copy.34, bf16[8,128,8,128]{3,2,1,0:T(8,128)(2,1)} %bitcast.128), kind=kOutput, calls=%fused_computation.28 | convolution fusion | flops 545259520 | bytes 14680064 | tf_op jit(solution)/shard_map/bqhd,bkhd->bhqk/dot_general | solution.py:41
  54.6 4.4 %fusion.85 = (f32[8,8,128]{2,1,0:T(8,128)S(1)}, f32[8,8,128,256]{2,3,1,0:T(8,128)}) fusion(f32[8,8,256,128]{3,2,1,0:T(8,128)S(1)} %fusion.19, pred[8,128,256]{1,2,0:T(8,128)(4,1)S(1)} %copy-done.9), kind=kOutput, calls=%fused_computation.118 | output fusion | flops 12583167 | bytes 17072128 | tf_op jit(solution)/shard_map/sub | solution.py:55
  59.0 6.6 %fusion.59 = f32[8,128,8,128]{1,3,2,0:T(8,128)} fusion(f32[8,8,128,256]{2,3,1,0:T(8,128)} %get-tuple-element.95, f32[8,8,128]{2,1,0:T(8,128)S(1)} %get-tuple-element.94, bf16[8,128,8,128]{1,3,2,0:T(8,128)(2,1)S(1)} %copy-done.6, bf16[8,128,8,128]{1,3,2,0:T(8,128)(2,1)S(1)} %copy-done.7), kind=kOutput, calls=%fused_computation.73 | convolution fusion | flops 549453824 | bytes 16809984 | tf_op jit(solution)/shard_map/bhqk,bkhd->bqhd/dot_general | solution.py:57
  65.6 5.3 %copy.38 = f32[8,128,8,128]{3,2,1,0:T(8,128)} copy(f32[8,128,8,128]{1,3,2,0:T(8,128)} %fusion.59) | data formatting | bytes 8388608 | tf_op jit(solution)/shard_map/bhqk,bkhd->bqhd/transpose | solution.py:57
  71.0 4.0 %fusion.14 = bf16[1024,1024]{1,0:T(8,128)(2,1)S(1)} fusion(f32[128,8,8,128]{3,2,1,0:T(8,128)} %bitcast.125, bf16[1024,1024]{1,0:T(8,128)(2,1)} %param.12), kind=kLoop, calls=%fused_computation.23 | loop fusion | flops 3145728 | bytes 8388608 | tf_op jit(solution)/shard_map/convert_element_type | solution.py:82
  76.7 30.9 %all-reduce.1 = bf16[1024,256]{1,0:T(8,128)(2,1)S(1)} all-reduce(f32[1024,256]{1,0:T(8,128)} %fusion.86), channel_id=1, replica_groups=mesh['groups'=2,'seq'=4,'head'=2,'fsdp'=2] {'head'}, use_global_device_ids=true, to_apply=%region_4.5 | all-reduce | flops 262144 | bytes 1572864 | tf_op jit(solution)/shard_map/psum | solution.py:88
  107.6 2.7 %fusion.62 = f32[128,1024]{1,0:T(8,128)S(1)} fusion(f32[1024,1024]{1,0:T(8,128)} %copy.43, bf16[1024,1024]{1,0:T(8,128)(2,1)S(1)} %fusion.14, bf16[1024,256]{1,0:T(8,128)(2,1)S(1)} %all-reduce.1), kind=kOutput, calls=%fused_computation.74 | convolution fusion | flops 271581184 | bytes 7077888 | tf_op jit(solution)/shard_map/dot_general | solution.py:98
  118.4 2.0 add_select_fusion.1
  121.9 10.7 %multiply_select_fusion = f32[1024,1024]{1,0:T(8,128)} fusion(f32[1024]{0:T(1024)} %bitcast.146, f32[1024]{0:T(1024)} %bitcast.147, f32[1024]{0:T(1024)} %bitcast.148, f32[1024]{0:T(1024)} %bitcast.149, f32[1024]{0:T(1024)} %bitcast.150, f32[1024]{0:T(1024)} %bitcast.151, f32[1024]{0:T(1024)} %bitcast.152, f32[1024]{0:T(1024)} %bitcast.153, ...), kind=kOutput, calls=%fused_computation.34 | convolution fusion | flops 329252864 | bytes 4763648 | tf_op jit(solution)/shard_map/dot_general | solution.py:115
  132.5 2.6 %copy.41 = bf16[1024,1024]{0,1:T(8,128)(2,1)} copy(bf16[1024,1024]{1,0:T(8,128)(2,1)S(1)} %fusion.14) | data formatting | bytes 4194304 | tf_op jit(solution)/shard_map/convert_element_type | solution.py:82
  135.1 2.0 fusion.68
  138.3 61.2 %while.11 = (s32[]{:T(128)}, f32[16,1024,64]{1,2,0:T(8,128)}, f32[16,1024]{1,0:T(8,128)S(1)}, f32[1024,1024]{1,0:T(8,128)}, bf16[16,1024,64]{1,2,0:T(8,128)(2,1)}, /*index=5*/s32[]{:T(128)}) while((s32[]{:T(128)}, f32[16,1024,64]{1,2,0:T(8,128)}, f32[16,1024]{1,0:T(8,128)S(1)}, f32[1024,1024]{1,0:T(8,128)}, ...), condition=%wide.region_6.7_spmd.clone, body=%wide.region_5.6_spmd.clone.sunk | while | flops 139460608 | bytes 4605001 | solution.py:126
  138.3 3.8 %fusion.93 = f32[16,1024,64]{1,2,0:T(8,128)} fusion(f32[16,1024,64]{1,2,0:T(8,128)} %get-tuple-element.134, s32[]{:T(128)} %get-tuple-element.133, f32[1024,1024]{1,0:T(8,128)} %get-tuple-element.142, f32[1024]{0:T(1024)S(1)} %bitcast.141, bf16[16,1024,64]{1,2,0:T(8,128)(2,1)} %get-tuple-element.143), kind=kOutput, calls=%fused_computation.5.clone.1 | convolution fusion | flops 139460608 | bytes 4596736 | tf_op jit(solution)/shard_map/while/body/eval_jaxpr/dot_general | solution.py:124
  142.1 3.8 %fusion.93 = f32[16,1024,64]{1,2,0:T(8,128)} fusion(f32[16,1024,64]{1,2,0:T(8,128)} %get-tuple-element.134, s32[]{:T(128)} %get-tuple-element.133, f32[1024,1024]{1,0:T(8,128)} %get-tuple-element.142, f32[1024]{0:T(1024)S(1)} %bitcast.141, bf16[16,1024,64]{1,2,0:T(8,128)(2,1)} %get-tuple-element.143), kind=kOutput, calls=%fused_computation.5.clone.1 | convolution fusion | flops 139460608 | bytes 4596736 | tf_op jit(solution)/shard_map/while/body/eval_jaxpr/dot_general | solution.py:124
  146.0 3.8 %fusion.93 = f32[16,1024,64]{1,2,0:T(8,128)} fusion(f32[16,1024,64]{1,2,0:T(8,128)} %get-tuple-element.134, s32[]{:T(128)} %get-tuple-element.133, f32[1024,1024]{1,0:T(8,128)} %get-tuple-element.142, f32[1024]{0:T(1024)S(1)} %bitcast.141, bf16[16,1024,64]{1,2,0:T(8,128)(2,1)} %get-tuple-element.143), kind=kOutput, calls=%fused_computation.5.clone.1 | convolution fusion | flops 139460608 | bytes 4596736 | tf_op jit(solution)/shard_map/while/body/eval_jaxpr/dot_general | solution.py:124
  149.8 3.8 %fusion.93 = f32[16,1024,64]{1,2,0:T(8,128)} fusion(f32[16,1024,64]{1,2,0:T(8,128)} %get-tuple-element.134, s32[]{:T(128)} %get-tuple-element.133, f32[1024,1024]{1,0:T(8,128)} %get-tuple-element.142, f32[1024]{0:T(1024)S(1)} %bitcast.141, bf16[16,1024,64]{1,2,0:T(8,128)(2,1)} %get-tuple-element.143), kind=kOutput, calls=%fused_computation.5.clone.1 | convolution fusion | flops 139460608 | bytes 4596736 | tf_op jit(solution)/shard_map/while/body/eval_jaxpr/dot_general | solution.py:124
  153.7 3.8 %fusion.93 = f32[16,1024,64]{1,2,0:T(8,128)} fusion(f32[16,1024,64]{1,2,0:T(8,128)} %get-tuple-element.134, s32[]{:T(128)} %get-tuple-element.133, f32[1024,1024]{1,0:T(8,128)} %get-tuple-element.142, f32[1024]{0:T(1024)S(1)} %bitcast.141, bf16[16,1024,64]{1,2,0:T(8,128)(2,1)} %get-tuple-element.143), kind=kOutput, calls=%fused_computation.5.clone.1 | convolution fusion | flops 139460608 | bytes 4596736 | tf_op jit(solution)/shard_map/while/body/eval_jaxpr/dot_general | solution.py:124
  157.5 3.8 %fusion.93 = f32[16,1024,64]{1,2,0:T(8,128)} fusion(f32[16,1024,64]{1,2,0:T(8,128)} %get-tuple-element.134, s32[]{:T(128)} %get-tuple-element.133, f32[1024,1024]{1,0:T(8,128)} %get-tuple-element.142, f32[1024]{0:T(1024)S(1)} %bitcast.141, bf16[16,1024,64]{1,2,0:T(8,128)(2,1)} %get-tuple-element.143), kind=kOutput, calls=%fused_computation.5.clone.1 | convolution fusion | flops 139460608 | bytes 4596736 | tf_op jit(solution)/shard_map/while/body/eval_jaxpr/dot_general | solution.py:124
  161.3 3.8 %fusion.93 = f32[16,1024,64]{1,2,0:T(8,128)} fusion(f32[16,1024,64]{1,2,0:T(8,128)} %get-tuple-element.134, s32[]{:T(128)} %get-tuple-element.133, f32[1024,1024]{1,0:T(8,128)} %get-tuple-element.142, f32[1024]{0:T(1024)S(1)} %bitcast.141, bf16[16,1024,64]{1,2,0:T(8,128)(2,1)} %get-tuple-element.143), kind=kOutput, calls=%fused_computation.5.clone.1 | convolution fusion | flops 139460608 | bytes 4596736 | tf_op jit(solution)/shard_map/while/body/eval_jaxpr/dot_general | solution.py:124
  165.1 3.8 %fusion.93 = f32[16,1024,64]{1,2,0:T(8,128)} fusion(f32[16,1024,64]{1,2,0:T(8,128)} %get-tuple-element.134, s32[]{:T(128)} %get-tuple-element.133, f32[1024,1024]{1,0:T(8,128)} %get-tuple-element.142, f32[1024]{0:T(1024)S(1)} %bitcast.141, bf16[16,1024,64]{1,2,0:T(8,128)(2,1)} %get-tuple-element.143), kind=kOutput, calls=%fused_computation.5.clone.1 | convolution fusion | flops 139460608 | bytes 4596736 | tf_op jit(solution)/shard_map/while/body/eval_jaxpr/dot_general | solution.py:124
  168.9 3.8 %fusion.93 = f32[16,1024,64]{1,2,0:T(8,128)} fusion(f32[16,1024,64]{1,2,0:T(8,128)} %get-tuple-element.134, s32[]{:T(128)} %get-tuple-element.133, f32[1024,1024]{1,0:T(8,128)} %get-tuple-element.142, f32[1024]{0:T(1024)S(1)} %bitcast.141, bf16[16,1024,64]{1,2,0:T(8,128)(2,1)} %get-tuple-element.143), kind=kOutput, calls=%fused_computation.5.clone.1 | convolution fusion | flops 139460608 | bytes 4596736 | tf_op jit(solution)/shard_map/while/body/eval_jaxpr/dot_general | solution.py:124
  172.8 3.8 %fusion.93 = f32[16,1024,64]{1,2,0:T(8,128)} fusion(f32[16,1024,64]{1,2,0:T(8,128)} %get-tuple-element.134, s32[]{:T(128)} %get-tuple-element.133, f32[1024,1024]{1,0:T(8,128)} %get-tuple-element.142, f32[1024]{0:T(1024)S(1)} %bitcast.141, bf16[16,1024,64]{1,2,0:T(8,128)(2,1)} %get-tuple-element.143), kind=kOutput, calls=%fused_computation.5.clone.1 | convolution fusion | flops 139460608 | bytes 4596736 | tf_op jit(solution)/shard_map/while/body/eval_jaxpr/dot_general | solution.py:124
  176.6 3.8 %fusion.93 = f32[16,1024,64]{1,2,0:T(8,128)} fusion(f32[16,1024,64]{1,2,0:T(8,128)} %get-tuple-element.134, s32[]{:T(128)} %get-tuple-element.133, f32[1024,1024]{1,0:T(8,128)} %get-tuple-element.142, f32[1024]{0:T(1024)S(1)} %bitcast.141, bf16[16,1024,64]{1,2,0:T(8,128)(2,1)} %get-tuple-element.143), kind=kOutput, calls=%fused_computation.5.clone.1 | convolution fusion | flops 139460608 | bytes 4596736 | tf_op jit(solution)/shard_map/while/body/eval_jaxpr/dot_general | solution.py:124
  180.4 3.8 %fusion.93 = f32[16,1024,64]{1,2,0:T(8,128)} fusion(f32[16,1024,64]{1,2,0:T(8,128)} %get-tuple-element.134, s32[]{:T(128)} %get-tuple-element.133, f32[1024,1024]{1,0:T(8,128)} %get-tuple-element.142, f32[1024]{0:T(1024)S(1)} %bitcast.141, bf16[16,1024,64]{1,2,0:T(8,128)(2,1)} %get-tuple-element.143), kind=kOutput, calls=%fused_computation.5.clone.1 | convolution fusion | flops 139460608 | bytes 4596736 | tf_op jit(solution)/shard_map/while/body/eval_jaxpr/dot_general | solution.py:124
  184.3 3.8 %fusion.93 = f32[16,1024,64]{1,2,0:T(8,128)} fusion(f32[16,1024,64]{1,2,0:T(8,128)} %get-tuple-element.134, s32[]{:T(128)} %get-tuple-element.133, f32[1024,1024]{1,0:T(8,128)} %get-tuple-element.142, f32[1024]{0:T(1024)S(1)} %bitcast.141, bf16[16,1024,64]{1,2,0:T(8,128)(2,1)} %get-tuple-element.143), kind=kOutput, calls=%fused_computation.5.clone.1 | convolution fusion | flops 139460608 | bytes 4596736 | tf_op jit(solution)/shard_map/while/body/eval_jaxpr/dot_general | solution.py:124
  188.1 3.8 %fusion.93 = f32[16,1024,64]{1,2,0:T(8,128)} fusion(f32[16,1024,64]{1,2,0:T(8,128)} %get-tuple-element.134, s32[]{:T(128)} %get-tuple-element.133, f32[1024,1024]{1,0:T(8,128)} %get-tuple-element.142, f32[1024]{0:T(1024)S(1)} %bitcast.141, bf16[16,1024,64]{1,2,0:T(8,128)(2,1)} %get-tuple-element.143), kind=kOutput, calls=%fused_computation.5.clone.1 | convolution fusion | flops 139460608 | bytes 4596736 | tf_op jit(solution)/shard_map/while/body/eval_jaxpr/dot_general | solution.py:124
  191.9 3.8 %fusion.93 = f32[16,1024,64]{1,2,0:T(8,128)} fusion(f32[16,1024,64]{1,2,0:T(8,128)} %get-tuple-element.134, s32[]{:T(128)} %get-tuple-element.133, f32[1024,1024]{1,0:T(8,128)} %get-tuple-element.142, f32[1024]{0:T(1024)S(1)} %bitcast.141, bf16[16,1024,64]{1,2,0:T(8,128)(2,1)} %get-tuple-element.143), kind=kOutput, calls=%fused_computation.5.clone.1 | convolution fusion | flops 139460608 | bytes 4596736 | tf_op jit(solution)/shard_map/while/body/eval_jaxpr/dot_general | solution.py:124
  195.7 3.8 %fusion.93 = f32[16,1024,64]{1,2,0:T(8,128)} fusion(f32[16,1024,64]{1,2,0:T(8,128)} %get-tuple-element.134, s32[]{:T(128)} %get-tuple-element.133, f32[1024,1024]{1,0:T(8,128)} %get-tuple-element.142, f32[1024]{0:T(1024)S(1)} %bitcast.141, bf16[16,1024,64]{1,2,0:T(8,128)(2,1)} %get-tuple-element.143), kind=kOutput, calls=%fused_computation.5.clone.1 | convolution fusion | flops 139460608 | bytes 4596736 | tf_op jit(solution)/shard_map/while/body/eval_jaxpr/dot_general | solution.py:124
  203.2 6.3 %fusion.70 = f32[1024,3,16,64]{0,3,2,1:T(8,128)} fusion(bf16[3,16,64,128]{3,2,1,0:T(8,128)(2,1)S(1)} %bitcast.133, bf16[1024,256]{1,0:T(8,128)(2,1)S(1)} %all-reduce.1), kind=kOutput, calls=%fused_computation.91 | convolution fusion | flops 805306368 | bytes 13631488 | tf_op jit(solution)/shard_map/dot_general | solution.py:149
  209.5 6.9 %fusion.10 = f32[1024,1024]{0,1:T(8,128)S(1)} fusion(f32[1024,3,16,64]{0,3,2,1:T(8,128)} %fusion.70, f32[1024,3]{0,1:T(4,128)S(1)} %slice.117), kind=kLoop, calls=%fused_computation.13 | loop fusion | flops 5242880 | bytes 16789504
  216.5 3.6 %multiply_reduce_fusion = f32[1024,16]{0,1:T(8,128)S(1)} fusion(f32[1024,16]{0,1:T(8,128)S(1)} %get-tuple-element.86, f32[16,1024,64]{1,2,0:T(8,128)} %get-tuple-element.37, f32[1024,1024]{0,1:T(8,128)S(1)} %fusion.10), kind=kLoop, calls=%fused_computation.33 | loop fusion | flops 4177920 | bytes 8519680 | tf_op jit(solution)/shard_map/reduce_sum | solution.py:155
  220.1 3.1 %broadcast_multiply_fusion = f32[1024,16,64]{0,2,1:T(8,128)} fusion(f32[1024,16]{0,1:T(8,128)S(1)} %add_rsqrt_fusion, f32[1024,16]{0,1:T(8,128)S(1)} %get-tuple-element.86, f32[16,1024,64]{1,2,0:T(8,128)S(1)} %copy-done, f32[1024,1024]{0,1:T(8,128)S(1)} %fusion.10), kind=kLoop, calls=%fused_computation.80 | loop fusion | flops 3145728 | bytes 12713984 | tf_op jit(solution)/shard_map/mul | solution.py:158
  223.1 5.4 %copy.45 = f32[1024,1024]{1,0:T(8,128)} copy(f32[1024,1024]{0,1:T(8,128)} %bitcast.123) | data formatting | bytes 8388608 | tf_op jit(solution)/shard_map/reshape | solution.py:158
  228.5 4.3 %fusion.13 = bf16[1024,1024]{1,0:T(8,128)(2,1)} fusion(bf16[1024,1024]{1,0:T(8,128)(2,1)S(1)} %fusion.14, f32[1024,1024]{1,0:T(8,128)} %copy.45, f32[1024]{0:T(1024)S(1)} %copy-done.13), kind=kLoop, calls=%fused_computation.21 | loop fusion | flops 4194304 | bytes 8392704 | tf_op jit(solution)/shard_map/convert_element_type | solution.py:160
  (101 shorter events, 25.4 us)
Async XLA Ops:
  6.6 104.6 %collective-permute-start.3 = (f32[16]{0:T(128)}, f32[16]{0:T(128)}, u32[]{:S(2)}, u32[]{:S(2)}) collective-permute-start(f32[16]{0:T(128)} %slice_reduce_fusion), channel_id=1, source_target_pairs={{0,1},{1,0},{4,5},{5,4},{8,9},{9,8},{12,13},{13,12},{2,3},{3,2},{6... | collective-permute-start | bytes 200 | tf_op jit(solution)/shard_map/ppermute | solution.py:21
  8.7 33.3 %collective-permute-start.1 = (bf16[128,1024]{1,0:T(8,128)(2,1)}, bf16[128,1024]{1,0:T(8,128)(2,1)S(1)}, u32[]{:S(2)}, u32[]{:S(2)}) collective-permute-start(bf16[128,1024]{1,0:T(8,128)(2,1)} %slice.81), channel_id=1, source_target_pairs={{0,1},{1,4},{4,5},{5,8},{8,9},{9,12},{12,13},{2,3},{3,6},{6,7},{7,... | collective-permute-start | bytes 786440 | tf_op jit(solution)/shard_map/ppermute | solution.py:17
  12.3 32.4 %collective-permute-start = (bf16[128,1024]{1,0:T(8,128)(2,1)}, bf16[128,1024]{1,0:T(8,128)(2,1)S(1)}, u32[]{:S(2)}, u32[]{:S(2)}) collective-permute-start(bf16[128,1024]{1,0:T(8,128)(2,1)} %slice.77), channel_id=1, source_target_pairs={{0,1},{1,4},{4,5},{5,8},{8,9},{9,12},{12,13},{2,3},{3,6},{6,7},{7,... | collective-permute-start | bytes 786440 | tf_op jit(solution)/shard_map/ppermute | solution.py:17
  17.7 4.3 %copy-start.5 = (bf16[1024,1024]{1,0:T(8,128)(2,1)S(1)}, bf16[1024,1024]{1,0:T(8,128)(2,1)}, u32[]{:S(2)}) copy-start(bf16[1024,1024]{1,0:T(8,128)(2,1)} %param.13) | copy-start | bytes 6291460
  20.1 3.9 %copy-start.2 = (bf16[1024,1024]{1,0:T(8,128)(2,1)S(1)}, bf16[1024,1024]{1,0:T(8,128)(2,1)}, u32[]{:S(2)}) copy-start(bf16[1024,1024]{1,0:T(8,128)(2,1)} %param.15) | copy-start | bytes 6291460
  32.5 5.5 %copy-start.12 = (s32[1024]{0:T(1024)S(1)}, s32[1024]{0:T(1024)}, u32[]{:S(2)}) copy-start(s32[1024]{0:T(1024)} %param.20) | copy-start | bytes 12292
  32.5 6.4 %copy-start.11 = (s32[1024,18]{0,1:T(8,128)S(1)}, s32[1024,18]{0,1:T(8,128)}, u32[]{:S(2)}) copy-start(s32[1024,18]{0,1:T(8,128)} %param.18) | copy-start | bytes 221188
  32.5 6.4 %copy-start.14 = (f32[18]{0:T(128)S(1)}, f32[18]{0:T(128)}, u32[]{:S(2)}) copy-start(f32[18]{0:T(128)} %param.19) | copy-start | bytes 220
  32.5 7.2 %copy-start.8 = (bf16[512,256]{1,0:T(8,128)(2,1)S(1)}, bf16[512,256]{1,0:T(8,128)(2,1)}, u32[]{:S(2)}) copy-start(bf16[512,256]{1,0:T(8,128)(2,1)} %param.16) | copy-start | bytes 786436
  32.5 9.4 %copy-start.1 = (bf16[1024,1024]{1,0:T(8,128)(2,1)S(1)}, bf16[1024,1024]{1,0:T(8,128)(2,1)}, u32[]{:S(2)}) copy-start(bf16[1024,1024]{1,0:T(8,128)(2,1)} %param.14) | copy-start | bytes 6291460
  42.1 2.6 %copy-start.3 = (bf16[1024,1024]{1,0:T(8,128)(2,1)S(1)}, bf16[1024,1024]{1,0:T(8,128)(2,1)}, u32[]{:S(2)}) copy-start(bf16[1024,1024]{1,0:T(8,128)(2,1)} %param.15) | copy-start | bytes 6291460
  44.9 6.1 %copy-start.4 = (bf16[8,128,8,128]{3,1,2,0:T(8,128)(2,1)S(1)}, bf16[8,128,8,128]{3,1,2,0:T(8,128)(2,1)}, u32[]{:S(2)}) copy-start(bf16[8,128,8,128]{3,1,2,0:T(8,128)(2,1)} %copy.35) | copy-start | bytes 6291460
  51.0 3.5 %copy-start.9 = (pred[8,128,256]{1,2,0:T(8,128)(4,1)S(1)}, pred[8,128,256]{1,2,0:T(8,128)(4,1)}, u32[]{:S(2)}) copy-start(pred[8,128,256]{1,2,0:T(8,128)(4,1)} %compare_and_fusion) | copy-start | bytes 786436
  54.6 4.4 %copy-start.6 = (bf16[8,128,8,128]{1,3,2,0:T(8,128)(2,1)S(1)}, bf16[8,128,8,128]{1,3,2,0:T(8,128)(2,1)}, u32[]{:S(2)}) copy-start(bf16[8,128,8,128]{1,3,2,0:T(8,128)(2,1)} %copy.33) | copy-start | bytes 6291460
  54.6 4.4 %copy-start.7 = (bf16[8,128,8,128]{1,3,2,0:T(8,128)(2,1)S(1)}, bf16[8,128,8,128]{1,3,2,0:T(8,128)(2,1)}, u32[]{:S(2)}) copy-start(bf16[8,128,8,128]{1,3,2,0:T(8,128)(2,1)} %copy.32) | copy-start | bytes 6291460
  76.7 33.8 %copy-start.10 = (f32[1024,18]{0,1:T(8,128)S(1)}, f32[1024,18]{0,1:T(8,128)}, u32[]{:S(2)}) copy-start(f32[1024,18]{0,1:T(8,128)} %convert_multiply_fusion.1) | copy-start | bytes 221188
  110.4 8.0 %collective-permute-start.2 = (f32[128,1024]{1,0:T(8,128)S(1)}, f32[128,1024]{1,0:T(8,128)}, u32[]{:S(2)}, u32[]{:S(2)}) collective-permute-start(f32[128,1024]{1,0:T(8,128)S(1)} %fusion.62), channel_id=1, source_target_pairs={{0,1},{1,0},{4,5},{5,4},{8,9},{9,8},{12,13},{13,12},{2,3},{3,2},{6... | collective-permute-start | bytes 1572872 | tf_op jit(solution)/shard_map/ppermute | solution.py:21
  111.8 3.5 %collective-permute-start.5 = (f32[16]{0:T(128)S(1)}, f32[16]{0:T(128)S(1)}, u32[]{:S(2)}, u32[]{:S(2)}) collective-permute-start(f32[16]{0:T(128)S(1)} %get-tuple-element.71), channel_id=1, source_target_pairs={{0,4},{1,5},{4,0},{5,1},{8,12},{9,13},{12,8},{13,9},{2,6},{3,7},{6... | collective-permute-start | bytes 200 | tf_op jit(solution)/shard_map/ppermute | solution.py:21
  120.3 14.8 %collective-permute-start.4 = (f32[128,1024]{1,0:T(8,128)}, f32[128,1024]{1,0:T(8,128)S(1)}, u32[]{:S(2)}, u32[]{:S(2)}) collective-permute-start(f32[128,1024]{1,0:T(8,128)} %add_select_fusion.1), channel_id=1, source_target_pairs={{0,4},{1,5},{4,0},{5,1},{8,12},{9,13},{12,8},{13,9},{2,6},{3,7},{6... | collective-permute-start | bytes 1572872 | tf_op jit(solution)/shard_map/ppermute | solution.py:21
  137.1 62.5 %collective-permute-start.6 = (f32[128,1024]{1,0:T(8,128)}, f32[128,1024]{1,0:T(8,128)}, u32[]{:S(2)}, u32[]{:S(2)}) collective-permute-start(f32[128,1024]{1,0:T(8,128)} %get-tuple-element.73), channel_id=1, source_target_pairs={{0,8},{1,9},{4,12},{5,13},{8,0},{9,1},{12,4},{13,5},{2,10},{3,11},... | collective-permute-start | bytes 1572872 | tf_op jit(solution)/shard_map/ppermute | solution.py:21
  216.5 3.6 %copy-start = (f32[16,1024,64]{1,2,0:T(8,128)S(1)}, f32[16,1024,64]{1,2,0:T(8,128)}, u32[]{:S(2)}) copy-start(f32[16,1024,64]{1,2,0:T(8,128)} %get-tuple-element.37) | copy-start | bytes 12582916
  223.1 5.4 %copy-start.13 = (f32[1024]{0:T(1024)S(1)}, f32[1024]{0:T(1024)}, u32[]{:S(2)}) copy-start(f32[1024]{0:T(1024)} %param.21) | copy-start | bytes 12292
where the time goes:
time: 234 us; the launch traced here: 233 us
  matrix products  92.7 us (40%)
  local copies, waits for them, and re-layouts  53 us (23%)
  other arithmetic  41 us (18%)
  blocking collectives  33.2 us (14%)
  starting transfers between devices  11.4 us (5%)
    dot_general x16, matrix products, head_term(): return jnp.dot(mixing, values_head, preferred_element_type=jnp.float32)  61.1 us
    psum x1, blocking collectives, body(): bc_full = lax.psum(partial_value, 'head').astype(jnp.bfloat16)  30.9 us
    dot_general x1, matrix products, body(): lax.dot_general(c_mat, b_mat, (((1,), (1,)), ((), ())), preferred_element...  10.7 us
    unnamed x37, local copies, waits for them, and re-layouts  9.81 us
    mul x2, local copies, waits for them, and re-layouts, body(): jnp.exp(log_end[None, :] - log_cum)[:, :, None]  7.98 us
    unnamed x3, other arithmetic  7.28 us
    dot_general x1, matrix products, window_attention(): jnp.einsum('bhqk,bkhd->bqhd', probabilities, value_pairs, preferred_eleme...  6.63 us
    ppermute x2, starting transfers between devices, from_behind(): return lax.ppermute(x, axis, pairs)  6.49 us
  transfers between devices with their start and end apart: 7, of which 1 were waited for; matrix products, arithmetic and copies ran while one was open for 61% of the time, Pallas kernels for 0%

commit v1 on v0

v1 whole, which is shorter than its diff:
```python
import functools
import math

import jax
import jax.numpy as jnp
import numpy as np
from jax import lax
from jax.experimental import pallas as pl
from jax.experimental.pallas import tpu as pltpu
from jax.sharding import PartitionSpec as P

HEAD_DIM = 128
HEAD_VALUES = 64
STATES = 128
WINDOW = 128
CHUNK = 128
NORM_TILE = 256
VMEM_LIMIT = 48 * 1024 * 1024
HIDDEN = -1e30

F32 = jnp.float32
BF16 = jnp.bfloat16


def params():
    return pltpu.CompilerParams(vmem_limit_bytes=VMEM_LIMIT)


def cost(flops, moved, transcendentals=0):
    return pl.CostEstimate(flops=flops, bytes_accessed=moved, transcendentals=transcendentals)


def fixed(shape):
    return pl.BlockSpec(shape, lambda i: (0,) * len(shape))


def dot(left, right):
    return jnp.dot(left, right, preferred_element_type=F32)


def widen_rows(rows, spread):
    high = rows.astype(BF16)
    low = (rows - high.astype(F32)).astype(BF16)
    return dot(high, spread) + dot(low, spread)


def decay_kernel(rate_ref, lower_ref, spread_ref, rise_ref, fall_ref, carry_ref, rows_ref, end_ref, prefix):
    @pl.when(pl.program_id(0) == 0)
    def _():
        prefix[...] = jnp.zeros_like(prefix)

    rate = rate_ref[...]
    first = rate.astype(BF16)
    rest = rate - first.astype(F32)
    second = rest.astype(BF16)
    third = (rest - second.astype(F32)).astype(BF16)
    total = dot(lower_ref[...], jnp.concatenate([first, second, third], axis=0))
    middle = total[CHUNK // 2 - 1 : CHUNK // 2]
    last = total[CHUNK - 1 :]
    before = prefix[0:1]
    rise_ref[...] = jnp.exp(total - middle)
    fall_ref[...] = jnp.exp(middle - total)
    carry_ref[...] = jnp.exp(-(total + before))
    after = before + last
    row_idx = lax.broadcasted_iota(jnp.int32, prefix.shape, 0)
    logs = jnp.where(
        row_idx == 0,
        middle - last,
        jnp.where(row_idx == 1, -last, jnp.where(row_idx == 2, -middle, 0.0)),
    )
    rows_ref[...] = widen_rows(jnp.exp(logs), spread_ref[...])
    prefix[...] = jnp.broadcast_to(after, prefix.shape)
    end_ref[...] = jnp.broadcast_to(-after, end_ref.shape)


def decay_factors(decay_rate, spread):
    row_count, heads = decay_rate.shape
    width = spread.shape[1]
    chunks = row_count // CHUNK
    lower = np.tril(np.ones((CHUNK, CHUNK), np.float32))
    lower = jnp.asarray(np.concatenate([lower] * 3, axis=1), BF16)
    rows = pl.BlockSpec((CHUNK, heads), lambda i: (i, 0))
    return pl.pallas_call(
        decay_kernel,
        grid=(chunks,),
        in_specs=[rows, fixed(lower.shape), fixed(spread.shape)],
        out_specs=[rows, rows, rows, pl.BlockSpec((8, width), lambda i: (i, 0)), fixed((8, heads))],
        out_shape=[jax.ShapeDtypeStruct((row_count, heads), F32)] * 3
        + [jax.ShapeDtypeStruct((chunks * 8, width), F32), jax.ShapeDtypeStruct((8, heads), F32)],
        scratch_shapes=[pltpu.VMEM((8, heads), F32)],
        compiler_params=params(),
        cost_estimate=cost(10**8, 5 * 10**6),
        name="decay_factors",
    )(decay_rate, lower, spread)


def attend_kernel(
    first_chunk,
    alias_count,
    half_ref,
    pos_ref,
    query_ref,
    key_before_ref,
    key_ref,
    value_before_ref,
    value_ref,
    residual_ref,
    own_weight_ref,
    other_weight_ref,
    rise_ref,
    spread_ref,
    *refs,
):
    hidden_ref, scaled_ref, b_ref, c_ref = refs[alias_count:]
    width = query_ref.shape[1]
    chunk = pl.program_id(0) + first_chunk
    key_row = lax.broadcasted_iota(jnp.int32, (WINDOW, WINDOW), 0)
    query_lane = lax.broadcasted_iota(jnp.int32, (WINDOW, WINDOW), 1)
    away = query_lane - key_row
    away = jnp.where(away < 0, away + WINDOW, away)
    doc_pos = pos_ref[pl.ds(chunk, 1), :]
    bias = jnp.where(away <= doc_pos, 0.0, HIDDEN).astype(F32).T
    current = query_lane <= key_row
    current_share = current.astype(F32).astype(BF16)
    before_share = (1.0 - current.astype(F32)).astype(BF16)
    ones = jnp.ones((2 * WINDOW, HEAD_DIM), BF16)
    factor = math.log2(math.e) / math.sqrt(HEAD_DIM)
    pieces = []
    for head in range(width // HEAD_DIM):
        lanes = slice(head * HEAD_DIM, (head + 1) * HEAD_DIM)
        keys = jnp.concatenate([key_before_ref[:, lanes], key_ref[:, lanes]], axis=0)
        values = jnp.concatenate([value_before_ref[:, lanes], value_ref[:, lanes]], axis=0)
        scores = lax.dot_general(
            query_ref[:, lanes], keys, (((1,), (1,)), ((), ())), preferred_element_type=F32
        )
        merged = jnp.where(current, scores[:, WINDOW:], scores[:, :WINDOW]) + bias
        top = jnp.max(merged, axis=1, keepdims=True)
        weights = jnp.exp2((merged - top) * factor).astype(BF16)
        weights = jnp.concatenate([weights * before_share, weights * current_share], axis=1)
        summed = dot(weights, jnp.concatenate([values, ones], axis=1))
        attended = summed[:, :HEAD_DIM] / summed[:, HEAD_DIM:]
        pieces.append((residual_ref[:, lanes].astype(F32) + attended).astype(BF16))
    hidden = jnp.concatenate(pieces, axis=1)
    hidden_ref[...] = hidden
    rise = widen_rows(rise_ref[...], spread_ref[...])
    scaled_ref[...] = (rise * hidden.astype(F32)).astype(BF16)
    low, high = hidden[:, : width // 2], hidden[:, width // 2 :]
    is_low = half_ref[0] == 0
    own = jnp.where(is_low, low, high)
    other = jnp.where(is_low, high, low)
    shared = dot(own, own_weight_ref[...]) + dot(other, other_weight_ref[...])
    b_ref[...] = shared[:, :STATES].astype(BF16)
    c_ref[...] = shared[:, STATES:].astype(BF16)


def attend(first, count, half, positions, query, key, value, edges, residual, weights, rise, spread, held):
    row_count, width = query.shape
    heads = rise.shape[1]

    def rows(columns, shift=0):
        return pl.BlockSpec((CHUNK, columns), lambda i: (i + first + shift, 0))

    if edges is None:
        key_before, value_before = key, value
        before = rows(width, -1)
    else:
        key_before, value_before = edges
        before = pl.BlockSpec((CHUNK, width), lambda i: (i, 0))
    aliased = [] if held is None else list(held)
    in_specs = [
        pl.BlockSpec(memory_space=pltpu.SMEM),
        fixed(positions.shape),
        rows(width),
        before,
        rows(width),
        before,
        rows(width),
        rows(width),
        fixed(weights[0].shape),
        fixed(weights[1].shape),
        rows(heads),
        fixed(spread.shape),
    ]
    arg_count = len(in_specs)
    in_specs += [pl.BlockSpec(memory_space=pl.ANY)] * len(aliased)
    part = pl.BlockSpec((CHUNK, STATES), lambda i: (i, 0))
    return pl.pallas_call(
        functools.partial(attend_kernel, first, len(aliased)),
        grid=(count,),
        in_specs=in_specs,
        out_specs=[rows(width), rows(width), part, part],
        out_shape=[jax.ShapeDtypeStruct((row_count, width), BF16)] * 2
        + [jax.ShapeDtypeStruct((count * CHUNK, STATES), BF16)] * 2,
        input_output_aliases={arg_count + i: i for i in range(len(aliased))},
        compiler_params=params(),
        cost_estimate=cost(count * 3 * 10**8, count * 2 * 10**6),
        name="window_attention",
    )(half, positions, query, key_before, key, value_before, value, residual, *weights, rise, spread, *aliased)


def state_kernel(own_ref, other_ref, scaled_ref, rows_ref, state_ref, turned):
    chunks = scaled_ref.shape[0] // CHUNK

    @pl.when(pl.program_id(0) == 0)
    def _():
        b_mat = own_ref[...].astype(F32) + other_ref[...].astype(F32)
        for chunk in range(chunks):
            span = slice(chunk * CHUNK, (chunk + 1) * CHUNK)
            turned[:, span] = b_mat[span].T.astype(BF16)

    total = None
    for chunk in range(chunks):
        span = slice(chunk * CHUNK, (chunk + 1) * CHUNK)
        added = dot(turned[:, span], scaled_ref[span, :]) * rows_ref[chunk * 8 : chunk * 8 + 1]
        total = added if total is None else total * rows_ref[chunk * 8 + 1 : chunk * 8 + 2] + added
    state_ref[...] = total.astype(BF16)


def block_state(b_own, b_other, scaled, factor_rows):
    row_count, width = scaled.shape
    tile = min(width, 256)
    return pl.pallas_call(
        state_kernel,
        grid=(width // tile,),
        in_specs=[
            fixed(b_own.shape),
            fixed(b_own.shape),
            pl.BlockSpec((row_count, tile), lambda i: (0, i)),
            pl.BlockSpec((factor_rows.shape[0], tile), lambda i: (0, i)),
        ],
        out_specs=pl.BlockSpec((STATES, tile), lambda i: (0, i)),
        out_shape=jax.ShapeDtypeStruct((STATES, width), BF16),
        scratch_shapes=[pltpu.VMEM((STATES, row_count), BF16)],
        compiler_params=params(),
        cost_estimate=cost(3 * 10**8, 4 * 10**6),
        name="block_state",
    )(b_own, b_other, scaled, factor_rows)


def local_kernel(
    local_levels,
    cross_levels,
    b_own_ref,
    b_other_ref,
    c_own_ref,
    c_other_ref,
    codes_ref,
    scale_ref,
    scaled_ref,
    fall_ref,
    rows_ref,
    spread_ref,
    local_ref,
    reads_ref,
    held,
):
    chunk = pl.program_id(0)

    @pl.when(chunk == 0)
    def _():
        held[...] = jnp.zeros_like(held)

    b_mat = b_own_ref[...].astype(F32) + b_other_ref[...].astype(F32)
    c_mat = (c_own_ref[...].astype(F32) + c_other_ref[...].astype(F32)).astype(BF16)
    lam = codes_ref[...].astype(F32) * scale_ref[...]
    gram = lax.dot_general(
        c_mat, b_mat.astype(BF16), (((1,), (1,)), ((), ())), preferred_element_type=F32
    )
    query_row = lax.broadcasted_iota(jnp.int32, (CHUNK, CHUNK), 0)
    key_lane = lax.broadcasted_iota(jnp.int32, (CHUNK, CHUNK), 1)
    differ = jnp.bitwise_xor(query_row, key_lane)
    inner_levels = CHUNK.bit_length() - 1

    def column(level):
        return jnp.broadcast_to(lam[:, level : level + 1], (CHUNK, CHUNK))

    weight = column(0)
    for level in range(1, inner_levels + 1):
        weight = jnp.where(differ >= 1 << (level - 1), column(level), weight)
    mixing = jnp.where(key_lane <= query_row, gram * weight, 0.0).astype(BF16)
    c_wide = c_mat.astype(F32)
    left = [mixing]
    right = [scaled_ref[...]]
    for level in range(local_levels):
        left.append((c_wide * column(inner_levels + 1 + level)).astype(BF16))
        right.append((held[level] * rows_ref[2:3]).astype(BF16))
    summed = dot(jnp.concatenate(left, axis=1), jnp.concatenate(right, axis=0))
    local_ref[...] = (summed * widen_rows(fall_ref[...], spread_ref[...])).astype(local_ref.dtype)
    for level in range(cross_levels):
        at = inner_levels + 1 + local_levels + level
        reads_ref[:, level * STATES : (level + 1) * STATES] = (c_wide * column(at)).astype(BF16)

    state = dot(b_mat.T.astype(BF16), scaled_ref[...]) * rows_ref[0:1]
    fade = rows_ref[1:2]

    def place(level, joined):
        if level == local_levels:
            return
        taken = jnp.bitwise_and(jnp.right_shift(chunk, level), 1) == 1

        @pl.when(jnp.logical_not(taken))
        def _():
            held[level] = joined
            for later in range(level + 1, local_levels):
                held[later] = held[later] * fade

        @pl.when(taken)
        def _():
            both = joined + held[level] * fade
            held[level] = jnp.zeros_like(joined)
            place(level + 1, both)

    place(0, state)


def local_terms(b_own, b_other, c_own, c_other, codes, scale, scaled, fall, factor_rows, spread, cross_levels):
    row_count, width = scaled.shape
    heads = fall.shape[1]
    levels = codes.shape[1]
    chunks = row_count // CHUNK
    local_levels = chunks.bit_length() - 1

    def rows(columns):
        return pl.BlockSpec((CHUNK, columns), lambda i: (i, 0))

    return pl.pallas_call(
        functools.partial(local_kernel, local_levels, cross_levels),
        grid=(chunks,),
        in_specs=[rows(STATES)] * 4
        + [
            rows(levels),
            fixed((1, levels)),
            rows(width),
            rows(heads),
            pl.BlockSpec((8, width), lambda i: (i, 0)),
            fixed(spread.shape),
        ],
        out_specs=[rows(width), rows(cross_levels * STATES)],
        out_shape=[
            jax.ShapeDtypeStruct((row_count, width), BF16),
            jax.ShapeDtypeStruct((row_count, cross_levels * STATES), BF16),
        ],
        scratch_shapes=[pltpu.VMEM((local_levels, STATES, width), F32)],
        compiler_params=params(),
        cost_estimate=cost(2 * 10**9, 8 * 10**6),
        name="local_terms",
    )(b_own, b_other, c_own, c_other, codes, scale, scaled, fall, factor_rows, spread)


def finish_kernel(
    cross_levels,
    half_ref,
    near_ref,
    own_ref,
    other_ref,
    before_ref,
    reads_ref,
    local_ref,
    hidden_ref,
    carry_ref,
    spread_ref,
    mean_ref,
    gain_ref,
    out_ref,
    carried,
):
    width = hidden_ref.shape[1]
    half_width = width // 2

    @pl.when(pl.program_id(0) == 0)
    def _():
        carried[0:STATES] = (near_ref[...].astype(F32) * before_ref[0:1]).astype(BF16)
        is_low = half_ref[0] == 0
        for level in range(1, cross_levels):
            span = slice((level - 1) * STATES, level * STATES)
            own, other = own_ref[span, :], other_ref[span, :]
            low = jnp.where(is_low, own, other).astype(F32)
            high = jnp.where(is_low, other, own).astype(F32)
            row = before_ref[level : level + 1]
            target = slice(level * STATES, (level + 1) * STATES)
            carried[target, :half_width] = (low * row[:, :half_width]).astype(BF16)
            carried[target, half_width:] = (high * row[:, half_width:]).astype(BF16)

    cross = dot(reads_ref[...], carried[...])
    mixed = local_ref[...].astype(F32) + cross * widen_rows(carry_ref[...], spread_ref[...])
    squares = (mixed * mixed).astype(BF16)
    tile = mean_ref.shape[0]
    for at in range(0, width, tile):
        lanes = slice(at, at + tile)
        mean = dot(squares[:, lanes], mean_ref[...])
        normed = mixed[:, lanes] * lax.rsqrt(mean + 1e-05) * gain_ref[:, lanes]
        out_ref[:, lanes] = (hidden_ref[:, lanes].astype(F32) + normed).astype(BF16)


def finish(half, near, own, other, before, reads, local, hidden, carry, spread, gain):
    row_count, width = hidden.shape
    heads = carry.shape[1]
    cross_levels = before.shape[0]
    tile = min(width, NORM_TILE)
    place = np.arange(tile) // HEAD_VALUES
    mean = jnp.asarray((place[:, None] == place[None, :]) / HEAD_VALUES, BF16)
    step = 2 * CHUNK

    def rows(columns):
        return pl.BlockSpec((step, columns), lambda i: (i, 0))

    return pl.pallas_call(
        functools.partial(finish_kernel, cross_levels),
        grid=(row_count // step,),
        in_specs=[
            pl.BlockSpec(memory_space=pltpu.SMEM),
            fixed(near.shape),
            fixed(own.shape),
            fixed(other.shape),
            fixed(before.shape),
            rows(cross_levels * STATES),
            rows(width),
            rows(width),
            rows(heads),
            fixed(spread.shape),
            fixed(mean.shape),
            fixed(gain.shape),
        ],
        out_specs=rows(width),
        out_shape=jax.ShapeDtypeStruct((row_count, width), BF16),
        scratch_shapes=[pltpu.VMEM((cross_levels * STATES, width), BF16)],
        compiler_params=params(),
        cost_estimate=cost(2 * 10**9, 8 * 10**6),
        name="carried_and_norm",
    )(half, near, own, other, before, reads, local, hidden, carry, spread, mean, gain)


def from_behind(x, axis, by):
    length = lax.axis_size(axis)
    return lax.ppermute(x, axis, [(i, i + by) for i in range(length - by)])


def partner(x, axis, distance):
    return lax.ppermute(x, axis, [(i, i ^ 1 << distance) for i in range(lax.axis_size(axis))])


def summed_over_heads(share):
    rounds = lax.axis_size("head").bit_length() - 1
    if rounds == 0:
        return share, jnp.zeros_like(share)
    total = share
    for distance in range(rounds - 1):
        total = (total.astype(F32) + partner(total, "head", distance).astype(F32)).astype(BF16)
    return total, partner(total, "head", rounds - 1)


def body(
    residual_in,
    query_rows,
    key_rows,
    value_rows,
    bc_weight,
    decay_rate,
    level_codes,
    level_scale,
    positions,
    ssm_gain,
):
    row_count, width = residual_in.shape
    heads = decay_rate.shape[1]
    chunks = row_count // CHUNK
    half_width = width // 2
    spread = jnp.asarray(np.arange(width)[None, :] // HEAD_VALUES == np.arange(heads)[:, None], BF16)
    half_index = lax.axis_index("fsdp")
    half = half_index.reshape(1).astype(jnp.int32)

    edges = from_behind(
        (key_rows[row_count - WINDOW :], value_rows[row_count - WINDOW :]), ("seq", "fsdp"), 1
    )
    weights = (bc_weight, partner(bc_weight, "fsdp", 0))
    rise, fall, carry, factor_rows, end_rows = decay_factors(decay_rate, spread)
    pos_rows = positions.reshape(chunks, CHUNK)

    held = None
    b_parts, c_parts = [], []
    split = chunks // 2
    for first, count in ((split, chunks - split), (1, split - 1), (0, 1)):
        hidden, scaled, b_part, c_part = attend(
            first,
            count,
            half,
            pos_rows,
            query_rows,
            key_rows,
            value_rows,
            edges if first == 0 else None,
            residual_in,
            weights,
            rise,
            spread,
            held,
        )
        held = (hidden, scaled)
        b_parts.insert(0, summed_over_heads(b_part))
        c_parts.insert(0, c_part)
    c_part = jnp.concatenate(c_parts, axis=0)
    c_own, c_other = summed_over_heads(c_part)
    b_own = jnp.concatenate([part[0] for part in b_parts], axis=0)
    b_other = jnp.concatenate([part[1] for part in b_parts], axis=0)
    state = block_state(b_own, b_other, scaled, factor_rows)

    shard_axes = ("seq", "fsdp")
    shard_total = lax.axis_size(shard_axes)
    shard = lax.axis_index(shard_axes)
    cross_levels = shard_total.bit_length() - 1
    ends = lax.all_gather(end_rows[0], shard_axes)
    shard_idx = jnp.arange(shard_total)
    before_rows, upper_fades, lower_fades = [], [], []
    for level in range(cross_levels):
        is_upper = jnp.bitwise_and(jnp.right_shift(shard, level), 1) == 1
        run = jnp.right_shift(shard, level) << level
        sibling = jnp.bitwise_xor(run, 1 << level)

        def run_end(start, stop):
            inside = (shard_idx >= start) & (shard_idx < stop)
            return jnp.sum(jnp.where(inside[:, None], ends, 0.0), axis=0)

        between = run_end(run, shard)
        own_end = run_end(run, run + (1 << level))
        other_end = run_end(sibling, sibling + (1 << level))
        before_rows.append(jnp.where(is_upper, jnp.exp(between), 0.0))
        upper_fades.append(jnp.where(is_upper, 1.0, jnp.exp(other_end)))
        lower_fades.append(jnp.where(is_upper, jnp.exp(own_end), 1.0))
    stacked = jnp.repeat(jnp.stack(before_rows + upper_fades + lower_fades), HEAD_VALUES, axis=-1)
    before = stacked[:cross_levels]
    own_fades = stacked[cross_levels : 2 * cross_levels]
    other_fades = stacked[2 * cross_levels :]

    def own_half(x):
        return jnp.where(half_index == 0, x[..., :half_width], x[..., half_width:])

    own_fades = own_half(own_fades)
    other_fades = own_half(other_fades)

    near = partner(state, "fsdp", 0)
    joined = (
        own_half(state).astype(F32) * own_fades[0] + own_half(near).astype(F32) * other_fades[0]
    ).astype(BF16)
    received = []
    for level in range(1, cross_levels):
        other = partner(joined, "seq", level - 1)
        received.append(other)
        joined = (joined.astype(F32) * own_fades[level] + other.astype(F32) * other_fades[level]).astype(BF16)
    own_received = jnp.concatenate(received, axis=0)
    other_received = jnp.concatenate([partner(x, "fsdp", 0) for x in received], axis=0)

    local, reads = local_terms(
        b_own,
        b_other,
        c_own,
        c_other,
        level_codes,
        level_scale[None, :],
        scaled,
        fall,
        factor_rows,
        spread,
        cross_levels,
    )
    return finish(
        half, near, own_received, other_received, before, reads, local, hidden, carry, spread, ssm_gain[None, :]
    )


def solution(mesh):
    in_specs = (
        P(("groups", "seq", "fsdp"), "head"),
        P(("groups", "seq", "fsdp"), "head"),
        P(("groups", "seq", "fsdp"), "head"),
        P(("groups", "seq", "fsdp"), "head"),
        P(("head", "fsdp"), None),
        P(("groups", "seq", "fsdp"), "head"),
        P(("groups", "seq", "fsdp"), None),
        P(),
        P(("groups", "seq", "fsdp")),
        P("head"),
    )
    out_specs = P(("groups", "seq", "fsdp"), "head")
    return jax.shard_map(body, mesh=mesh, in_specs=in_specs, out_specs=out_specs, check_vma=False)
```

time: 234 us -> 88.4 us (0.38)
  matrix products: 92.7 us -> 0 us
  local copies, waits for them, and re-layouts: 53 us -> 11.9 us
  other arithmetic: 41 us -> 0.41 us
  Pallas kernels: 0 us -> 33.1 us
  blocking collectives: 33.2 us -> 10 us
  waiting for transfers between devices: 1.11 us -> 18.8 us
    dot_general x22 -> x0, matrix products: 92.7 us -> none  [the longest x16 61.1 us: head_term(): return jnp.dot(mixing, values_head, preferred_element_type=jnp.float32)]
    pallas_call x0 -> x7, Pallas kernels: none -> 33.1 us  [the longest x3 13.4 us: attend(): pl.pallas_call(functools.partial(attend_kernel, first, len(aliased)), gri...]
    psum x1 -> x0, blocking collectives: 30.9 us -> none  [body(): bc_full = lax.psum(partial_value, 'head').astype(jnp.bfloat16)]
    ppermute x5 -> x10, waiting for transfers between devices: 1.1 us -> 18.8 us  [partner(): lax.ppermute(x, axis, [(i, i ^ 1 << distance) for i in range(lax.axis_siz...]
    slice x9 -> x5, local copies, waits for them, and re-layouts: 13.7 us -> 0.27 us  [the longest x1 0.09 us: body(): other_fades = stacked[2 * cross_levels:]]
    mul x8 -> x0, local copies, waits for them, and re-layouts: 10.8 us -> none  [the longest x2 7.98 us: body(): jnp.exp(log_end[None, :] - log_cum)[:, :, None]]
    convert_element_type x2, other arithmetic: 8.31 us -> 0.14 us  [the longest x1 0.09 us: body(): joined = (own_half(state).astype(F32) * own_fades[0] + own_half(near).ast...]
    all_gather x1, blocking collectives: 2.29 us -> 10 us  [body(): ends = lax.all_gather(end_rows[0], shard_axes)]
  transfers between devices with their start and end apart: 7 -> 12, of which waited for: 1 -> 6; matrix products, arithmetic and copies ran while one was open for 61% -> 6% of each run, Pallas kernels for 0% -> 26%
where the time goes in v1:
time: 88.4 us; the launch traced here: 87.5 us
  Pallas kernels  33.1 us (37%)
  waiting for transfers between devices  18.8 us (21%)
  starting transfers between devices  12.8 us (14%)
  local copies, waits for them, and re-layouts  11.9 us (13%)
  blocking collectives  10 us (11%)
    ppermute x10, waiting for transfers between devices, partner(): lax.ppermute(x, axis, [(i, i ^ 1 << distance) for i in range(lax.axis_siz...  18.8 us
    pallas_call x3, Pallas kernels, attend(): pl.pallas_call(functools.partial(attend_kernel, first, len(aliased)), gri...  13.4 us
    all_gather x1, blocking collectives, body(): ends = lax.all_gather(end_rows[0], shard_axes)  10 us
    pallas_call x1, Pallas kernels, local_terms(): pl.pallas_call(functools.partial(local_kernel, local_levels, cross_levels...  8.82 us
    unnamed x49, local copies, waits for them, and re-layouts  8.01 us
    ppermute x2, starting transfers between devices, from_behind(): return lax.ppermute(x, axis, [(i, i + by) for i in range(length - by)])  7.22 us
    pallas_call x1, Pallas kernels, finish(): pl.pallas_call(functools.partial(finish_kernel, cross_levels), grid=(row_...  6.33 us
    ppermute x10, starting transfers between devices, partner(): lax.ppermute(x, axis, [(i, i ^ 1 << distance) for i in range(lax.axis_siz...  5.61 us
  transfers between devices with their start and end apart: 12, of which 6 were waited for; matrix products, arithmetic and copies ran while one was open for 6% of the time, Pallas kernels for 26%

profile of v1, /device:TPU:0, one launch (start us, length us, event | category | flops | bytes accessed | tf_op | source)
XLA Modules:
  0.0 87.5 jit_solution(12848340928799049491)
XLA Ops:
  0.0 0.5 collective-permute-start.2
  0.5 1.7 %slice.63 = bf16[128,1024]{1,0:T(8,128)(2,1)} slice(bf16[1024,1024]{1,0:T(8,128)(2,1)} %key_ref.5), slice={[896:1024], [0:1024]} | slice | bytes 524288 | tf_op jit(solution)/shard_map/slice | solution.py:473
  2.2 2.0 %collective-permute-start = (bf16[128,1024]{1,0:T(8,128)(2,1)}, bf16[128,1024]{1,0:T(8,128)(2,1)S(1)}, u32[]{:S(2)}, u32[]{:S(2)}) collective-permute-start(bf16[128,1024]{1,0:T(8,128)(2,1)} %slice.63), channel_id=1, source_target_pairs={{0,1},{1,4},{4,5},{5,8},{8,9},{9,12},{12,13},{2,3},{3,6},{6,7},{7,... | collective-permute-start | bytes 786440 | tf_op jit(solution)/shard_map/ppermute | solution.py:435
  4.2 1.7 %slice.64 = bf16[128,1024]{1,0:T(8,128)(2,1)} slice(bf16[1024,1024]{1,0:T(8,128)(2,1)} %value_ref.5), slice={[896:1024], [0:1024]} | slice | bytes 524288 | tf_op jit(solution)/shard_map/slice | solution.py:473
  5.8 5.3 %collective-permute-start.1 = (bf16[128,1024]{1,0:T(8,128)(2,1)}, bf16[128,1024]{1,0:T(8,128)(2,1)}, u32[]{:S(2)}, u32[]{:S(2)}) collective-permute-start(bf16[128,1024]{1,0:T(8,128)(2,1)} %slice.64), channel_id=1, source_target_pairs={{0,1},{1,4},{4,5},{5,8},{8,9},{9,12},{12,13},{2,3},{3,6},{6,7},{7,... | collective-permute-start | bytes 786440 | tf_op jit(solution)/shard_map/ppermute | solution.py:435
  11.1 1.0 %copy.20.rate_ref = f32[1024,16]{1,0:T(8,128)S(1)} copy(f32[1024,16]{0,1:T(8,128)} %param.18) | data formatting | bytes 131072 | tf_op args[5]
  12.2 0.0 copy-start.3
  12.2 0.7 copy-done.3
  12.9 0.9 %copy-done.13 = bf16[128,384]{1,0:T(8,128)(2,1)S(1)} copy-done((bf16[128,384]{1,0:T(8,128)(2,1)S(1)}, bf16[128,384]{1,0:T(8,128)(2,1)}, u32[]{:S(2)}) %copy-start.13) | copy-done | bytes 98328
  13.8 2.9 %decay_factors.1 = (f32[1024,16]{1,0:T(8,128)S(1)}, f32[1024,16]{1,0:T(8,128)S(1)}, f32[1024,16]{1,0:T(8,128)S(1)}, f32[64,1024]{1,0:T(8,128)S(1)}, f32[8,16]{1,0:T(8,128)S(1)}) custom-call(f32[1024,16]{1,0:T(8,128)S(1)} %copy.20.rate_ref, bf16[128,384]{1,0:T(8,128)(2,1)S(1)} %copy-done.13, bf16[16,1024]{1,0:T(8,128)(2,1)S(1)} %copy-done.3), custom_call_target="tpu_custom_call" | custom-call | flops 100000000 | bytes 5000000 | tf_op jit(solution)/shard_map/decay_factors/pallas_call | solution.py:83
  16.7 0.0 copy-start.5
  16.7 0.8 copy-done.5
  17.5 0.7 copy-done.9
  18.2 0.8 copy-done.16
  19.0 10.0 %all-gather = f32[8,1,16]{2,1,0:T(1,128)S(1)} all-gather(f32[1,1,16]{2,1,0:T(1,128)S(1)} %slice_bitcast_fusion), channel_id=1, replica_groups=mesh['groups'=2,'seq'=4,'head'=2,'fsdp'=2] {'seq','fsdp'}, dimensions={0}, use_global_device_ids=true | all-gather | bytes 576 | tf_op jit(solution)/shard_map/all_gather | solution.py:511
  29.1 0.1 select_reduce_fusion.2
  29.3 0.1 broadcast_in_dim.106
  29.3 0.1 slice.74
  29.5 0.1 broadcast_in_dim.102
  29.6 0.1 slice.68
  29.7 6.1 %window_attention.3 = (bf16[1024,1024]{1,0:T(8,128)(2,1)S(1)}, bf16[1024,1024]{1,0:T(8,128)(2,1)S(1)}, bf16[512,128]{1,0:T(8,128)(2,1)S(1)}, bf16[512,128]{1,0:T(8,128)(2,1)S(1)}) custom-call(s32[1]{0:T(128)} %bitcast.half_ref, s32[8,128]{1,0:T(8,128)S(1)} %bitcast.29, bf16[1024,1024]{1,0:T(8,128)(2,1)} %query_ref.5, bf16[1024,1024]{1,0:T(8,128)(2,1)} %key_ref.5, ...), custom_call_target="tpu_custom_call" | custom-call | flops 1200000000 | bytes 8000000 | tf_op jit(solution)/shard_map/window_attention/pallas_call | solution.py:187
  35.8 4.9 %window_attention.4 = (bf16[1024,1024]{1,0:T(8,128)(2,1)S(1)}, bf16[1024,1024]{1,0:T(8,128)(2,1)S(1)}, bf16[384,128]{1,0:T(8,128)(2,1)S(1)}, bf16[384,128]{1,0:T(8,128)(2,1)S(1)}) custom-call(s32[1]{0:T(128)} %bitcast.half_ref, s32[8,128]{1,0:T(8,128)S(1)} %bitcast.30, bf16[1024,1024]{1,0:T(8,128)(2,1)} %query_ref.5, ...), custom_call_target="tpu_custom_call", output_to_operand_aliasing={{0}: (12, {}), {1}: (13, {})} | custom-call | flops 900000000 | bytes 6000000 | tf_op jit(solution)/shard_map/window_attention/pallas_call | solution.py:187
  40.8 2.4 %window_attention.5 = (bf16[1024,1024]{1,0:T(8,128)(2,1)S(1)}, bf16[1024,1024]{1,0:T(8,128)(2,1)S(1)}, bf16[128,128]{1,0:T(8,128)(2,1)S(1)}, bf16[128,128]{1,0:T(8,128)(2,1)S(1)}) custom-call(s32[1]{0:T(128)} %bitcast.half_ref, s32[8,128]{1,0:T(8,128)S(1)} %bitcast.31, bf16[1024,1024]{1,0:T(8,128)(2,1)} %query_ref.5, ...), custom_call_target="tpu_custom_call", output_to_operand_aliasing={{0}: (12, {}), {1}: (13, {})} | custom-call | flops 300000000 | bytes 2000000 | tf_op jit(solution)/shard_map/window_attention/pallas_call | solution.py:187
  43.2 1.6 %collective-permute-start.3 = (bf16[128,128]{1,0:T(8,128)(2,1)S(1)}, bf16[128,128]{1,0:T(8,128)(2,1)S(1)}, u32[]{:S(2)}, u32[]{:S(2)}) collective-permute-start(bf16[128,128]{1,0:T(8,128)(2,1)S(1)} %get-tuple-element.29), channel_id=1, source_target_pairs={{0,2},{2,0},{1,3},{3,1},{4,6},{6,4},{5,7},{7,5},{8,10},{10,8},{9,1... | collective-permute-start | bytes 98312 | tf_op jit(solution)/shard_map/ppermute | solution.py:439
  44.7 0.5 collective-permute-start.4
  45.3 1.5 %collective-permute-start.5 = (bf16[512,128]{1,0:T(8,128)(2,1)S(1)}, bf16[512,128]{1,0:T(8,128)(2,1)S(1)}, u32[]{:S(2)}, u32[]{:S(2)}) collective-permute-start(bf16[512,128]{1,0:T(8,128)(2,1)S(1)} %get-tuple-element.31), channel_id=1, source_target_pairs={{0,2},{2,0},{1,3},{3,1},{4,6},{6,4},{5,7},{7,5},{8,10},{10,8},{9,1... | collective-permute-start | bytes 393224 | tf_op jit(solution)/shard_map/ppermute | solution.py:439
  46.8 0.4 collective-permute-done.3
  47.2 3.2 %collective-permute-done.4 = bf16[384,128]{1,0:T(8,128)(2,1)S(1)} collective-permute-done((bf16[384,128]{1,0:T(8,128)(2,1)S(1)}, bf16[384,128]{1,0:T(8,128)(2,1)S(1)}, u32[]{:S(2)}, u32[]{:S(2)}) %collective-permute-start.4) | collective-permute-done | bytes 98336 | tf_op jit(solution)/shard_map/ppermute | solution.py:439
  50.4 1.9 %collective-permute-done.5 = bf16[512,128]{1,0:T(8,128)(2,1)S(1)} collective-permute-done((bf16[512,128]{1,0:T(8,128)(2,1)S(1)}, bf16[512,128]{1,0:T(8,128)(2,1)S(1)}, u32[]{:S(2)}, u32[]{:S(2)}) %collective-permute-start.5) | collective-permute-done | bytes 131104 | tf_op jit(solution)/shard_map/ppermute | solution.py:439
  52.3 0.0 copy-start.19
  52.3 1.7 %block_state.1 = bf16[128,1024]{1,0:T(8,128)(2,1)S(1)} custom-call(bf16[1024,128]{1,0:T(8,128)(2,1)S(1)} %constant_dynamic-update-slice_fusion.own_ref.b_own_ref, bf16[1024,128]{1,0:T(8,128)(2,1)S(1)} %constant_dynamic-update-slice_fusion.3.other_ref.b_other_ref, bf16[1024,1024]{1,0:T(8,128)(2,1)S(1)} %get-tuple-element.32.scaled_ref, f32[64,1024]{1,0:T(8,128)S(1)} %copy-done.10), custom_call_target="tpu_custom_call" | custom-call | flops 300000000 | bytes 4000000 | tf_op jit(solution)/shard_map/block_state/pallas_call | solution.py:222
  54.1 0.7 copy-done.7
  54.8 1.5 %collective-permute-done.6.near_ref = bf16[128,1024]{1,0:T(8,128)(2,1)S(1)} collective-permute-done((bf16[128,1024]{1,0:T(8,128)(2,1)S(1)}, bf16[128,1024]{1,0:T(8,128)(2,1)S(1)}, u32[]{:S(2)}, u32[]{:S(2)}) %collective-permute-start.6) | collective-permute-done | bytes 262176 | tf_op jit(solution)/shard_map/ppermute | solution.py:439
  56.3 0.1 add_convert_fusion.1
  56.4 0.4 collective-permute-start.7
  56.8 1.0 %collective-permute-start.11 = (bf16[1024,128]{1,0:T(8,128)(2,1)S(1)}, bf16[1024,128]{1,0:T(8,128)(2,1)S(1)}, u32[]{:S(2)}, u32[]{:S(2)}) collective-permute-start(bf16[1024,128]{1,0:T(8,128)(2,1)S(1)} %constant_dynamic-update-slice_fusion.6.c_own_ref), channel_id=1, source_target_pairs={{0,2},{2,0},{1,3},{3,1},{4,6},{6,4},{5,7},{7,5},{8,10},{10,8},{9,1... | collective-permute-start | bytes 786440 | tf_op jit(solution)/shard_map/ppermute | solution.py:439
  57.8 4.2 %collective-permute-done.7 = bf16[128,512]{1,0:T(8,128)(2,1)S(1)} collective-permute-done((bf16[128,512]{1,0:T(8,128)(2,1)S(1)}, bf16[128,512]{1,0:T(8,128)(2,1)S(1)}, u32[]{:S(2)}, u32[]{:S(2)}) %collective-permute-start.7) | collective-permute-done | bytes 131104 | tf_op jit(solution)/shard_map/ppermute | solution.py:439
  62.0 0.1 add_convert_fusion
  62.0 0.1 collective-permute-start.8
  62.1 0.2 copy.21.codes_ref
  62.4 0.1 broadcast_in_dim.111
  62.5 0.1 slice.80.before_ref
  62.5 0.0 collective-permute-start.9
  62.6 7.7 %collective-permute-done.8 = bf16[128,512]{1,0:T(8,128)(2,1)S(1)} collective-permute-done((bf16[128,512]{1,0:T(8,128)(2,1)S(1)}, bf16[128,512]{1,0:T(8,128)(2,1)S(1)}, u32[]{:S(2)}, u32[]{:S(2)}) %collective-permute-start.8) | collective-permute-done | bytes 131104 | tf_op jit(solution)/shard_map/ppermute | solution.py:439
  70.3 0.9 %copy-done.11 = f32[64,1024]{1,0:T(8,128)S(1)} copy-done((f32[64,1024]{1,0:T(8,128)S(1)}, f32[64,1024]{1,0:T(8,128)}, u32[]{:S(2)}) %copy-start.11) | copy-done | bytes 262168
  71.2 1.0 %copy-done.17 = f32[1024,16]{1,0:T(8,128)S(1)} copy-done((f32[1024,16]{1,0:T(8,128)S(1)}, f32[1024,16]{1,0:T(8,128)}, u32[]{:S(2)}) %copy-start.17) | copy-done | bytes 65560
  72.3 8.8 %local_terms.1 = (bf16[1024,1024]{1,0:T(8,128)(2,1)S(1)}, bf16[1024,384]{1,0:T(8,128)(2,1)S(1)}) custom-call(bf16[1024,128]{1,0:T(8,128)(2,1)S(1)} %constant_dynamic-update-slice_fusion.own_ref.b_own_ref, bf16[1024,128]{1,0:T(8,128)(2,1)S(1)} %copy-done.8, bf16[1024,128]{1,0:T(8,128)(2,1)S(1)} %constant_dynamic-update-slice_fusion.6.c_own_ref, ...), custom_call_target="tpu_custom_call" | custom-call | flops 2000000000 | bytes 8000000 | tf_op jit(solution)/shard_map/local_terms/pallas_call | solution.py:326
  81.2 6.3 %carried_and_norm.1 = bf16[1024,1024]{1,0:T(8,128)(2,1)} custom-call(s32[1]{0:T(128)} %bitcast.half_ref, bf16[128,1024]{1,0:T(8,128)(2,1)S(1)} %collective-permute-done.6.near_ref, bf16[256,512]{1,0:T(8,128)(2,1)S(1)} %pad_maximum_fusion.own_ref, bf16[256,512]{1,0:T(8,128)(2,1)S(1)} %pad_maximum_fusion.1.other_ref, f32[3,1024]{1,0:T(4,128)S(1)} %slice.80.before_ref, ...), custom_call_target="tpu_custom_call" | custom-call | flops 2000000000 | bytes 8000000 | tf_op jit(solution)/shard_map/carried_and_norm/pallas_call | solution.py:407
  (70 shorter events, 0.4 us)
Async XLA Ops:
  0.0 29.7 %copy-start.4 = (bf16[16,1024]{1,0:T(8,128)(2,1)S(1)}, bf16[16,1024]{1,0:T(8,128)(2,1)}, u32[]{:S(2)}) copy-start(bf16[16,1024]{1,0:T(8,128)(2,1)} %constant.27.clone.spread_ref) | copy-start | bytes 98308
  0.0 29.7 %copy-start.2 = (bf16[512,256]{1,0:T(8,128)(2,1)S(1)}, bf16[512,256]{1,0:T(8,128)(2,1)}, u32[]{:S(2)}) copy-start(bf16[512,256]{1,0:T(8,128)(2,1)} %own_weight_ref.5) | copy-start | bytes 786436
  0.0 29.7 %copy-start.14 = (s32[1024]{0:T(1024)S(1)}, s32[1024]{0:T(1024)}, u32[]{:S(2)}) copy-start(s32[1024]{0:T(1024)} %param.21) | copy-start | bytes 12292
  0.0 29.7 %collective-permute-start.2 = (bf16[512,256]{1,0:T(8,128)(2,1)}, bf16[512,256]{1,0:T(8,128)(2,1)S(1)}, u32[]{:S(2)}, u32[]{:S(2)}) collective-permute-start(bf16[512,256]{1,0:T(8,128)(2,1)} %own_weight_ref.5), channel_id=1, source_target_pairs={{0,1},{1,0},{2,3},{3,2},{4,5},{5,4},{6,7},{7,6},{8,9},{9,8},{10,11... | collective-permute-start | bytes 786440 | tf_op jit(solution)/shard_map/ppermute | solution.py:439
  2.2 38.6 %collective-permute-start = (bf16[128,1024]{1,0:T(8,128)(2,1)}, bf16[128,1024]{1,0:T(8,128)(2,1)S(1)}, u32[]{:S(2)}, u32[]{:S(2)}) collective-permute-start(bf16[128,1024]{1,0:T(8,128)(2,1)} %slice.63), channel_id=1, source_target_pairs={{0,1},{1,4},{4,5},{5,8},{8,9},{9,12},{12,13},{2,3},{3,6},{6,7},{7,... | collective-permute-start | bytes 786440 | tf_op jit(solution)/shard_map/ppermute | solution.py:435
  5.8 34.9 %collective-permute-start.1 = (bf16[128,1024]{1,0:T(8,128)(2,1)}, bf16[128,1024]{1,0:T(8,128)(2,1)}, u32[]{:S(2)}, u32[]{:S(2)}) collective-permute-start(bf16[128,1024]{1,0:T(8,128)(2,1)} %slice.64), channel_id=1, source_target_pairs={{0,1},{1,4},{4,5},{5,8},{8,9},{9,12},{12,13},{2,3},{3,6},{6,7},{7,... | collective-permute-start | bytes 786440 | tf_op jit(solution)/shard_map/ppermute | solution.py:435
  12.2 0.8 copy-start.3
  12.9 0.9 %copy-start.13 = (bf16[128,384]{1,0:T(8,128)(2,1)S(1)}, bf16[128,384]{1,0:T(8,128)(2,1)}, u32[]{:S(2)}) copy-start(bf16[128,384]{1,0:T(8,128)(2,1)} %constant.28.clone.lower_ref) | copy-start | bytes 294916
  16.7 0.8 copy-start.5
  17.5 0.7 copy-start.9
  18.2 0.8 copy-start.16
  40.8 11.5 %copy-start.10 = (f32[64,1024]{1,0:T(8,128)S(1)}, f32[64,1024]{1,0:T(8,128)}, u32[]{:S(2)}) copy-start(f32[64,1024]{1,0:T(8,128)} %copy-done.9) | copy-start | bytes 786436
  43.2 10.9 %copy-start = (bf16[1024,1024]{1,0:T(8,128)(2,1)}, bf16[1024,1024]{1,0:T(8,128)(2,1)S(1)}, u32[]{:S(2)}) copy-start(bf16[1024,1024]{1,0:T(8,128)(2,1)S(1)} %get-tuple-element.32.scaled_ref) | copy-start | bytes 6291460
  43.2 10.9 %copy-start.1 = (bf16[1024,1024]{1,0:T(8,128)(2,1)}, bf16[1024,1024]{1,0:T(8,128)(2,1)S(1)}, u32[]{:S(2)}) copy-start(bf16[1024,1024]{1,0:T(8,128)(2,1)S(1)} %get-tuple-element.41.hidden_ref) | copy-start | bytes 6291460
  43.2 4.0 %collective-permute-start.3 = (bf16[128,128]{1,0:T(8,128)(2,1)S(1)}, bf16[128,128]{1,0:T(8,128)(2,1)S(1)}, u32[]{:S(2)}, u32[]{:S(2)}) collective-permute-start(bf16[128,128]{1,0:T(8,128)(2,1)S(1)} %get-tuple-element.29), channel_id=1, source_target_pairs={{0,2},{2,0},{1,3},{3,1},{4,6},{6,4},{5,7},{7,5},{8,10},{10,8},{9,1... | collective-permute-start | bytes 98312 | tf_op jit(solution)/shard_map/ppermute | solution.py:439
  44.7 5.7 %collective-permute-start.4 = (bf16[384,128]{1,0:T(8,128)(2,1)S(1)}, bf16[384,128]{1,0:T(8,128)(2,1)S(1)}, u32[]{:S(2)}, u32[]{:S(2)}) collective-permute-start(bf16[384,128]{1,0:T(8,128)(2,1)S(1)} %get-tuple-element.30), channel_id=1, source_target_pairs={{0,2},{2,0},{1,3},{3,1},{4,6},{6,4},{5,7},{7,5},{8,10},{10,8},{9,1... | collective-permute-start | bytes 294920 | tf_op jit(solution)/shard_map/ppermute | solution.py:439
  45.3 7.0 %collective-permute-start.5 = (bf16[512,128]{1,0:T(8,128)(2,1)S(1)}, bf16[512,128]{1,0:T(8,128)(2,1)S(1)}, u32[]{:S(2)}, u32[]{:S(2)}) collective-permute-start(bf16[512,128]{1,0:T(8,128)(2,1)S(1)} %get-tuple-element.31), channel_id=1, source_target_pairs={{0,2},{2,0},{1,3},{3,1},{4,6},{6,4},{5,7},{7,5},{8,10},{10,8},{9,1... | collective-permute-start | bytes 393224 | tf_op jit(solution)/shard_map/ppermute | solution.py:439
  52.3 9.8 %copy-start.19 = (s32[1024,18]{0,1:T(8,128)S(1)}, s32[1024,18]{0,1:T(8,128)}, u32[]{:S(2)}) copy-start(s32[1024,18]{0,1:T(8,128)} %param.19) | copy-start | bytes 221188
  52.3 18.0 %copy-start.18 = (f32[18]{0:T(128)S(1)}, f32[18]{0:T(128)}, u32[]{:S(2)}) copy-start(f32[18]{0:T(128)} %param.20) | copy-start | bytes 220
  54.1 0.7 copy-start.7
  54.8 1.5 %collective-permute-start.6 = (bf16[128,1024]{1,0:T(8,128)(2,1)S(1)}, bf16[128,1024]{1,0:T(8,128)(2,1)S(1)}, u32[]{:S(2)}, u32[]{:S(2)}) collective-permute-start(bf16[128,1024]{1,0:T(8,128)(2,1)S(1)} %block_state.1), channel_id=1, source_target_pairs={{0,1},{1,0},{2,3},{3,2},{4,5},{5,4},{6,7},{7,6},{8,9},{9,8},{10,11... | collective-permute-start | bytes 786440 | tf_op jit(solution)/shard_map/ppermute | solution.py:439
  54.8 15.5 %copy-start.8 = (bf16[1024,128]{1,0:T(8,128)(2,1)S(1)}, bf16[1024,128]{1,0:T(8,128)(2,1)}, u32[]{:S(2)}) copy-start(bf16[1024,128]{1,0:T(8,128)(2,1)} %copy-done.7) | copy-start | bytes 786436
  56.4 5.6 %collective-permute-start.7 = (bf16[128,512]{1,0:T(8,128)(2,1)S(1)}, bf16[128,512]{1,0:T(8,128)(2,1)S(1)}, u32[]{:S(2)}, u32[]{:S(2)}) collective-permute-start(bf16[128,512]{1,0:T(8,128)(2,1)S(1)} %add_convert_fusion.1), channel_id=1, source_target_pairs={{0,4},{4,0},{8,12},{12,8},{1,5},{5,1},{9,13},{13,9},{2,6},{6,2},{1... | collective-permute-start | bytes 393224 | tf_op jit(solution)/shard_map/ppermute | solution.py:439
  56.8 13.5 %collective-permute-start.11 = (bf16[1024,128]{1,0:T(8,128)(2,1)S(1)}, bf16[1024,128]{1,0:T(8,128)(2,1)S(1)}, u32[]{:S(2)}, u32[]{:S(2)}) collective-permute-start(bf16[1024,128]{1,0:T(8,128)(2,1)S(1)} %constant_dynamic-update-slice_fusion.6.c_own_ref), channel_id=1, source_target_pairs={{0,2},{2,0},{1,3},{3,1},{4,6},{6,4},{5,7},{7,5},{8,10},{10,8},{9,1... | collective-permute-start | bytes 786440 | tf_op jit(solution)/shard_map/ppermute | solution.py:439
  62.0 8.2 %collective-permute-start.8 = (bf16[128,512]{1,0:T(8,128)(2,1)S(1)}, bf16[128,512]{1,0:T(8,128)(2,1)S(1)}, u32[]{:S(2)}, u32[]{:S(2)}) collective-permute-start(bf16[128,512]{1,0:T(8,128)(2,1)S(1)} %add_convert_fusion), channel_id=1, source_target_pairs={{0,8},{4,12},{8,0},{12,4},{1,9},{5,13},{9,1},{13,5},{2,10},{6,14},... | collective-permute-start | bytes 393224 | tf_op jit(solution)/shard_map/ppermute | solution.py:439
  62.5 18.6 %collective-permute-start.9 = (bf16[128,512]{1,0:T(8,128)(2,1)S(1)}, bf16[128,512]{1,0:T(8,128)(2,1)S(1)}, u32[]{:S(2)}, u32[]{:S(2)}) collective-permute-start(bf16[128,512]{1,0:T(8,128)(2,1)S(1)} %collective-permute-done.7), channel_id=1, source_target_pairs={{0,1},{1,0},{2,3},{3,2},{4,5},{5,4},{6,7},{7,6},{8,9},{9,8},{10,11... | collective-permute-start | bytes 393224 | tf_op jit(solution)/shard_map/ppermute | solution.py:439
  70.3 10.9 %collective-permute-start.10 = (bf16[128,512]{1,0:T(8,128)(2,1)S(1)}, bf16[128,512]{1,0:T(8,128)(2,1)S(1)}, u32[]{:S(2)}, u32[]{:S(2)}) collective-permute-start(bf16[128,512]{1,0:T(8,128)(2,1)S(1)} %collective-permute-done.8), channel_id=1, source_target_pairs={{0,1},{1,0},{2,3},{3,2},{4,5},{5,4},{6,7},{7,6},{8,9},{9,8},{10,11... | collective-permute-start | bytes 393224 | tf_op jit(solution)/shard_map/ppermute | solution.py:439
  70.3 1.0 %copy-start.11 = (f32[64,1024]{1,0:T(8,128)S(1)}, f32[64,1024]{1,0:T(8,128)}, u32[]{:S(2)}) copy-start(f32[64,1024]{1,0:T(8,128)} %copy-done.9) | copy-start | bytes 786436
  71.2 1.0 %copy-start.17 = (f32[1024,16]{1,0:T(8,128)S(1)}, f32[1024,16]{1,0:T(8,128)}, u32[]{:S(2)}) copy-start(f32[1024,16]{1,0:T(8,128)} %copy-done.16) | copy-start | bytes 196612
  72.3 8.9 %copy-start.6 = (f32[1024,16]{1,0:T(8,128)S(1)}, f32[1024,16]{1,0:T(8,128)}, u32[]{:S(2)}) copy-start(f32[1024,16]{1,0:T(8,128)} %copy-done.5) | copy-start | bytes 196612
  72.3 8.9 %copy-start.12 = (bf16[256,256]{1,0:T(8,128)(2,1)S(1)}, bf16[256,256]{1,0:T(8,128)(2,1)}, u32[]{:S(2)}) copy-start(bf16[256,256]{1,0:T(8,128)(2,1)} %constant.29.clone.mean_ref) | copy-start | bytes 393220
  72.3 8.9 %copy-start.15 = (f32[1024]{0:T(1024)S(1)}, f32[1024]{0:T(1024)}, u32[]{:S(2)}) copy-start(f32[1024]{0:T(1024)} %param.22) | copy-start | bytes 12292

commit v2 on v0

v2 whole, which is shorter than its diff:
```python
import functools
import math

import jax
import jax.numpy as jnp
from jax import lax
from jax.experimental import pallas as pl
from jax.experimental.pallas import tpu as pltpu
from jax.sharding import PartitionSpec as P

HEAD_DIM = 128
HEAD_VALUES = 64
STATES = 128
WINDOW = 128
CHUNK = 128
EXTRA = 16
VMEM_LIMIT = 24 * 1024 * 1024
HIDDEN = -1e30

F32 = jnp.float32
BF16 = jnp.bfloat16
VMEM = pl.BlockSpec(memory_space=pltpu.VMEM)
SMEM = pl.BlockSpec(memory_space=pltpu.SMEM)
HBM = pl.BlockSpec(memory_space=pltpu.HBM)


def params():
    return pltpu.CompilerParams(vmem_limit_bytes=VMEM_LIMIT)


def cost(flops, moved, transcendentals=0):
    return pl.CostEstimate(flops=flops, bytes_accessed=moved, transcendentals=transcendentals)


def shaped(shape, dtype):
    return pltpu.VMEM(shape, dtype)


def far_shaped(shape, dtype):
    return pltpu.HBM(shape, dtype)


def near_by(*arrays):
    return [pltpu.with_memory_space_constraint(x, pltpu.VMEM) for x in arrays]


def far_off(*arrays):
    return [pltpu.with_memory_space_constraint(x, pltpu.HBM) for x in arrays]


def dot(left, right):
    return jnp.dot(left, right, preferred_element_type=F32)


def dot_turned(left, right):
    return lax.dot_general(left, right, (((1,), (1,)), ((), ())), preferred_element_type=F32)


def chunk_rows(index, count=1):
    return pl.ds(pl.multiple_of(index * CHUNK, CHUNK), count * CHUNK)


def spread_matrix(heads, width):
    lane = lax.broadcasted_iota(jnp.int32, (heads, width), 1)
    start = lax.broadcasted_iota(jnp.int32, (heads, width), 0) * HEAD_VALUES
    return ((lane >= start) & (lane < start + HEAD_VALUES)).astype(F32).astype(BF16)


def lane_tiles(width):
    tile = min(width, 256)
    return [slice(at, at + tile) for at in range(0, width, tile)]


def split_rows(rows):
    high = rows.astype(BF16)
    return high, (rows - high.astype(F32)).astype(BF16)


def edge_kernel(key_ref, value_ref, edge_ref, sems):
    row_count = key_ref.shape[0]
    copies = [
        pltpu.make_async_copy(
            ref.at[pl.ds(row_count - WINDOW, WINDOW)], edge_ref.at[pl.ds(at * WINDOW, WINDOW)], sems.at[at]
        )
        for at, ref in enumerate((key_ref, value_ref))
    ]
    for copy in copies:
        copy.start()
    for copy in copies:
        copy.wait()


def edge_rows(key_rows, value_rows):
    width = key_rows.shape[1]
    return pl.pallas_call(
        edge_kernel,
        in_specs=[HBM, HBM],
        out_specs=VMEM,
        out_shape=shaped((2 * WINDOW, width), BF16),
        scratch_shapes=[pltpu.SemaphoreType.DMA((2,))],
        compiler_params=params(),
        cost_estimate=cost(0, 2**20),
        name="edge_rows",
    )(*far_off(key_rows, value_rows))


def chunk_masks(doc_pos):
    key_row = lax.broadcasted_iota(jnp.int32, (WINDOW, WINDOW), 0)
    query_lane = lax.broadcasted_iota(jnp.int32, (WINDOW, WINDOW), 1)
    away = query_lane - key_row
    away = jnp.where(away < 0, away + WINDOW, away)
    bias = jnp.where(away <= doc_pos, 0.0, HIDDEN).astype(F32).T
    return bias


def attend_chunk(bias, query, key_before, key, value_before, value, residual):
    query_row = lax.broadcasted_iota(jnp.int32, (WINDOW, WINDOW), 0)
    key_lane = lax.broadcasted_iota(jnp.int32, (WINDOW, WINDOW), 1)
    current = key_lane <= query_row
    current_share = current.astype(F32).astype(BF16)
    before_share = (1.0 - current.astype(F32)).astype(BF16)
    ones = jnp.ones((2 * WINDOW, HEAD_DIM), BF16)
    factor = math.log2(math.e) / math.sqrt(HEAD_DIM)
    scores = dot_turned(query, jnp.concatenate([key_before, key], axis=0))
    merged = jnp.where(current, scores[:, WINDOW:], scores[:, :WINDOW]) + bias
    top = jnp.max(merged, axis=1, keepdims=True)
    weights = jnp.exp2((merged - top) * factor).astype(BF16)
    weights = jnp.concatenate([weights * before_share, weights * current_share], axis=1)
    values = jnp.concatenate([value_before, value], axis=0)
    summed = dot(weights, jnp.concatenate([values, ones], axis=1))
    attended = summed[:, :HEAD_DIM] / summed[:, HEAD_DIM:]
    return (residual.astype(F32) + attended).astype(BF16)


def attend_heads(bias, width, query, key_before, key, value_before, value, residual, hidden):
    def lanes_of(at, ref, rows):
        return ref[rows, at : at + HEAD_DIM]

    for at in range(0, width, HEAD_DIM):
        hidden[0][hidden[1], at : at + HEAD_DIM] = attend_chunk(
            bias,
            lanes_of(at, *query),
            lanes_of(at, *key_before),
            lanes_of(at, *key),
            lanes_of(at, *value_before),
            lanes_of(at, *value),
            lanes_of(at, *residual),
        )


def most_kernel(
    place_ref,
    pos_ref,
    query_ref,
    key_ref,
    value_ref,
    residual_ref,
    own_weight_ref,
    other_weight_ref,
    hidden_ref,
    hidden_far_ref,
    b_ref,
    c_ref,
    weight_ref,
    first_query_ref,
    first_key_ref,
    first_value_ref,
    first_residual_ref,
    query_buf,
    key_buf,
    value_buf,
    residual_buf,
    sems,
    out_sems,
):
    row_count, width = query_ref.shape
    chunks = row_count // CHUNK
    half_width = width // 2
    arrays = (
        (key_ref, key_buf, first_key_ref),
        (value_ref, value_buf, first_value_ref),
        (query_ref, query_buf, first_query_ref),
        (residual_ref, residual_buf, first_residual_ref),
    )

    def copy(which, chunk):
        source, buffer, _ = arrays[which]
        rows = chunk_rows(chunk)
        return pltpu.make_async_copy(source.at[rows], buffer.at[rows], sems.at[which, chunk])

    def copy_out(chunk):
        rows = chunk_rows(chunk)
        return pltpu.make_async_copy(hidden_ref.at[rows], hidden_far_ref.at[rows], out_sems.at[chunk])

    for which in range(2):
        copy(which, 0).start()
    for chunk in range(1, chunks):
        for which in range(4):
            copy(which, chunk).start()
    for which in range(2, 4):
        copy(which, 0).start()
    is_low = place_ref[0] == 0
    own_weight, other_weight = own_weight_ref[...], other_weight_ref[...]
    weight_ref[:half_width, :] = jnp.where(is_low, own_weight, other_weight)
    weight_ref[half_width:, :] = jnp.where(is_low, other_weight, own_weight)
    for which in range(2):
        copy(which, 0).wait()

    def step(chunk, carry):
        for which in range(4):
            copy(which, chunk).wait()
        rows, before = chunk_rows(chunk), chunk_rows(chunk - 1)
        bias = chunk_masks(pos_ref[pl.ds(chunk, 1), :])
        attend_heads(
            bias,
            width,
            (query_buf, rows),
            (key_buf, before),
            (key_buf, rows),
            (value_buf, before),
            (value_buf, rows),
            (residual_buf, rows),
            (hidden_ref, rows),
        )
        copy_out(chunk).start()
        shared = dot(hidden_ref[rows, :], weight_ref[...])
        b_ref[chunk_rows(chunk - 1), :] = shared[:, :STATES].astype(BF16)
        c_ref[rows, :] = shared[:, STATES:].astype(BF16)
        return carry

    lax.fori_loop(1, chunks, step, 0)
    for which in range(2, 4):
        copy(which, 0).wait()
    for _, buffer, first in arrays:
        first[...] = buffer[:CHUNK]
    for chunk in range(1, chunks):
        copy_out(chunk).wait()


def attend_most(place, positions, query, key, value, residual, weights):
    row_count, width = query.shape
    chunks = row_count // CHUNK
    return pl.pallas_call(
        most_kernel,
        in_specs=[SMEM, VMEM] + [HBM] * 4 + [VMEM] * 2,
        out_specs=[VMEM, HBM] + [VMEM] * 7,
        out_shape=[
            shaped((row_count, width), BF16),
            far_shaped((row_count, width), BF16),
            shaped((row_count - CHUNK, STATES), BF16),
            shaped((row_count, STATES), BF16),
            shaped((width, 2 * STATES), BF16),
        ]
        + [shaped((CHUNK, width), BF16)] * 4,
        scratch_shapes=[pltpu.VMEM((row_count, width), BF16)] * 4
        + [pltpu.SemaphoreType.DMA((4, chunks)), pltpu.SemaphoreType.DMA((chunks,))],
        compiler_params=params(),
        cost_estimate=cost(3 * 10**9, 10**7),
        name="attention_most",
    )(place, *near_by(positions), *far_off(query, key, value, residual), *near_by(*weights))


def first_kernel(
    pos_ref,
    edge_ref,
    query_ref,
    key_ref,
    value_ref,
    residual_ref,
    weight_ref,
    hidden_in_ref,
    hidden_far_in_ref,
    c_in_ref,
    hidden_ref,
    hidden_far_ref,
    c_ref,
    b_ref,
    c_far_ref,
    sems,
):
    width = query_ref.shape[1]
    rows = slice(0, CHUNK)
    attend_heads(
        chunk_masks(pos_ref[0:1, :]),
        width,
        (query_ref, rows),
        (edge_ref, slice(0, WINDOW)),
        (key_ref, rows),
        (edge_ref, slice(WINDOW, 2 * WINDOW)),
        (value_ref, rows),
        (residual_ref, rows),
        (hidden_ref, rows),
    )
    span = pl.ds(0, CHUNK)
    hidden_copy = pltpu.make_async_copy(hidden_ref.at[span], hidden_far_ref.at[span], sems.at[0])
    hidden_copy.start()
    shared = dot(hidden_ref[rows, :], weight_ref[...])
    b_ref[...] = shared[:, :STATES].astype(BF16)
    c_ref[rows, :] = shared[:, STATES:].astype(BF16)
    c_copy = pltpu.make_async_copy(c_ref, c_far_ref, sems.at[1])
    c_copy.start()
    hidden_copy.wait()
    c_copy.wait()


def attend_first(positions, edges, firsts, weight, hidden, hidden_far, c_mat):
    width = hidden.shape[1]
    return pl.pallas_call(
        first_kernel,
        in_specs=[VMEM] * 8 + [HBM, VMEM],
        out_specs=[VMEM, HBM, VMEM, VMEM, HBM],
        out_shape=[
            shaped(hidden.shape, BF16),
            far_shaped(hidden.shape, BF16),
            shaped(c_mat.shape, BF16),
            shaped((CHUNK, STATES), BF16),
            far_shaped(c_mat.shape, BF16),
        ],
        input_output_aliases={7: 0, 8: 1, 9: 2},
        scratch_shapes=[pltpu.SemaphoreType.DMA((2,))],
        compiler_params=params(),
        cost_estimate=cost(4 * 10**8, 2 * 10**6),
        name="attention_first",
    )(*near_by(positions, edges, *firsts, weight, hidden), *far_off(hidden_far), *near_by(c_mat))


def lower_ones():
    row = lax.broadcasted_iota(jnp.int32, (CHUNK, CHUNK), 0)
    lane = lax.broadcasted_iota(jnp.int32, (CHUNK, CHUNK), 1)
    lower = (lane <= row).astype(F32).astype(BF16)
    return jnp.concatenate([lower] * 3, axis=1)


def chunk_sums(lower, rate):
    first = rate.astype(BF16)
    second, third = split_rows(rate - first.astype(F32))
    return dot_turned(lower, jnp.concatenate([first, second, third], axis=1))


def scale_kernel(rate_ref, hidden_ref, scaled_ref, rows_ref):
    heads, row_count = rate_ref.shape
    width = hidden_ref.shape[1]
    spread = spread_matrix(heads, width)
    lower = lower_ones()
    row_idx = lax.broadcasted_iota(jnp.int32, (8, heads), 0)

    def step(chunk, token):
        rows = chunk_rows(chunk)
        total = chunk_sums(lower, rate_ref[:, rows])
        middle = total[CHUNK // 2 - 1 : CHUNK // 2]
        last = total[CHUNK - 1 :]
        rise = jnp.exp(total - middle).astype(BF16)
        logs = jnp.where(
            row_idx == 0,
            middle - last,
            jnp.where(row_idx == 1, -last, jnp.where(row_idx == 2, -middle, 0.0)),
        )
        high, low = split_rows(jnp.exp(logs))
        factors = pl.ds(pl.multiple_of(chunk * 8, 8), 8)
        for lanes in lane_tiles(width):
            wide = dot(rise, spread[:, lanes])
            scaled_ref[rows, lanes] = (wide * hidden_ref[rows, lanes].astype(F32)).astype(BF16)
            rows_ref[factors, lanes] = dot(high, spread[:, lanes]) + dot(low, spread[:, lanes])
        return token

    lax.fori_loop(0, row_count // CHUNK, step, 0)


def scale_hidden(rate_turned, hidden):
    row_count, width = hidden.shape
    return pl.pallas_call(
        scale_kernel,
        in_specs=[VMEM] * 2,
        out_specs=[VMEM] * 2,
        out_shape=[shaped((row_count, width), BF16), shaped((row_count // CHUNK * 8, width), F32)],
        compiler_params=params(),
        cost_estimate=cost(10**9, 4 * 10**6),
        name="scale_hidden",
    )(*near_by(rate_turned, hidden))


def state_kernel(
    own_first_ref,
    own_most_ref,
    other_first_ref,
    other_most_ref,
    scaled_ref,
    rows_ref,
    state_ref,
    b_far_ref,
    b_buf,
    turned,
    sems,
):
    row_count, width = scaled_ref.shape
    chunks = row_count // CHUNK
    b_buf[:CHUNK, :] = (own_first_ref[...].astype(F32) + other_first_ref[...].astype(F32)).astype(BF16)
    b_buf[CHUNK:, :] = (own_most_ref[...].astype(F32) + other_most_ref[...].astype(F32)).astype(BF16)
    b_copy = pltpu.make_async_copy(b_buf, b_far_ref, sems.at[0])
    b_copy.start()
    for chunk in range(chunks):
        span = slice(chunk * CHUNK, (chunk + 1) * CHUNK)
        turned[:, span] = b_buf[span, :].astype(F32).T.astype(BF16)
    tile = min(width, 256)

    def step(at, carry):
        lanes = pl.ds(pl.multiple_of(at * tile, tile), tile)
        total = fade = None
        for chunk in range(chunks):
            span = slice(chunk * CHUNK, (chunk + 1) * CHUNK)
            added = dot(turned[:, span], scaled_ref[span, lanes]) * rows_ref[chunk * 8 : chunk * 8 + 1, lanes]
            fades = rows_ref[chunk * 8 + 1 : chunk * 8 + 2, lanes]
            total = added if total is None else total * fades + added
            fade = fades if fade is None else fade * fades
        state_ref[:STATES, lanes] = total.astype(BF16)
        state_ref[STATES:, lanes] = fade_rows(fade)
        return carry

    lax.fori_loop(0, width // tile, step, 0)
    b_copy.wait()


def fade_rows(fade):
    high, low = split_rows(fade)
    row = lax.broadcasted_iota(jnp.int32, (EXTRA, fade.shape[1]), 0)
    return jnp.where(row == 0, high.astype(F32), jnp.where(row == 1, low.astype(F32), 0.0)).astype(BF16)


def fade_of(message):
    return message[STATES : STATES + 1].astype(F32) + message[STATES + 1 : STATES + 2].astype(F32)


def block_state(own_first, own_most, other_first, other_most, scaled, factor_rows):
    row_count, width = scaled.shape
    return pl.pallas_call(
        state_kernel,
        in_specs=[VMEM] * 6,
        out_specs=[VMEM, HBM],
        out_shape=[shaped((STATES + EXTRA, width), BF16), far_shaped((row_count, STATES), BF16)],
        scratch_shapes=[
            pltpu.VMEM((row_count, STATES), BF16),
            pltpu.VMEM((STATES, row_count), BF16),
            pltpu.SemaphoreType.DMA((1,)),
        ],
        compiler_params=params(),
        cost_estimate=cost(3 * 10**8, 4 * 10**6),
        name="block_state",
    )(*near_by(own_first, own_most, other_first, other_most, scaled, factor_rows))


def join_kernel(level, place_ref, own_ref, other_ref, joined_ref):
    half_width = joined_ref.shape[1]
    own, other = own_ref[...], other_ref[...]
    if own.shape[1] != half_width:
        is_low = place_ref[0] == 0
        own = jnp.where(is_low, own[:, :half_width], own[:, half_width:])
        other = jnp.where(is_low, other[:, :half_width], other[:, half_width:])
    upper = place_ref[1 + level] == 1
    own_fade, other_fade = fade_of(own), fade_of(other)
    lower, higher = jnp.where(upper, other, own), jnp.where(upper, own, other)
    fade = jnp.where(upper, own_fade, other_fade)
    joined_ref[:STATES, :] = (lower[:STATES].astype(F32) * fade + higher[:STATES].astype(F32)).astype(BF16)
    joined_ref[STATES:, :] = fade_rows(own_fade * other_fade)


def join(level, place, own, other, half_width):
    return pl.pallas_call(
        functools.partial(join_kernel, level),
        in_specs=[SMEM, VMEM, VMEM],
        out_specs=VMEM,
        out_shape=shaped((own.shape[0], half_width), BF16),
        compiler_params=params(),
        cost_estimate=cost(10**6, 10**5),
        name="join_runs",
    )(place, *near_by(own, other))


def local_kernel(
    local_levels,
    cross_levels,
    b_far_ref,
    c_far_ref,
    c_other_ref,
    codes_ref,
    scale_ref,
    rate_ref,
    scaled_ref,
    rows_ref,
    local_ref,
    reads_ref,
    carry_wide_ref,
    b_buf,
    c_buf,
    held,
    fresh,
    sems,
):
    row_count, width = scaled_ref.shape
    heads = rate_ref.shape[0]
    copies = [
        pltpu.make_async_copy(b_far_ref, b_buf, sems.at[0]),
        pltpu.make_async_copy(c_far_ref, c_buf, sems.at[1]),
    ]
    for copy in copies:
        copy.start()
    spread = spread_matrix(heads, width)
    lower = lower_ones()
    held[...] = jnp.zeros_like(held)
    query_row = lax.broadcasted_iota(jnp.int32, (CHUNK, CHUNK), 0)
    key_lane = lax.broadcasted_iota(jnp.int32, (CHUNK, CHUNK), 1)
    differ = jnp.bitwise_xor(query_row, key_lane)
    inner_levels = CHUNK.bit_length() - 1
    for copy in copies:
        copy.wait()

    def step(chunk, prefix):
        rows = chunk_rows(chunk)
        factors = pl.ds(pl.multiple_of(chunk * 8, 8), 8)
        total = chunk_sums(lower, rate_ref[:, rows])
        fall = jnp.exp(total[CHUNK // 2 - 1 : CHUNK // 2] - total).astype(BF16)
        carry = jnp.exp(-(total + prefix)).astype(BF16)
        b_mat = b_buf[rows, :]
        c_wide = (c_buf[rows, :].astype(F32) + c_other_ref[rows, :].astype(F32)).astype(BF16).astype(F32)
        lam = codes_ref[:, rows].astype(F32).T * scale_ref[...]
        gram = dot_turned(c_wide.astype(BF16), b_mat)

        def column(level):
            return jnp.broadcast_to(lam[:, level : level + 1], (CHUNK, CHUNK))

        weight = column(0)
        for level in range(1, inner_levels + 1):
            weight = jnp.where(differ >= 1 << (level - 1), column(level), weight)
        left = [jnp.where(key_lane <= query_row, gram * weight, 0.0).astype(BF16)]
        for level in range(local_levels):
            left.append((c_wide * column(inner_levels + 1 + level)).astype(BF16))
        left = jnp.concatenate(left, axis=1)
        for level in range(cross_levels):
            at = inner_levels + 1 + local_levels + level
            reads_ref[rows, level * STATES : (level + 1) * STATES] = (c_wide * column(at)).astype(BF16)
        b_turned = b_mat.astype(F32).T.astype(BF16)
        for lanes in lane_tiles(width):
            factor = rows_ref[factors, lanes]
            scaled = scaled_ref[rows, lanes]
            right = [scaled]
            for level in range(local_levels):
                right.append((held[level, :, lanes] * factor[2:3]).astype(BF16))
            summed = dot(left, jnp.concatenate(right, axis=0))
            local_ref[rows, lanes] = (summed * dot(fall, spread[:, lanes])).astype(BF16)
            carry_wide_ref[rows, lanes] = dot(carry, spread[:, lanes]).astype(BF16)
            fresh[:, lanes] = dot(b_turned, scaled) * factor[0:1]

        fade = rows_ref[factors, :][1:2]

        def put(level):
            if level == local_levels:
                return
            taken = jnp.bitwise_and(jnp.right_shift(chunk, level), 1) == 1

            @pl.when(jnp.logical_not(taken))
            def _():
                held[level] = fresh[...]
                for later in range(level + 1, local_levels):
                    held[later] = held[later] * fade

            @pl.when(taken)
            def _():
                fresh[...] = fresh[...] + held[level] * fade
                held[level] = jnp.zeros((STATES, width), F32)
                put(level + 1)

        put(0)
        return prefix + total[CHUNK - 1 :]

    lax.fori_loop(0, row_count // CHUNK, step, jnp.zeros((1, heads), F32))


def local_terms(b_far, c_far, c_other, codes_turned, scale, rate_turned, scaled, factor_rows, cross_levels):
    row_count, width = scaled.shape
    local_levels = (row_count // CHUNK).bit_length() - 1
    return pl.pallas_call(
        functools.partial(local_kernel, local_levels, cross_levels),
        in_specs=[HBM] * 2 + [VMEM] * 6,
        out_specs=[VMEM] * 3,
        out_shape=[
            shaped((row_count, width), BF16),
            shaped((row_count, cross_levels * STATES), BF16),
            shaped((row_count, width), BF16),
        ],
        scratch_shapes=[
            pltpu.VMEM((row_count, STATES), BF16),
            pltpu.VMEM((row_count, STATES), BF16),
            pltpu.VMEM((local_levels, STATES, width), F32),
            pltpu.VMEM((STATES, width), F32),
            pltpu.SemaphoreType.DMA((2,)),
        ],
        compiler_params=params(),
        cost_estimate=cost(3 * 10**9, 10**7),
        name="local_terms",
    )(
        *far_off(b_far, c_far),
        *near_by(c_other, codes_turned, scale, rate_turned, scaled, factor_rows),
    )


def finish_kernel(cross_levels, place_ref, hidden_far_ref, reads_ref, local_ref, carry_wide_ref, gain_ref, near_ref, *refs):
    received = refs[: cross_levels - 1]
    swapped = refs[cross_levels - 1 : 2 * (cross_levels - 1)]
    out_ref, carried, hidden_buf, result, in_sems, out_sems = refs[2 * (cross_levels - 1) :]
    row_count, width = local_ref.shape
    chunks = row_count // CHUNK
    step_chunks = 2 if chunks % 2 == 0 else 1
    steps = chunks // step_chunks

    def copy_in(at):
        rows = chunk_rows(at * step_chunks, step_chunks)
        return pltpu.make_async_copy(hidden_far_ref.at[rows], hidden_buf.at[rows], in_sems.at[at])

    def copy_out(at):
        rows = chunk_rows(at * step_chunks, step_chunks)
        return pltpu.make_async_copy(result.at[rows], out_ref.at[rows], out_sems.at[at])

    for at in range(steps):
        copy_in(at).start()
    is_low = place_ref[0] == 0
    before = jnp.ones((1, width), F32)
    for level in range(cross_levels):
        upper = place_ref[1 + level]
        if level == 0:
            message = near_ref[...]
        else:
            own, other = received[level - 1][...], swapped[level - 1][...]
            message = jnp.concatenate(
                [jnp.where(is_low, own, other), jnp.where(is_low, other, own)], axis=1
            )
        carried[level * STATES : (level + 1) * STATES, :] = (
            message[:STATES].astype(F32) * (before * upper.astype(F32))
        ).astype(BF16)
        before = jnp.where(upper == 1, before * fade_of(message), before)

    tiles = lane_tiles(width)
    tile = tiles[0].stop
    row = lax.broadcasted_iota(jnp.int32, (tile, tile), 0) // HEAD_VALUES
    lane = lax.broadcasted_iota(jnp.int32, (tile, tile), 1) // HEAD_VALUES
    mean_mat = jnp.where(row == lane, 1.0 / HEAD_VALUES, 0.0).astype(BF16)

    def step(at, token):
        rows = chunk_rows(at * step_chunks, step_chunks)
        copy_in(at).wait()
        reads = reads_ref[rows, :]
        for lanes in tiles:
            cross = dot(reads, carried[:, lanes])
            mixed = local_ref[rows, lanes].astype(F32) + cross * carry_wide_ref[rows, lanes].astype(F32)
            mean = dot((mixed * mixed).astype(BF16), mean_mat)
            normed = mixed * lax.rsqrt(mean + 1e-05) * gain_ref[:, lanes]
            result[rows, lanes] = (hidden_buf[rows, lanes].astype(F32) + normed).astype(BF16)
        copy_out(at).start()
        return token

    lax.fori_loop(0, steps, step, 0)
    for at in range(steps):
        copy_out(at).wait()


def finish(place, hidden_far, reads, local, carry_wide, gain, near, received, swapped):
    row_count, width = local.shape
    cross_levels = 1 + len(received)
    chunks = row_count // CHUNK
    return pl.pallas_call(
        functools.partial(finish_kernel, cross_levels),
        in_specs=[SMEM, HBM] + [VMEM] * (5 + 2 * len(received)),
        out_specs=HBM,
        out_shape=jax.ShapeDtypeStruct((row_count, width), BF16),
        scratch_shapes=[
            pltpu.VMEM((cross_levels * STATES, width), BF16),
            pltpu.VMEM((row_count, width), BF16),
            pltpu.VMEM((row_count, width), BF16),
            pltpu.SemaphoreType.DMA((chunks,)),
            pltpu.SemaphoreType.DMA((chunks,)),
        ],
        compiler_params=params(),
        cost_estimate=cost(2 * 10**9, 8 * 10**6),
        name="carried_and_norm",
    )(place, *far_off(hidden_far), *near_by(reads, local, carry_wide, gain, near, *received, *swapped))


def from_behind(x, axis, by):
    length = lax.axis_size(axis)
    return lax.ppermute(x, axis, [(i, i + by) for i in range(length - by)])


def partner(x, axis, distance):
    return lax.ppermute(x, axis, [(i, i ^ 1 << distance) for i in range(lax.axis_size(axis))])


def summed_over_heads(share):
    rounds = lax.axis_size("head").bit_length() - 1
    if rounds == 0:
        return share, jnp.zeros_like(share)
    total = share
    for distance in range(rounds - 1):
        total = (total.astype(F32) + partner(total, "head", distance).astype(F32)).astype(BF16)
    return total, partner(total, "head", rounds - 1)


def body(
    residual_in,
    query_rows,
    key_rows,
    value_rows,
    bc_weight,
    decay_rate,
    level_codes,
    level_scale,
    positions,
    ssm_gain,
):
    row_count, width = residual_in.shape
    half_width = width // 2
    shard_axes = ("seq", "fsdp")
    cross_levels = lax.axis_size(shard_axes).bit_length() - 1
    shard = lax.axis_index(shard_axes)
    half_index = lax.axis_index("fsdp")
    place = jnp.stack(
        [half_index] + [jnp.bitwise_and(jnp.right_shift(shard, level), 1) for level in range(cross_levels)]
    ).astype(jnp.int32)

    weights = (bc_weight, partner(bc_weight, "fsdp", 0))
    edges = from_behind(edge_rows(key_rows, value_rows), shard_axes, 1)
    pos_rows = positions.reshape(row_count // CHUNK, CHUNK)
    hidden, hidden_far, b_most, c_mat, weight, *firsts = attend_most(
        place, pos_rows, query_rows, key_rows, value_rows, residual_in, weights
    )
    b_most, b_most_other = summed_over_heads(b_most)
    hidden, hidden_far, c_mat, b_first, c_far = attend_first(
        pos_rows, edges, firsts, weight, hidden, hidden_far, c_mat
    )
    b_first, b_first_other = summed_over_heads(b_first)
    c_sent, c_other = summed_over_heads(c_mat)
    if lax.axis_size("head") > 2:
        c_far = c_sent
    rate_turned = decay_rate.T
    scaled, factor_rows = scale_hidden(rate_turned, hidden)
    state, b_far = block_state(b_first, b_most, b_first_other, b_most_other, scaled, factor_rows)

    near = partner(state, "fsdp", 0)
    joined = join(0, place, state, near, half_width)
    received = []
    for level in range(1, cross_levels):
        if level == cross_levels - 1:
            joined, c_other = lax.optimization_barrier((joined, c_other))
        received.append(partner(joined, "seq", level - 1))
        if level < cross_levels - 1:
            joined = join(level, place, joined, received[-1], half_width)
    local, reads, carry_wide = local_terms(
        b_far, c_far, c_other, level_codes.T, level_scale[None, :], rate_turned, scaled, factor_rows, cross_levels
    )
    received[-1], local = lax.optimization_barrier((received[-1], local))
    swapped = [partner(x, "fsdp", 0) for x in received]
    return finish(
        place, hidden_far, reads, local, carry_wide, ssm_gain[None, :], near, received, swapped
    )


def solution(mesh):
    in_specs = (
        P(("groups", "seq", "fsdp"), "head"),
        P(("groups", "seq", "fsdp"), "head"),
        P(("groups", "seq", "fsdp"), "head"),
        P(("groups", "seq", "fsdp"), "head"),
        P(("head", "fsdp"), None),
        P(("groups", "seq", "fsdp"), "head"),
        P(("groups", "seq", "fsdp"), None),
        P(),
        P(("groups", "seq", "fsdp")),
        P("head"),
    )
    out_specs = P(("groups", "seq", "fsdp"), "head")
    return jax.shard_map(body, mesh=mesh, in_specs=in_specs, out_specs=out_specs, check_vma=False)
```

time: 234 us -> 56 us (0.24)
  matrix products: 92.7 us -> 0 us
  local copies, waits for them, and re-layouts: 53 us -> 0.03 us
  other arithmetic: 41 us -> 0.08 us
  Pallas kernels: 0 us -> 35.8 us
  blocking collectives: 33.2 us -> 0 us
  waiting for transfers between devices: 1.11 us -> 6.77 us
    dot_general x22 -> x0, matrix products: 92.7 us -> none  [the longest x16 61.1 us: head_term(): return jnp.dot(mixing, values_head, preferred_element_type=jnp.float32)]
    pallas_call x0 -> x9, Pallas kernels: none -> 35.8 us  [the longest x1 10.1 us: attend_most(): pl.pallas_call(most_kernel, in_specs=[SMEM, VMEM] + [HBM] * 4 + [VMEM] *...]
    psum x1 -> x0, blocking collectives: 30.9 us -> none  [body(): bc_full = lax.psum(partial_value, 'head').astype(jnp.bfloat16)]
    slice x11 -> x0, local copies, waits for them, and re-layouts: 17 us -> none  [the longest x1 4.13 us: window_attention(): value_blocks[:block_total]]
    mul x8 -> x0, local copies, waits for them, and re-layouts: 10.8 us -> none  [the longest x2 7.98 us: body(): jnp.exp(log_end[None, :] - log_cum)[:, :, None]]
    unnamed x37 -> x12, local copies, waits for them, and re-layouts: 9.81 us -> 0.03 us
    convert_element_type x2 -> x0, other arithmetic: 8.31 us -> none  [the longest x1 4.28 us: body(): return result.astype(jnp.bfloat16)]
    another operation x5 -> x1, other arithmetic: 7.67 us -> 0.08 us  [body(): jnp.stack([half_index] + [jnp.bitwise_and(jnp.right_shift(shard, level),...]
  transfers between devices with their start and end apart: 7 -> 10, of which waited for: 1 -> 4; matrix products, arithmetic and copies ran while one was open for 61% -> 0% of each run, Pallas kernels for 0% -> 48%
where the time goes in v2:
time: 56 us; the launch traced here: 55.9 us
  Pallas kernels  35.8 us (64%)
  starting transfers between devices  13 us (23%)
  waiting for transfers between devices  6.77 us (12%)
    ppermute x9, starting transfers between devices, partner(): lax.ppermute(x, axis, [(i, i ^ 1 << distance) for i in range(lax.axis_siz...  11 us
    pallas_call x1, Pallas kernels, attend_most(): pl.pallas_call(most_kernel, in_specs=[SMEM, VMEM] + [HBM] * 4 + [VMEM] *...  10.1 us
    pallas_call x1, Pallas kernels, local_terms(): pl.pallas_call(functools.partial(local_kernel, local_levels, cross_levels...  9.79 us
    pallas_call x1, Pallas kernels, finish(): pl.pallas_call(functools.partial(finish_kernel, cross_levels), in_specs=[...  7.4 us
    ppermute x9, waiting for transfers between devices, partner(): lax.ppermute(x, axis, [(i, i ^ 1 << distance) for i in range(lax.axis_siz...  6.77 us
    pallas_call x1, Pallas kernels, scale_hidden(): pl.pallas_call(scale_kernel, in_specs=[VMEM] * 2, out_specs=[VMEM] * 2, o...  3.11 us
    ppermute x1, starting transfers between devices, from_behind(): return lax.ppermute(x, axis, [(i, i + by) for i in range(length - by)])  2.03 us
    pallas_call x1, Pallas kernels, attend_first(): pl.pallas_call(first_kernel, in_specs=[VMEM] * 8 + [HBM, VMEM], out_specs...  1.76 us
  transfers between devices with their start and end apart: 10, of which 4 were waited for; matrix products, arithmetic and copies ran while one was open for 0% of the time, Pallas kernels for 48%

profile of v2, /device:TPU:0, one launch (start us, length us, event | category | flops | bytes accessed | tf_op | source)
XLA Modules:
  0.0 55.9 jit_solution(18238452461918858368)
XLA Ops:
  0.0 0.0 copy-start.2
  0.0 0.0 copy-start.1
  0.0 0.5 collective-permute-start.1
  0.5 1.0 %edge_rows.1 = bf16[256,1024]{1,0:T(8,128)(2,1)S(1)} custom-call(bf16[1024,1024]{1,0:T(8,128)(2,1)} %key_ref.3, bf16[1024,1024]{1,0:T(8,128)(2,1)} %value_ref.3), custom_call_target="tpu_custom_call" | custom-call | bytes 1048576 | tf_op jit(solution)/shard_map/edge_rows/pallas_call | solution.py:95
  1.5 2.0 %collective-permute-start = (bf16[256,1024]{1,0:T(8,128)(2,1)S(1)}, bf16[256,1024]{1,0:T(8,128)(2,1)S(1)}, u32[]{:S(2)}, u32[]{:S(2)}) collective-permute-start(bf16[256,1024]{1,0:T(8,128)(2,1)S(1)} %edge_rows.1), channel_id=1, source_target_pairs={{0,1},{1,4},{4,5},{5,8},{8,9},{9,12},{12,13},{2,3},{3,6},{6,7},{7,... | collective-permute-start | bytes 1572872 | tf_op jit(solution)/shard_map/ppermute | solution.py:688
  3.6 0.1 pad_add_fusion.place_ref
  3.6 0.0 collective-permute-done.1.other_weight_ref
  3.6 0.0 copy-done.2
  3.6 0.0 copy-done.1
  3.6 10.1 %attention_most.1 = (bf16[1024,1024]{1,0:T(8,128)(2,1)S(1)}, bf16[1024,1024]{1,0:T(8,128)(2,1)}, bf16[896,128]{1,0:T(8,128)(2,1)S(1)}, bf16[1024,128]{1,0:T(8,12...) custom-call(s32[4]{0:T(128)S(1)} %pad_add_fusion.place_ref, ...), custom_call_target="tpu_custom_call" | custom-call | flops 3000000000 | bytes 10000000 | tf_op jit(solution)/shard_map/attention_most/pallas_call | solution.py:243
  13.8 3.0 %collective-permute-start.3 = (bf16[896,128]{1,0:T(8,128)(2,1)S(1)}, bf16[896,128]{1,0:T(8,128)(2,1)S(1)}, u32[]{:S(2)}, u32[]{:S(2)}) collective-permute-start(bf16[896,128]{1,0:T(8,128)(2,1)S(1)} %get-tuple-element.40.own_most_ref), channel_id=1, source_target_pairs={{0,2},{2,0},{1,3},{3,1},{4,6},{6,4},{5,7},{7,5},{8,10},{10,8},{9,1... | collective-permute-start | bytes 688136 | tf_op jit(solution)/shard_map/ppermute | solution.py:692
  16.8 0.0 collective-permute-done.edge_ref
  16.8 0.0 copy-start.4
  16.8 1.8 %attention_first.1 = (bf16[1024,1024]{1,0:T(8,128)(2,1)S(1)}, bf16[1024,1024]{1,0:T(8,128)(2,1)}, bf16[1024,128]{1,0:T(8,128)(2,1)S(1)}, bf16[128,128]{1,0:T(8,128)(2,1)S(1)}, bf16[1024,128]{1,0:T(8,128)(2,1)}) custom-call(s32[8,128]{1,0:T(8,128)S(1)} %bitcast.11, ...), custom_call_target="tpu_custom_call", output_to_operand_aliasing={{0}: (7, {}), {1}: (8, {}), {2}: (9, {})} | custom-call | flops 400000000 | bytes 2000000 | tf_op jit(solution)/shard_map/attention_first/pallas_call | solution.py:308
  18.5 0.1 collective-permute-start.2
  18.6 0.0 copy-done.4
  18.6 3.1 %scale_hidden.1 = (bf16[1024,1024]{1,0:T(8,128)(2,1)S(1)}, f32[64,1024]{1,0:T(8,128)S(1)}) custom-call(f32[16,1024]{1,0:T(8,128)S(1)} %bitcast.13, bf16[1024,1024]{1,0:T(8,128)(2,1)S(1)} %get-tuple-element.41.hidden_ref), custom_call_target="tpu_custom_call" | custom-call | flops 1000000000 | bytes 4000000 | tf_op jit(solution)/shard_map/scale_hidden/pallas_call | solution.py:371
  21.7 0.0 copy-start.3
  21.8 0.0 copy-start.5
  21.8 0.7 %collective-permute-done.3.other_most_ref = bf16[896,128]{1,0:T(8,128)(2,1)S(1)} collective-permute-done((bf16[896,128]{1,0:T(8,128)(2,1)S(1)}, bf16[896,128]{1,0:T(8,128)(2,1)S(1)}, u32[]{:S(2)}, u32[]{:S(2)}) %collective-permute-start.3) | collective-permute-done | bytes 229408 | tf_op jit(solution)/shard_map/ppermute | solution.py:692
  22.5 0.7 %collective-permute-done.2.other_first_ref = bf16[128,128]{1,0:T(8,128)(2,1)S(1)} collective-permute-done((bf16[128,128]{1,0:T(8,128)(2,1)S(1)}, bf16[128,128]{1,0:T(8,128)(2,1)S(1)}, u32[]{:S(2)}, u32[]{:S(2)}) %collective-permute-start.2) | collective-permute-done | bytes 32800 | tf_op jit(solution)/shard_map/ppermute | solution.py:692
  23.2 1.4 %block_state.1 = (bf16[144,1024]{1,0:T(8,128)(2,1)S(1)}, bf16[1024,128]{1,0:T(8,128)(2,1)}) custom-call(bf16[128,128]{1,0:T(8,128)(2,1)S(1)} %get-tuple-element.39.own_first_ref, bf16[896,128]{1,0:T(8,128)(2,1)S(1)} %get-tuple-element.40.own_most_ref, bf16[128,128]{1,0:T(8,128)(2,1)S(1)} %collective-permute-done.2.other_first_ref, ...), custom_call_target="tpu_custom_call" | custom-call | flops 300000000 | bytes 4000000 | tf_op jit(solution)/shard_map/block_state/pallas_call | solution.py:435
  24.6 0.6 %collective-permute-start.4 = (bf16[144,1024]{1,0:T(8,128)(2,1)S(1)}, bf16[144,1024]{1,0:T(8,128)(2,1)S(1)}, u32[]{:S(2)}, u32[]{:S(2)}) collective-permute-start(bf16[144,1024]{1,0:T(8,128)(2,1)S(1)} %get-tuple-element.46.own_ref), channel_id=1, source_target_pairs={{0,1},{1,0},{2,3},{3,2},{4,5},{5,4},{6,7},{7,6},{8,9},{9,8},{10,11... | collective-permute-start | bytes 884744 | tf_op jit(solution)/shard_map/ppermute | solution.py:692
  25.2 2.1 %collective-permute-start.6 = (bf16[1024,128]{1,0:T(8,128)(2,1)S(1)}, bf16[1024,128]{1,0:T(8,128)(2,1)S(1)}, u32[]{:S(2)}, u32[]{:S(2)}) collective-permute-start(bf16[1024,128]{1,0:T(8,128)(2,1)S(1)} %get-tuple-element.47), channel_id=1, source_target_pairs={{0,2},{2,0},{1,3},{3,1},{4,6},{6,4},{5,7},{7,5},{8,10},{10,8},{9,1... | collective-permute-start | bytes 786440 | tf_op jit(solution)/shard_map/ppermute | solution.py:692
  27.3 0.0 collective-permute-done.4.other_ref.near_ref
  27.3 0.6 %join_runs.2.own_ref = bf16[144,512]{1,0:T(8,128)(2,1)S(1)} custom-call(s32[4]{0:T(128)S(1)} %pad_add_fusion.place_ref, bf16[144,1024]{1,0:T(8,128)(2,1)S(1)} %get-tuple-element.46.own_ref, bf16[144,1024]{1,0:T(8,128)(2,1)S(1)} %collective-permute-done.4.other_ref.near_ref), custom_call_target="tpu_custom_call" | custom-call | flops 1000000 | bytes 100000 | tf_op jit(solution)/shard_map/join_runs/pallas_call | solution.py:467
  27.9 1.6 %collective-permute-start.5 = (bf16[144,512]{1,0:T(8,128)(2,1)S(1)}, bf16[144,512]{1,0:T(8,128)(2,1)S(1)}, u32[]{:S(2)}, u32[]{:S(2)}) collective-permute-start(bf16[144,512]{1,0:T(8,128)(2,1)S(1)} %join_runs.2.own_ref), channel_id=1, source_target_pairs={{0,4},{4,0},{8,12},{12,8},{1,5},{5,1},{9,13},{13,9},{2,6},{6,2},{1... | collective-permute-start | bytes 442376 | tf_op jit(solution)/shard_map/ppermute | solution.py:692
  29.5 4.3 %collective-permute-done.5.other_ref.refs_0_ = bf16[144,512]{1,0:T(8,128)(2,1)S(1)} collective-permute-done((bf16[144,512]{1,0:T(8,128)(2,1)S(1)}, bf16[144,512]{1,0:T(8,128)(2,1)S(1)}, u32[]{:S(2)}, u32[]{:S(2)}) %collective-permute-start.5) | collective-permute-done | bytes 147488 | tf_op jit(solution)/shard_map/ppermute | solution.py:692
  33.8 0.6 %join_runs.3 = bf16[144,512]{1,0:T(8,128)(2,1)S(1)} custom-call(s32[4]{0:T(128)S(1)} %pad_add_fusion.place_ref, bf16[144,512]{1,0:T(8,128)(2,1)S(1)} %join_runs.2.own_ref, bf16[144,512]{1,0:T(8,128)(2,1)S(1)} %collective-permute-done.5.other_ref.refs_0_), custom_call_target="tpu_custom_call" | custom-call | flops 1000000 | bytes 100000 | tf_op jit(solution)/shard_map/join_runs/pallas_call | solution.py:467
  34.4 0.0 collective-permute-done.6.c_other_ref
  34.4 2.6 %collective-permute-start.7 = (bf16[144,512]{1,0:T(8,128)(2,1)S(1)}, bf16[144,512]{1,0:T(8,128)(2,1)S(1)}, u32[]{:S(2)}, u32[]{:S(2)}) collective-permute-start(bf16[144,512]{1,0:T(8,128)(2,1)S(1)} %join_runs.3), channel_id=1, source_target_pairs={{0,8},{4,12},{8,0},{12,4},{1,9},{5,13},{9,1},{13,5},{2,10},{6,14},... | collective-permute-start | bytes 442376 | tf_op jit(solution)/shard_map/ppermute | solution.py:692
  37.0 0.0 collective-permute-start.8
  37.0 0.0 copy-done.3
  37.0 0.0 copy-done.5
  37.0 0.0 copy-start
  37.1 9.8 %local_terms.1 = (bf16[1024,1024]{1,0:T(8,128)(2,1)S(1)}, bf16[1024,384]{1,0:T(8,128)(2,1)S(1)}, bf16[1024,1024]{1,0:T(8,128)(2,1)S(1)}) custom-call(bf16[1024,128]{1,0:T(8,128)(2,1)} %get-tuple-element.44.b_far_ref, bf16[1024,128]{1,0:T(8,128)(2,1)} %get-tuple-element.45.c_far_ref, bf16[1024,128]{1,0:T(8,128)(2,1)S(1)} %collective-permute-done.6.c_other_ref, ...), custom_call_target="tpu_custom_call" | custom-call | flops 3000000000 | bytes 10000000 | tf_op jit(solution)/shard_map/local_terms/pallas_call | solution.py:580
  46.9 0.0 collective-permute-done.7.refs_1_
  46.9 0.6 %collective-permute-start.9 = (bf16[144,512]{1,0:T(8,128)(2,1)S(1)}, bf16[144,512]{1,0:T(8,128)(2,1)S(1)}, u32[]{:S(2)}, u32[]{:S(2)}) collective-permute-start(bf16[144,512]{1,0:T(8,128)(2,1)S(1)} %collective-permute-done.7.refs_1_), channel_id=1, source_target_pairs={{0,1},{1,0},{2,3},{3,2},{4,5},{5,4},{6,7},{7,6},{8,9},{9,8},{10,11... | collective-permute-start | bytes 442376 | tf_op jit(solution)/shard_map/ppermute | solution.py:692
  47.4 0.0 collective-permute-done.8.refs_2_
  47.4 1.0 %collective-permute-done.9.refs_3_ = bf16[144,512]{1,0:T(8,128)(2,1)S(1)} collective-permute-done((bf16[144,512]{1,0:T(8,128)(2,1)S(1)}, bf16[144,512]{1,0:T(8,128)(2,1)S(1)}, u32[]{:S(2)}, u32[]{:S(2)}) %collective-permute-start.9) | collective-permute-done | bytes 147488 | tf_op jit(solution)/shard_map/ppermute | solution.py:692
  48.5 0.0 copy-done
  48.5 7.4 %carried_and_norm.1 = bf16[1024,1024]{1,0:T(8,128)(2,1)} custom-call(s32[4]{0:T(128)S(1)} %pad_add_fusion.place_ref, bf16[1024,1024]{1,0:T(8,128)(2,1)} %get-tuple-element.38.hidden_far_ref, bf16[1024,384]{1,0:T(8,128)(2,1)S(1)} %get-tuple-element.49.reads_ref, bf16[1024,1024]{1,0:T(8,128)(2,1)S(1)} %get-tuple-element.52.local_ref, ...), custom_call_target="tpu_custom_call" | custom-call | flops 2000000000 | bytes 8000000 | tf_op jit(solution)/shard_map/carried_and_norm/pallas_call | solution.py:668
Async XLA Ops:
  0.0 3.6 %copy-start.2 = (bf16[512,256]{1,0:T(8,128)(2,1)S(1)}, bf16[512,256]{1,0:T(8,128)(2,1)}, u32[]{:S(2)}) copy-start(bf16[512,256]{1,0:T(8,128)(2,1)} %own_weight_ref.1) | copy-start | bytes 786436
  0.0 3.6 %copy-start.1 = (s32[1024]{0:T(1024)S(1)}, s32[1024]{0:T(1024)}, u32[]{:S(2)}) copy-start(s32[1024]{0:T(1024)} %param.18) | copy-start | bytes 12292
  0.0 3.6 %collective-permute-start.1 = (bf16[512,256]{1,0:T(8,128)(2,1)}, bf16[512,256]{1,0:T(8,128)(2,1)S(1)}, u32[]{:S(2)}, u32[]{:S(2)}) collective-permute-start(bf16[512,256]{1,0:T(8,128)(2,1)} %own_weight_ref.1), channel_id=1, source_target_pairs={{0,1},{1,0},{2,3},{3,2},{4,5},{5,4},{6,7},{7,6},{8,9},{9,8},{10,11... | collective-permute-start | bytes 786440 | tf_op jit(solution)/shard_map/ppermute | solution.py:692
  1.5 15.2 %collective-permute-start = (bf16[256,1024]{1,0:T(8,128)(2,1)S(1)}, bf16[256,1024]{1,0:T(8,128)(2,1)S(1)}, u32[]{:S(2)}, u32[]{:S(2)}) collective-permute-start(bf16[256,1024]{1,0:T(8,128)(2,1)S(1)} %edge_rows.1), channel_id=1, source_target_pairs={{0,1},{1,4},{4,5},{5,8},{8,9},{9,12},{12,13},{2,3},{3,6},{6,7},{7,... | collective-permute-start | bytes 1572872 | tf_op jit(solution)/shard_map/ppermute | solution.py:688
  13.8 8.7 %collective-permute-start.3 = (bf16[896,128]{1,0:T(8,128)(2,1)S(1)}, bf16[896,128]{1,0:T(8,128)(2,1)S(1)}, u32[]{:S(2)}, u32[]{:S(2)}) collective-permute-start(bf16[896,128]{1,0:T(8,128)(2,1)S(1)} %get-tuple-element.40.own_most_ref), channel_id=1, source_target_pairs={{0,2},{2,0},{1,3},{3,1},{4,6},{6,4},{5,7},{7,5},{8,10},{10,8},{9,1... | collective-permute-start | bytes 688136 | tf_op jit(solution)/shard_map/ppermute | solution.py:692
  16.8 1.9 %copy-start.4 = (f32[1024,16]{0,1:T(8,128)S(1)}, f32[1024,16]{0,1:T(8,128)}, u32[]{:S(2)}) copy-start(f32[1024,16]{0,1:T(8,128)} %param.15) | copy-start | bytes 196612
  18.5 4.7 %collective-permute-start.2 = (bf16[128,128]{1,0:T(8,128)(2,1)S(1)}, bf16[128,128]{1,0:T(8,128)(2,1)S(1)}, u32[]{:S(2)}, u32[]{:S(2)}) collective-permute-start(bf16[128,128]{1,0:T(8,128)(2,1)S(1)} %get-tuple-element.39.own_first_ref), channel_id=1, source_target_pairs={{0,2},{2,0},{1,3},{3,1},{4,6},{6,4},{5,7},{7,5},{8,10},{10,8},{9,1... | collective-permute-start | bytes 98312 | tf_op jit(solution)/shard_map/ppermute | solution.py:692
  21.7 15.3 %copy-start.3 = (s32[1024,18]{0,1:T(8,128)S(1)}, s32[1024,18]{0,1:T(8,128)}, u32[]{:S(2)}) copy-start(s32[1024,18]{0,1:T(8,128)} %param.16) | copy-start | bytes 221188
  21.8 15.3 %copy-start.5 = (f32[18]{0:T(128)S(1)}, f32[18]{0:T(128)}, u32[]{:S(2)}) copy-start(f32[18]{0:T(128)} %param.17) | copy-start | bytes 220
  24.6 2.7 %collective-permute-start.4 = (bf16[144,1024]{1,0:T(8,128)(2,1)S(1)}, bf16[144,1024]{1,0:T(8,128)(2,1)S(1)}, u32[]{:S(2)}, u32[]{:S(2)}) collective-permute-start(bf16[144,1024]{1,0:T(8,128)(2,1)S(1)} %get-tuple-element.46.own_ref), channel_id=1, source_target_pairs={{0,1},{1,0},{2,3},{3,2},{4,5},{5,4},{6,7},{7,6},{8,9},{9,8},{10,11... | collective-permute-start | bytes 884744 | tf_op jit(solution)/shard_map/ppermute | solution.py:692
  25.2 9.2 %collective-permute-start.6 = (bf16[1024,128]{1,0:T(8,128)(2,1)S(1)}, bf16[1024,128]{1,0:T(8,128)(2,1)S(1)}, u32[]{:S(2)}, u32[]{:S(2)}) collective-permute-start(bf16[1024,128]{1,0:T(8,128)(2,1)S(1)} %get-tuple-element.47), channel_id=1, source_target_pairs={{0,2},{2,0},{1,3},{3,1},{4,6},{6,4},{5,7},{7,5},{8,10},{10,8},{9,1... | collective-permute-start | bytes 786440 | tf_op jit(solution)/shard_map/ppermute | solution.py:692
  27.9 5.9 %collective-permute-start.5 = (bf16[144,512]{1,0:T(8,128)(2,1)S(1)}, bf16[144,512]{1,0:T(8,128)(2,1)S(1)}, u32[]{:S(2)}, u32[]{:S(2)}) collective-permute-start(bf16[144,512]{1,0:T(8,128)(2,1)S(1)} %join_runs.2.own_ref), channel_id=1, source_target_pairs={{0,4},{4,0},{8,12},{12,8},{1,5},{5,1},{9,13},{13,9},{2,6},{6,2},{1... | collective-permute-start | bytes 442376 | tf_op jit(solution)/shard_map/ppermute | solution.py:692
  34.4 12.4 %collective-permute-start.7 = (bf16[144,512]{1,0:T(8,128)(2,1)S(1)}, bf16[144,512]{1,0:T(8,128)(2,1)S(1)}, u32[]{:S(2)}, u32[]{:S(2)}) collective-permute-start(bf16[144,512]{1,0:T(8,128)(2,1)S(1)} %join_runs.3), channel_id=1, source_target_pairs={{0,8},{4,12},{8,0},{12,4},{1,9},{5,13},{9,1},{13,5},{2,10},{6,14},... | collective-permute-start | bytes 442376 | tf_op jit(solution)/shard_map/ppermute | solution.py:692
  37.0 10.4 %collective-permute-start.8 = (bf16[144,512]{1,0:T(8,128)(2,1)S(1)}, bf16[144,512]{1,0:T(8,128)(2,1)S(1)}, u32[]{:S(2)}, u32[]{:S(2)}) collective-permute-start(bf16[144,512]{1,0:T(8,128)(2,1)S(1)} %collective-permute-done.5.other_ref.refs_0_), channel_id=1, source_target_pairs={{0,1},{1,0},{2,3},{3,2},{4,5},{5,4},{6,7},{7,6},{8,9},{9,8},{10,11... | collective-permute-start | bytes 442376 | tf_op jit(solution)/shard_map/ppermute | solution.py:692
  37.0 11.4 %copy-start = (f32[1024]{0:T(1024)S(1)}, f32[1024]{0:T(1024)}, u32[]{:S(2)}) copy-start(f32[1024]{0:T(1024)} %param.19) | copy-start | bytes 12292
  46.9 1.6 %collective-permute-start.9 = (bf16[144,512]{1,0:T(8,128)(2,1)S(1)}, bf16[144,512]{1,0:T(8,128)(2,1)S(1)}, u32[]{:S(2)}, u32[]{:S(2)}) collective-permute-start(bf16[144,512]{1,0:T(8,128)(2,1)S(1)} %collective-permute-done.7.refs_1_), channel_id=1, source_target_pairs={{0,1},{1,0},{2,3},{3,2},{4,5},{5,4},{6,7},{7,6},{8,9},{9,8},{10,11... | collective-permute-start | bytes 442376 | tf_op jit(solution)/shard_map/ppermute | solution.py:692

commit v3 on v2

v3 whole, which is shorter than its diff:
```python
import functools
import math

import jax
import jax.numpy as jnp
from jax import lax
from jax.experimental import pallas as pl
from jax.experimental.pallas import tpu as pltpu
from jax.sharding import PartitionSpec as P

HEAD_DIM = 128
HEAD_VALUES = 64
STATES = 128
WINDOW = 128
CHUNK = 128
EXTRA = 16
OUT_PIECES = 4
VMEM_LIMIT = 24 * 1024 * 1024
HIDDEN = -1e30

F32 = jnp.float32
BF16 = jnp.bfloat16
VMEM = pl.BlockSpec(memory_space=pltpu.VMEM)
SMEM = pl.BlockSpec(memory_space=pltpu.SMEM)
HBM = pl.BlockSpec(memory_space=pltpu.HBM)


def params():
    return pltpu.CompilerParams(vmem_limit_bytes=VMEM_LIMIT)


def cost(flops, moved, transcendentals=0):
    return pl.CostEstimate(flops=flops, bytes_accessed=moved, transcendentals=transcendentals)


def shaped(shape, dtype):
    return pltpu.VMEM(shape, dtype)


def far_shaped(shape, dtype):
    return pltpu.HBM(shape, dtype)


def near_by(*arrays):
    return [pltpu.with_memory_space_constraint(x, pltpu.VMEM) for x in arrays]


def far_off(*arrays):
    return [pltpu.with_memory_space_constraint(x, pltpu.HBM) for x in arrays]


def dot(left, right):
    return jnp.dot(left, right, preferred_element_type=F32)


def dot_turned(left, right):
    return lax.dot_general(left, right, (((1,), (1,)), ((), ())), preferred_element_type=F32)


def chunk_rows(index, count=1):
    return pl.ds(pl.multiple_of(index * CHUNK, CHUNK), count * CHUNK)


def spread_matrix(heads, width):
    lane = lax.broadcasted_iota(jnp.int32, (heads, width), 1)
    start = lax.broadcasted_iota(jnp.int32, (heads, width), 0) * HEAD_VALUES
    return ((lane >= start) & (lane < start + HEAD_VALUES)).astype(F32).astype(BF16)


def lane_tiles(width):
    tile = min(width, 256)
    return [slice(at, at + tile) for at in range(0, width, tile)]


def split_rows(rows):
    high = rows.astype(BF16)
    return high, (rows - high.astype(F32)).astype(BF16)


def edge_kernel(key_ref, value_ref, edge_ref, sems):
    row_count = key_ref.shape[0]
    part = WINDOW // 4
    copies = [
        pltpu.make_async_copy(
            ref.at[pl.ds(row_count - WINDOW + piece * part, part)],
            edge_ref.at[pl.ds(at * WINDOW + piece * part, part)],
            sems.at[at, piece],
        )
        for at, ref in enumerate((key_ref, value_ref))
        for piece in range(4)
    ]
    for copy in copies:
        copy.start()
    for copy in copies:
        copy.wait()


def edge_rows(key_rows, value_rows):
    width = key_rows.shape[1]
    return pl.pallas_call(
        edge_kernel,
        in_specs=[HBM, HBM],
        out_specs=VMEM,
        out_shape=shaped((2 * WINDOW, width), BF16),
        scratch_shapes=[pltpu.SemaphoreType.DMA((2, 4))],
        compiler_params=params(),
        cost_estimate=cost(0, 2**20),
        name="edge_rows",
    )(*far_off(key_rows, value_rows))


def chunk_masks(doc_pos):
    key_row = lax.broadcasted_iota(jnp.int32, (WINDOW, WINDOW), 0)
    query_lane = lax.broadcasted_iota(jnp.int32, (WINDOW, WINDOW), 1)
    away = query_lane - key_row
    away = jnp.where(away < 0, away + WINDOW, away)
    bias = jnp.where(away <= doc_pos, 0.0, HIDDEN).astype(F32).T
    return bias


def attend_chunk(bias, query, key_before, key, value_before, value, residual):
    query_row = lax.broadcasted_iota(jnp.int32, (WINDOW, WINDOW), 0)
    key_lane = lax.broadcasted_iota(jnp.int32, (WINDOW, WINDOW), 1)
    current = key_lane <= query_row
    current_share = current.astype(F32).astype(BF16)
    before_share = (1.0 - current.astype(F32)).astype(BF16)
    ones = jnp.ones((2 * WINDOW, HEAD_DIM), BF16)
    factor = math.log2(math.e) / math.sqrt(HEAD_DIM)
    scores = dot_turned(query, jnp.concatenate([key_before, key], axis=0))
    merged = jnp.where(current, scores[:, WINDOW:], scores[:, :WINDOW]) + bias
    top = jnp.max(merged, axis=1, keepdims=True)
    weights = jnp.exp2((merged - top) * factor).astype(BF16)
    weights = jnp.concatenate([weights * before_share, weights * current_share], axis=1)
    values = jnp.concatenate([value_before, value], axis=0)
    summed = dot(weights, jnp.concatenate([values, ones], axis=1))
    attended = summed[:, :HEAD_DIM] / summed[:, HEAD_DIM:]
    return (residual.astype(F32) + attended).astype(BF16)


def attend_heads(bias, width, query, key_before, key, value_before, value, residual, hidden):
    def lanes_of(at, ref, rows):
        return ref[rows, at : at + HEAD_DIM]

    for at in range(0, width, HEAD_DIM):
        hidden[0][hidden[1], at : at + HEAD_DIM] = attend_chunk(
            bias,
            lanes_of(at, *query),
            lanes_of(at, *key_before),
            lanes_of(at, *key),
            lanes_of(at, *value_before),
            lanes_of(at, *value),
            lanes_of(at, *residual),
        )


def late_kernel(
    split,
    place_ref,
    pos_ref,
    query_ref,
    key_ref,
    value_ref,
    residual_ref,
    own_weight_ref,
    other_weight_ref,
    hidden_ref,
    c_ref,
    weight_ref,
    b_ref,
    key_early_ref,
    query_early_ref,
    value_early_ref,
    residual_early_ref,
    query_buf,
    value_buf,
    residual_buf,
    sems,
):
    row_count, width = query_ref.shape
    chunks = row_count // CHUNK
    half_width = width // 2
    arrays = (
        (value_ref, value_buf, value_early_ref),
        (query_ref, query_buf, query_early_ref),
        (residual_ref, residual_buf, residual_early_ref),
    )

    def copy(which, chunk):
        source, buffer, _ = arrays[which]
        return pltpu.make_async_copy(
            source.at[chunk_rows(chunk)], buffer.at[chunk_rows(chunk - split)], sems.at[which, chunk - split]
        )

    def copy_early(which, chunk):
        source, _, early = arrays[which]
        rows = chunk_rows(chunk)
        return pltpu.make_async_copy(source.at[rows], early.at[rows], sems.at[which, chunk + chunks - split])

    copy_early(0, split - 1).start()
    for chunk in range(split, chunks):
        for which in range(3):
            copy(which, chunk).start()
    for which in range(1, 3):
        copy_early(which, split - 1).start()
    for chunk in range(split - 1):
        for which in range(3):
            copy_early(which, chunk).start()
    is_low = place_ref[0] == 0
    own_weight, other_weight = own_weight_ref[...], other_weight_ref[...]
    weight_ref[:half_width, :] = jnp.where(is_low, own_weight, other_weight)
    weight_ref[half_width:, :] = jnp.where(is_low, other_weight, own_weight)
    key_early_ref[...] = key_ref[: split * CHUNK, :]

    def attend_one(chunk, value_before):
        for which in range(3):
            copy(which, chunk).wait()
        rows = chunk_rows(chunk - split)
        attend_heads(
            chunk_masks(pos_ref[pl.ds(chunk, 1), :]),
            width,
            (query_buf, rows),
            (key_ref, chunk_rows(chunk - 1)),
            (key_ref, chunk_rows(chunk)),
            value_before,
            (value_buf, rows),
            (residual_buf, rows),
            (hidden_ref, chunk_rows(chunk)),
        )

    copy_early(0, split - 1).wait()
    attend_one(split, (value_early_ref, chunk_rows(split - 1)))

    def step(chunk, token):
        attend_one(chunk, (value_buf, chunk_rows(chunk - split - 1)))
        return token

    lax.fori_loop(split + 1, chunks, step, 0)
    shared = dot(hidden_ref[split * CHUNK :, :], weight_ref[...])
    b_ref[...] = shared[:, :STATES].astype(BF16)
    c_ref[split * CHUNK :, :] = shared[:, STATES:].astype(BF16)
    for which in range(1, 3):
        copy_early(which, split - 1).wait()
    for chunk in range(split - 1):
        for which in range(3):
            copy_early(which, chunk).wait()


def attend_late(split, place, positions, query, key, value, residual, weights):
    row_count, width = query.shape
    chunks = row_count // CHUNK
    late = row_count - split * CHUNK
    return pl.pallas_call(
        functools.partial(late_kernel, split),
        in_specs=[SMEM, VMEM, HBM, VMEM, HBM, HBM, VMEM, VMEM],
        out_specs=[VMEM] * 8,
        out_shape=[
            shaped((row_count, width), BF16),
            shaped((row_count, STATES), BF16),
            shaped((width, 2 * STATES), BF16),
            shaped((late, STATES), BF16),
        ]
        + [shaped((split * CHUNK, width), BF16)] * 4,
        scratch_shapes=[pltpu.VMEM((late, width), BF16)] * 3 + [pltpu.SemaphoreType.DMA((3, chunks))],
        compiler_params=params(),
        cost_estimate=cost(6 * 10**9, 10**7),
        name="attention_late",
    )(
        place,
        *near_by(positions),
        *far_off(query),
        *near_by(key),
        *far_off(value, residual),
        *near_by(*weights),
    )


def early_kernel(
    split,
    pos_ref,
    edge_ref,
    key_ref,
    query_ref,
    value_ref,
    residual_ref,
    weight_ref,
    hidden_in_ref,
    c_in_ref,
    hidden_ref,
    c_ref,
    b_ref,
):
    width = query_ref.shape[1]
    early = split * CHUNK

    def attend_one(chunk, key_before, value_before):
        rows = chunk_rows(chunk)
        attend_heads(
            chunk_masks(pos_ref[pl.ds(chunk, 1), :]),
            width,
            (query_ref, rows),
            key_before,
            (key_ref, rows),
            value_before,
            (value_ref, rows),
            (residual_ref, rows),
            (hidden_ref, rows),
        )

    def step(chunk, token):
        rows = chunk_rows(chunk - 1)
        attend_one(chunk, (key_ref, rows), (value_ref, rows))
        return token

    lax.fori_loop(1, split, step, 0)
    attend_one(0, (edge_ref, slice(0, WINDOW)), (edge_ref, slice(WINDOW, 2 * WINDOW)))
    shared = dot(hidden_ref[:early, :], weight_ref[...])
    b_ref[...] = shared[:, :STATES].astype(BF16)
    c_ref[:early, :] = shared[:, STATES:].astype(BF16)


def attend_early(split, positions, edges, parts, weight, hidden, c_mat):
    return pl.pallas_call(
        functools.partial(early_kernel, split),
        in_specs=[VMEM] * 9,
        out_specs=[VMEM] * 3,
        out_shape=[
            shaped(hidden.shape, BF16),
            shaped(c_mat.shape, BF16),
            shaped((split * CHUNK, STATES), BF16),
        ],
        input_output_aliases={7: 0, 8: 1},
        compiler_params=params(),
        cost_estimate=cost(2 * 10**9, 2 * 10**6),
        name="attention_early",
    )(*near_by(positions, edges, *parts, weight, hidden, c_mat))


def lower_ones():
    row = lax.broadcasted_iota(jnp.int32, (CHUNK, CHUNK), 0)
    lane = lax.broadcasted_iota(jnp.int32, (CHUNK, CHUNK), 1)
    lower = (lane <= row).astype(F32).astype(BF16)
    return jnp.concatenate([lower] * 3, axis=1)


def chunk_sums(lower, rate):
    first = rate.astype(BF16)
    second, third = split_rows(rate - first.astype(F32))
    return dot_turned(lower, jnp.concatenate([first, second, third], axis=1))


def scale_kernel(
    rate_ref,
    hidden_ref,
    c_ref,
    scaled_ref,
    rows_ref,
    fall_ref,
    carry_ref,
    hidden_far_ref,
    c_far_ref,
    rise,
    fall,
    carry,
    logs,
    sems,
):
    heads, row_count = rate_ref.shape
    width = hidden_ref.shape[1]
    chunks = row_count // CHUNK
    copies = [pltpu.make_async_copy(c_ref, c_far_ref, sems.at[chunks])]
    for chunk in range(chunks):
        rows = pl.ds(chunk * CHUNK, CHUNK)
        copies.append(pltpu.make_async_copy(hidden_ref.at[rows], hidden_far_ref.at[rows], sems.at[chunk]))
    for copy in copies:
        copy.start()
    spread = spread_matrix(heads, width)
    lower = lower_ones()
    row_idx = lax.broadcasted_iota(jnp.int32, (8, heads), 0)
    prefix = jnp.zeros((1, heads), F32)
    for chunk in range(chunks):
        rows = slice(chunk * CHUNK, (chunk + 1) * CHUNK)
        total = chunk_sums(lower, rate_ref[:, rows])
        middle = total[CHUNK // 2 - 1 : CHUNK // 2]
        last = total[CHUNK - 1 :]
        rise[rows, :] = jnp.exp(total - middle).astype(BF16)
        fall[rows, :] = jnp.exp(middle - total).astype(BF16)
        carry[rows, :] = jnp.exp(-(total + prefix)).astype(BF16)
        logs[chunk * 8 : (chunk + 1) * 8, :] = jnp.where(
            row_idx == 0,
            middle - last,
            jnp.where(row_idx == 1, -last, jnp.where(row_idx == 2, -middle, 0.0)),
        )
        prefix = prefix + last
    high, low = split_rows(jnp.exp(logs[...]))
    for lanes in lane_tiles(width):
        wide = dot(rise[...], spread[:, lanes])
        scaled_ref[:, lanes] = (wide * hidden_ref[:, lanes].astype(F32)).astype(BF16)
        rows_ref[:, lanes] = dot(high, spread[:, lanes]) + dot(low, spread[:, lanes])
        fall_ref[:, lanes] = dot(fall[...], spread[:, lanes]).astype(BF16)
        carry_ref[:, lanes] = dot(carry[...], spread[:, lanes]).astype(BF16)
    for copy in copies:
        copy.wait()


def scale_hidden(rate_turned, hidden, c_mat):
    row_count, width = hidden.shape
    heads = rate_turned.shape[0]
    chunks = row_count // CHUNK
    return pl.pallas_call(
        scale_kernel,
        in_specs=[VMEM] * 3,
        out_specs=[VMEM] * 4 + [HBM] * 2,
        out_shape=[
            shaped((row_count, width), BF16),
            shaped((chunks * 8, width), F32),
            shaped((row_count, width), BF16),
            shaped((row_count, width), BF16),
            far_shaped(hidden.shape, BF16),
            far_shaped(c_mat.shape, BF16),
        ],
        scratch_shapes=[pltpu.VMEM((row_count, heads), BF16)] * 3
        + [pltpu.VMEM((chunks * 8, heads), F32), pltpu.SemaphoreType.DMA((chunks + 1,))],
        compiler_params=params(),
        cost_estimate=cost(10**9, 4 * 10**6),
        name="scale_hidden",
    )(*near_by(rate_turned, hidden, c_mat))


def state_kernel(
    local_levels,
    early_own_ref,
    early_other_ref,
    late_own_ref,
    late_other_ref,
    scaled_ref,
    rows_ref,
    state_ref,
    runs_ref,
    turned_far_ref,
    turned,
    sems,
):
    row_count, width = scaled_ref.shape
    chunks = row_count // CHUNK
    early = early_own_ref.shape[0]
    for chunk in range(chunks):
        at = chunk * CHUNK
        if at < early:
            span = slice(at, at + CHUNK)
            own, other = early_own_ref[span, :], early_other_ref[span, :]
        else:
            span = slice(at - early, at - early + CHUNK)
            own, other = late_own_ref[span, :], late_other_ref[span, :]
        turned[:, at : at + CHUNK] = (own.astype(F32) + other.astype(F32)).T.astype(BF16)
    turned_copy = pltpu.make_async_copy(turned, turned_far_ref, sems.at[0])
    turned_copy.start()
    tile = min(width, 256)

    def step(at, carry):
        lanes = pl.ds(pl.multiple_of(at * tile, tile), tile)
        held = {}
        fade = None
        for chunk in range(chunks):
            factor = rows_ref[chunk * 8 : (chunk + 1) * 8, lanes]
            fades = factor[1:2]
            for level in range(local_levels):
                start = (chunk * local_levels + level) * STATES
                if level in held:
                    run = (held[level] * factor[2:3]).astype(BF16)
                else:
                    run = jnp.zeros((STATES, tile), BF16)
                runs_ref[start : start + STATES, lanes] = run
            span = slice(chunk * CHUNK, (chunk + 1) * CHUNK)
            joined = dot(turned[:, span], scaled_ref[span, lanes]) * factor[0:1]
            held = {level: state * fades for level, state in held.items()}
            level = 0
            while level in held:
                joined = joined + held.pop(level)
                level += 1
            held[level] = joined
            fade = fades if fade is None else fade * fades
        state_ref[:STATES, lanes] = held[local_levels].astype(BF16)
        state_ref[STATES:, lanes] = fade_rows(fade)
        return carry

    lax.fori_loop(0, width // tile, step, 0)
    turned_copy.wait()


def fade_rows(fade):
    high, low = split_rows(fade)
    row = lax.broadcasted_iota(jnp.int32, (EXTRA, fade.shape[1]), 0)
    return jnp.where(row == 0, high.astype(F32), jnp.where(row == 1, low.astype(F32), 0.0)).astype(BF16)


def fade_of(message):
    return message[STATES : STATES + 1].astype(F32) + message[STATES + 1 : STATES + 2].astype(F32)


def block_state(early_own, early_other, late_own, late_other, scaled, factor_rows):
    row_count, width = scaled.shape
    chunks = row_count // CHUNK
    local_levels = chunks.bit_length() - 1
    return pl.pallas_call(
        functools.partial(state_kernel, local_levels),
        in_specs=[VMEM] * 6,
        out_specs=[VMEM, VMEM, HBM],
        out_shape=[
            shaped((STATES + EXTRA, width), BF16),
            shaped((chunks * local_levels * STATES, width), BF16),
            far_shaped((STATES, row_count), BF16),
        ],
        scratch_shapes=[pltpu.VMEM((STATES, row_count), BF16), pltpu.SemaphoreType.DMA((1,))],
        compiler_params=params(),
        cost_estimate=cost(3 * 10**8, 4 * 10**6),
        name="block_state",
    )(*near_by(early_own, early_other, late_own, late_other, scaled, factor_rows))


def join_kernel(level, place_ref, own_ref, other_ref, joined_ref):
    half_width = joined_ref.shape[1]
    own, other = own_ref[...], other_ref[...]
    if own.shape[1] != half_width:
        is_low = place_ref[0] == 0
        own = jnp.where(is_low, own[:, :half_width], own[:, half_width:])
        other = jnp.where(is_low, other[:, :half_width], other[:, half_width:])
    upper = place_ref[1 + level] == 1
    own_fade, other_fade = fade_of(own), fade_of(other)
    lower, higher = jnp.where(upper, other, own), jnp.where(upper, own, other)
    fade = jnp.where(upper, own_fade, other_fade)
    joined_ref[:STATES, :] = (lower[:STATES].astype(F32) * fade + higher[:STATES].astype(F32)).astype(BF16)
    joined_ref[STATES:, :] = fade_rows(own_fade * other_fade)


def join(level, place, own, other, half_width):
    return pl.pallas_call(
        functools.partial(join_kernel, level),
        in_specs=[SMEM, VMEM, VMEM],
        out_specs=VMEM,
        out_shape=shaped((own.shape[0], half_width), BF16),
        compiler_params=params(),
        cost_estimate=cost(10**6, 10**5),
        name="join_runs",
    )(place, *near_by(own, other))


def codes_kernel(codes_ref, wide_ref):
    codes = codes_ref[...].astype(F32).T.astype(BF16)
    levels = codes.shape[1]
    pair = 2 * CHUNK
    level_of = lax.broadcasted_iota(jnp.int32, (levels, pair), 0)
    lane = lax.broadcasted_iota(jnp.int32, (levels, pair), 1)
    for at in range(0, wide_ref.shape[1], pair):
        start = (level_of * CHUNK) - at
        pick = ((lane >= start) & (lane < start + CHUNK)).astype(F32).astype(BF16)
        wide_ref[:, at : at + pair] = dot(codes, pick).astype(BF16)


def widen_codes(codes_turned):
    levels, row_count = codes_turned.shape
    levels += levels % 2
    return pl.pallas_call(
        codes_kernel,
        in_specs=[VMEM],
        out_specs=VMEM,
        out_shape=shaped((row_count, levels * CHUNK), BF16),
        compiler_params=params(),
        cost_estimate=cost(10**9, 10**6),
        name="widen_codes",
    )(*near_by(codes_turned))


def weights_kernel(
    local_levels,
    cross_levels,
    scale_ref,
    turned_far_ref,
    c_far_ref,
    c_other_ref,
    codes_ref,
    left_ref,
    early_reads_ref,
    last_reads_ref,
    turned,
    c_buf,
    sems,
):
    row_count = c_other_ref.shape[0]
    copies = [
        pltpu.make_async_copy(turned_far_ref, turned, sems.at[0]),
        pltpu.make_async_copy(c_far_ref, c_buf, sems.at[1]),
    ]
    for copy in copies:
        copy.start()
    for copy in copies:
        copy.wait()

    query_row = lax.broadcasted_iota(jnp.int32, (CHUNK, CHUNK), 0)
    key_lane = lax.broadcasted_iota(jnp.int32, (CHUNK, CHUNK), 1)
    differ = jnp.bitwise_xor(query_row, key_lane)
    inner_levels = CHUNK.bit_length() - 1

    def step(chunk, token):
        rows = chunk_rows(chunk)

        def lam_of(level):
            return codes_ref[rows, level * CHUNK : (level + 1) * CHUNK].astype(F32) * scale_ref[level]

        c_wide = (c_buf[rows, :].astype(F32) + c_other_ref[rows, :].astype(F32)).astype(BF16).astype(F32)
        gram = dot(c_wide.astype(BF16), turned[:, rows])
        weight = lam_of(0)
        for level in range(1, inner_levels + 1):
            weight = jnp.where(differ >= 1 << (level - 1), lam_of(level), weight)
        left_ref[rows, :CHUNK] = jnp.where(key_lane <= query_row, gram * weight, 0.0).astype(BF16)
        for level in range(local_levels + cross_levels):
            read = (c_wide * lam_of(inner_levels + 1 + level)).astype(BF16)
            if level < local_levels:
                left_ref[rows, (level + 1) * CHUNK : (level + 2) * CHUNK] = read
            elif level < local_levels + cross_levels - 1:
                at = (level - local_levels) * STATES
                early_reads_ref[rows, at : at + STATES] = read
            else:
                last_reads_ref[rows, :] = read
        return token

    lax.fori_loop(0, row_count // CHUNK, step, 0)


def level_products(scale, turned_far, c_far, c_other, codes_wide, cross_levels):
    row_count = c_other.shape[0]
    local_levels = (row_count // CHUNK).bit_length() - 1
    return pl.pallas_call(
        functools.partial(weights_kernel, local_levels, cross_levels),
        in_specs=[SMEM] + [HBM] * 2 + [VMEM] * 2,
        out_specs=[VMEM] * 3,
        out_shape=[
            shaped((row_count, (1 + local_levels) * STATES), BF16),
            shaped((row_count, (cross_levels - 1) * STATES), BF16),
            shaped((row_count, STATES), BF16),
        ],
        scratch_shapes=[
            pltpu.VMEM((STATES, row_count), BF16),
            pltpu.VMEM((row_count, STATES), BF16),
            pltpu.SemaphoreType.DMA((2,)),
        ],
        compiler_params=params(),
        cost_estimate=cost(10**9, 10**7),
        name="level_products",
    )(scale, *far_off(turned_far, c_far), *near_by(c_other, codes_wide))


def carried_state(message, before, upper):
    return (message[:STATES].astype(F32) * (before * upper.astype(F32))).astype(BF16)


def local_kernel(
    local_levels,
    cross_levels,
    place_ref,
    hidden_far_ref,
    left_ref,
    early_reads_ref,
    scaled_ref,
    fall_ref,
    carry_ref,
    runs_ref,
    near_ref,
    *refs,
):
    received = refs[: cross_levels - 2]
    swapped = refs[cross_levels - 2 : 2 * (cross_levels - 2)]
    local_ref, hidden_ref, before_ref, carried, crossed, sems = refs[2 * (cross_levels - 2) :]
    row_count, width = scaled_ref.shape
    chunks = row_count // CHUNK
    copies = [
        pltpu.make_async_copy(
            hidden_far_ref.at[chunk_rows(chunk)], hidden_ref.at[chunk_rows(chunk)], sems.at[chunk]
        )
        for chunk in range(chunks)
    ]
    for copy in copies:
        copy.start()

    is_low = place_ref[0] == 0
    before = jnp.ones((1, width), F32)
    for level in range(cross_levels - 1):
        upper = place_ref[1 + level]
        if level == 0:
            message = near_ref[...]
        else:
            own, other = received[level - 1][...], swapped[level - 1][...]
            message = jnp.concatenate(
                [jnp.where(is_low, own, other), jnp.where(is_low, other, own)], axis=1
            )
        carried[level * STATES : (level + 1) * STATES, :] = carried_state(message, before, upper)
        before = jnp.where(upper == 1, before * fade_of(message), before)
    before_ref[...] = jnp.broadcast_to(before, before_ref.shape)
    tiles = lane_tiles(width)
    for lanes in tiles:
        crossed[:, lanes] = dot(early_reads_ref[...], carried[:, lanes]) * carry_ref[:, lanes].astype(F32)

    def step(chunk, token):
        rows = chunk_rows(chunk)
        left = left_ref[rows, :]
        run_rows = local_levels * STATES
        runs = pl.ds(pl.multiple_of(chunk * run_rows, run_rows), run_rows)
        for lanes in tiles:
            summed = dot(left, jnp.concatenate([scaled_ref[rows, lanes], runs_ref[runs, lanes]], axis=0))
            local_ref[rows, lanes] = (
                summed * fall_ref[rows, lanes].astype(F32) + crossed[rows, lanes]
            ).astype(BF16)
        return token

    lax.fori_loop(0, chunks, step, 0)
    for copy in copies:
        copy.wait()


def local_terms(place, hidden_far, left, early_reads, scaled, fall, carry, runs, near, received, swapped):
    row_count, width = scaled.shape
    local_levels = (row_count // CHUNK).bit_length() - 1
    cross_levels = 2 + len(received)
    return pl.pallas_call(
        functools.partial(local_kernel, local_levels, cross_levels),
        in_specs=[SMEM, HBM] + [VMEM] * (7 + 2 * len(received)),
        out_specs=[VMEM] * 3,
        out_shape=[shaped((row_count, width), BF16)] * 2 + [shaped((8, width), F32)],
        scratch_shapes=[
            pltpu.VMEM(((cross_levels - 1) * STATES, width), BF16),
            pltpu.VMEM((row_count, width), F32),
            pltpu.SemaphoreType.DMA((row_count // CHUNK,)),
        ],
        compiler_params=params(),
        cost_estimate=cost(3 * 10**9, 10**7),
        name="local_terms",
    )(
        place,
        *far_off(hidden_far),
        *near_by(left, early_reads, scaled, fall, carry, runs, near, *received, *swapped),
    )


def finish_kernel(
    swap, place_ref, message_ref, before_ref, hidden_ref, reads_ref, local_ref, carry_ref, gain_ref, *refs
):
    row_count, width = local_ref.shape
    half_width = width // 2
    own_start = place_ref[0] * half_width
    start = half_width - own_start if swap else own_start
    upper = place_ref[place_ref.shape[0] - 1]
    tile = min(half_width, 256)
    row = lax.broadcasted_iota(jnp.int32, (tile, tile), 0) // HEAD_VALUES
    lane = lax.broadcasted_iota(jnp.int32, (tile, tile), 1) // HEAD_VALUES
    mean_mat = jnp.where(row == lane, 1.0 / HEAD_VALUES, 0.0).astype(BF16)
    copies = []
    if swap:
        held_ref, out_ref, result, sems = refs
    else:
        (result,) = refs

    def copy_out(source, here, lanes, at):
        for piece in range(OUT_PIECES):
            rows = pl.ds(piece * (row_count // OUT_PIECES), row_count // OUT_PIECES)
            copies.append(
                pltpu.make_async_copy(source.at[rows, here], out_ref.at[rows, lanes], sems.at[at, piece])
            )
            copies[-1].start()

    if swap:
        lanes = pl.ds(pl.multiple_of(own_start, half_width), half_width)
        copy_out(held_ref, pl.ds(0, half_width), lanes, 0)
    for at in range(half_width // tile):
        lanes = pl.ds(pl.multiple_of(start + at * tile, tile), tile)
        here = slice(at * tile, (at + 1) * tile)
        carried = carried_state(message_ref[:, here], before_ref[0:1, lanes], upper)
        cross = dot(reads_ref[...], carried)
        mixed = local_ref[:, lanes].astype(F32) + cross * carry_ref[:, lanes].astype(F32)
        mean = dot((mixed * mixed).astype(BF16), mean_mat)
        normed = mixed * lax.rsqrt(mean + 1e-05) * gain_ref[:, lanes]
        result[:, here] = (hidden_ref[:, lanes].astype(F32) + normed).astype(BF16)
        if swap:
            copy_out(result, here, lanes, 1 + at)
    for copy in copies:
        copy.wait()


def finish(place, message, before, hidden, reads, local, carry, gain, held):
    row_count, width = local.shape
    half_width = width // 2
    swap = held is not None
    half_shape = (row_count, half_width)
    return pl.pallas_call(
        functools.partial(finish_kernel, swap),
        in_specs=[SMEM] + [VMEM] * (8 if swap else 7),
        out_specs=HBM if swap else VMEM,
        out_shape=far_shaped((row_count, width), BF16) if swap else shaped(half_shape, BF16),
        scratch_shapes=[
            pltpu.VMEM(half_shape, BF16),
            pltpu.SemaphoreType.DMA((1 + max(1, half_width // 256), OUT_PIECES)),
        ]
        if swap
        else [],
        compiler_params=params(),
        cost_estimate=cost(2 * 10**9, 8 * 10**6),
        name="carried_and_norm",
    )(place, *near_by(message, before, hidden, reads, local, carry, gain, *([held] if swap else [])))


def from_behind(x, axis, by):
    length = lax.axis_size(axis)
    return lax.ppermute(x, axis, [(i, i + by) for i in range(length - by)])


def partner(x, axis, distance):
    return lax.ppermute(x, axis, [(i, i ^ 1 << distance) for i in range(lax.axis_size(axis))])


def summed_over_heads(share):
    rounds = lax.axis_size("head").bit_length() - 1
    if rounds == 0:
        return share, jnp.zeros_like(share)
    total = share
    for distance in range(rounds - 1):
        total = (total.astype(F32) + partner(total, "head", distance).astype(F32)).astype(BF16)
    return total, partner(total, "head", rounds - 1)


def body(
    residual_in,
    query_rows,
    key_rows,
    value_rows,
    bc_weight,
    decay_rate,
    level_codes,
    level_scale,
    positions,
    ssm_gain,
):
    row_count, width = residual_in.shape
    half_width = width // 2
    shard_axes = ("seq", "fsdp")
    cross_levels = lax.axis_size(shard_axes).bit_length() - 1
    shard = lax.axis_index(shard_axes)
    half_index = lax.axis_index("fsdp")
    place = jnp.stack(
        [half_index] + [jnp.bitwise_and(jnp.right_shift(shard, level), 1) for level in range(cross_levels)]
    ).astype(jnp.int32)

    weights = (bc_weight, partner(bc_weight, "fsdp", 0))
    edges = from_behind(edge_rows(key_rows, value_rows), shard_axes, 1)
    pos_rows = positions.reshape(row_count // CHUNK, CHUNK)
    split = max(1, row_count // CHUNK // 4)
    hidden, c_mat, weight, b_late, *parts = attend_late(
        split, place, pos_rows, query_rows, key_rows, value_rows, residual_in, weights
    )
    late_own, late_other = summed_over_heads(b_late)
    hidden, c_mat, b_early = attend_early(split, pos_rows, edges, parts, weight, hidden, c_mat)
    early_own, early_other = summed_over_heads(b_early)
    scaled, factor_rows, fall, carry, hidden_far, c_far = scale_hidden(decay_rate.T, hidden, c_mat)
    c_mat, scaled = lax.optimization_barrier((c_mat, scaled))
    c_sent, c_other = summed_over_heads(c_mat)
    if lax.axis_size("head") > 2:
        c_far = c_sent
    state, runs, turned_far = block_state(
        early_own, early_other, late_own, late_other, scaled, factor_rows
    )
    near = partner(state, "fsdp", 0)
    joined = join(0, place, state, near, half_width)
    received, swapped = [], []
    for level in range(1, cross_levels):
        other = partner(joined, "seq", level - 1)
        if level == 1:
            codes_wide = widen_codes(level_codes.T)
            other, codes_wide = lax.optimization_barrier((other, codes_wide))
        received.append(other)
        if level < cross_levels - 1:
            joined = join(level, place, joined, other, half_width)
            swapped.append(partner(other, "fsdp", 0))
    left, early_reads, last_reads = level_products(
        level_scale, turned_far, c_far, c_other, codes_wide, cross_levels
    )
    local, hidden, before = local_terms(
        place, hidden_far, left, early_reads, scaled, fall, carry, runs, near, received[:-1], swapped
    )
    last, local = lax.optimization_barrier((received[-1], local))
    last_swapped = partner(last, "fsdp", 0)
    gain = ssm_gain[None, :]
    half = finish(place, last, before, hidden, last_reads, local, carry, gain, None)
    return finish(place, last_swapped, before, hidden, last_reads, local, carry, gain, half)


def solution(mesh):
    in_specs = (
        P(("groups", "seq", "fsdp"), "head"),
        P(("groups", "seq", "fsdp"), "head"),
        P(("groups", "seq", "fsdp"), "head"),
        P(("groups", "seq", "fsdp"), "head"),
        P(("head", "fsdp"), None),
        P(("groups", "seq", "fsdp"), "head"),
        P(("groups", "seq", "fsdp"), None),
        P(),
        P(("groups", "seq", "fsdp")),
        P("head"),
    )
    out_specs = P(("groups", "seq", "fsdp"), "head")
    return jax.shard_map(body, mesh=mesh, in_specs=in_specs, out_specs=out_specs, check_vma=False)
```

time: 56 us -> 46.6 us (0.83)
  Pallas kernels: 35.8 us -> 28 us
  waiting for transfers between devices: 6.77 us -> 5.81 us
  starting transfers between devices: 13 us -> 12.3 us
    pallas_call x1, Pallas kernels: 9.79 us -> 3.96 us  [local_terms(): pl.pallas_call(functools.partial(local_kernel, local_levels, cross_levels...]
    pallas_call x5 -> x8, Pallas kernels: 23.8 us -> 21.5 us  [the longest x1 6.79 us: attend_late(): pl.pallas_call(functools.partial(late_kernel, split), in_specs=[SMEM, VME...]
    ppermute x9, waiting for transfers between devices: 6.77 us -> 5.81 us  [partner(): lax.ppermute(x, axis, [(i, i ^ 1 << distance) for i in range(lax.axis_siz...]
    ppermute x9, starting transfers between devices: 11 us -> 10.4 us  [partner(): lax.ppermute(x, axis, [(i, i ^ 1 << distance) for i in range(lax.axis_siz...]
  transfers between devices with their start and end apart: 10 -> 10, of which waited for: 4 -> 4; matrix products, arithmetic and copies ran while one was open for 0% -> 0% of each run, Pallas kernels for 48% -> 51%
where the time goes in v3:
time: 46.6 us; the launch traced here: 46.3 us
  Pallas kernels  28 us (60%)
  starting transfers between devices  12.3 us (26%)
  waiting for transfers between devices  5.81 us (12%)
    ppermute x9, starting transfers between devices, partner(): lax.ppermute(x, axis, [(i, i ^ 1 << distance) for i in range(lax.axis_siz...  10.4 us
    pallas_call x1, Pallas kernels, attend_late(): pl.pallas_call(functools.partial(late_kernel, split), in_specs=[SMEM, VME...  6.79 us
    ppermute x9, waiting for transfers between devices, partner(): lax.ppermute(x, axis, [(i, i ^ 1 << distance) for i in range(lax.axis_siz...  5.81 us
    pallas_call x2, Pallas kernels, finish(): pl.pallas_call(functools.partial(finish_kernel, swap), in_specs=[SMEM] +...  4.1 us
    pallas_call x1, Pallas kernels, local_terms(): pl.pallas_call(functools.partial(local_kernel, local_levels, cross_levels...  3.96 us
    pallas_call x1, Pallas kernels, level_products(): pl.pallas_call(functools.partial(weights_kernel, local_levels, cross_leve...  3.07 us
    pallas_call x1, Pallas kernels, scale_hidden(): pl.pallas_call(scale_kernel, in_specs=[VMEM] * 3, out_specs=[VMEM] * 4 +...  2.95 us
    ppermute x1, starting transfers between devices, from_behind(): return lax.ppermute(x, axis, [(i, i + by) for i in range(length - by)])  1.9 us
  transfers between devices with their start and end apart: 10, of which 4 were waited for; matrix products, arithmetic and copies ran while one was open for 0% of the time, Pallas kernels for 51%

profile of v3, /device:TPU:0, one launch (start us, length us, event | category | flops | bytes accessed | tf_op | source)
XLA Modules:
  0.0 46.3 jit_solution(3594081209969031245)
XLA Ops:
  0.0 0.0 copy-start.4
  0.0 0.0 copy-start
  0.0 0.0 copy-start.6
  0.0 0.5 %collective-permute-start.1 = (bf16[512,256]{1,0:T(8,128)(2,1)}, bf16[512,256]{1,0:T(8,128)(2,1)}, u32[]{:S(2)}, u32[]{:S(2)}) collective-permute-start(bf16[512,256]{1,0:T(8,128)(2,1)} %own_weight_ref.1), channel_id=1, source_target_pairs={{0,1},{1,0},{2,3},{3,2},{4,5},{5,4},{6,7},{7,6},{8,9},{9,8},{10,11... | collective-permute-start | bytes 786440 | tf_op jit(solution)/shard_map/ppermute | solution.py:815
  0.5 1.3 %edge_rows.1 = bf16[256,1024]{1,0:T(8,128)(2,1)S(1)} custom-call(bf16[1024,1024]{1,0:T(8,128)(2,1)} %key_ref.3, bf16[1024,1024]{1,0:T(8,128)(2,1)} %value_ref.3), custom_call_target="tpu_custom_call" | custom-call | bytes 1048576 | tf_op jit(solution)/shard_map/edge_rows/pallas_call | solution.py:100
  1.9 1.9 %collective-permute-start = (bf16[256,1024]{1,0:T(8,128)(2,1)S(1)}, bf16[256,1024]{1,0:T(8,128)(2,1)S(1)}, u32[]{:S(2)}, u32[]{:S(2)}) collective-permute-start(bf16[256,1024]{1,0:T(8,128)(2,1)S(1)} %edge_rows.1), channel_id=1, source_target_pairs={{0,1},{1,4},{4,5},{5,8},{8,9},{9,12},{12,13},{2,3},{3,6},{6,7},{7,... | collective-permute-start | bytes 1572872 | tf_op jit(solution)/shard_map/ppermute | solution.py:811
  3.8 0.1 pad_add_fusion.place_ref
  3.9 0.0 collective-permute-done.1.other_weight_ref
  3.9 0.0 copy-done.4
  3.9 0.0 copy-done
  3.9 0.0 copy-done.6
  3.9 6.8 %attention_late.1 = (bf16[1024,1024]{1,0:T(8,128)(2,1)S(1)}, bf16[1024,128]{1,0:T(8,128)(2,1)S(1)}, bf16[1024,256]{1,0:T(8,128)(2,1)S(1)}, bf16[768,128]{1,0:T(8...) custom-call(s32[4]{0:T(128)S(1)} %pad_add_fusion.place_ref, ...), custom_call_target="tpu_custom_call" | custom-call | flops 6000000000 | bytes 10000000 | tf_op jit(solution)/shard_map/attention_late/pallas_call | solution.py:252
  10.7 2.9 %collective-permute-start.3 = (bf16[768,128]{1,0:T(8,128)(2,1)S(1)}, bf16[768,128]{1,0:T(8,128)(2,1)S(1)}, u32[]{:S(2)}, u32[]{:S(2)}) collective-permute-start(bf16[768,128]{1,0:T(8,128)(2,1)S(1)} %get-tuple-element.45.late_own_ref), channel_id=1, source_target_pairs={{0,2},{2,0},{1,3},{3,1},{4,6},{6,4},{5,7},{7,5},{8,10},{10,8},{9,1... | collective-permute-start | bytes 589832 | tf_op jit(solution)/shard_map/ppermute | solution.py:815
  13.6 0.0 collective-permute-done.edge_ref
  13.6 0.0 copy-start.5
  13.6 1.2 %attention_early.1 = (bf16[1024,1024]{1,0:T(8,128)(2,1)S(1)}, bf16[1024,128]{1,0:T(8,128)(2,1)S(1)}, bf16[256,128]{1,0:T(8,128)(2,1)S(1)}) custom-call(s32[8,128]{1,0:T(8,128)S(1)} %bitcast.13, bf16[256,1024]{1,0:T(8,128)(2,1)S(1)} %collective-permute-done.edge_ref, ...), custom_call_target="tpu_custom_call", output_to_operand_aliasing={{0}: (7, {}), {1}: (8, {})} | custom-call | flops 2000000000 | bytes 2000000 | tf_op jit(solution)/shard_map/attention_early/pallas_call | solution.py:322
  14.8 0.1 collective-permute-start.2
  14.9 0.0 copy-done.5
  14.9 3.0 %scale_hidden.1 = (bf16[1024,1024]{1,0:T(8,128)(2,1)S(1)}, f32[64,1024]{1,0:T(8,128)S(1)}, bf16[1024,1024]{1,0:T(8,128)(2,1)S(1)}, bf16[1024,1024]{1,0:T(8,128)(...) custom-call(f32[16,1024]{1,0:T(8,128)S(1)} %bitcast.11, ...), custom_call_target="tpu_custom_call" | custom-call | flops 1000000000 | bytes 4000000 | tf_op jit(solution)/shard_map/scale_hidden/pallas_call | solution.py:409
  17.9 0.0 copy-start.1
  17.9 0.7 %collective-permute-done.3.late_other_ref = bf16[768,128]{1,0:T(8,128)(2,1)S(1)} collective-permute-done((bf16[768,128]{1,0:T(8,128)(2,1)S(1)}, bf16[768,128]{1,0:T(8,128)(2,1)S(1)}, u32[]{:S(2)}, u32[]{:S(2)}) %collective-permute-start.3) | collective-permute-done | bytes 196640 | tf_op jit(solution)/shard_map/ppermute | solution.py:815
  18.6 1.4 %collective-permute-done.2.early_other_ref = bf16[256,128]{1,0:T(8,128)(2,1)S(1)} collective-permute-done((bf16[256,128]{1,0:T(8,128)(2,1)S(1)}, bf16[256,128]{1,0:T(8,128)(2,1)S(1)}, u32[]{:S(2)}, u32[]{:S(2)}) %collective-permute-start.2) | collective-permute-done | bytes 65568 | tf_op jit(solution)/shard_map/ppermute | solution.py:815
  20.0 1.9 %block_state.1 = (bf16[144,1024]{1,0:T(8,128)(2,1)S(1)}, bf16[3072,1024]{1,0:T(8,128)(2,1)S(1)}, bf16[128,1024]{1,0:T(8,128)(2,1)}) custom-call(bf16[256,128]{1,0:T(8,128)(2,1)S(1)} %get-tuple-element.44.early_own_ref, bf16[256,128]{1,0:T(8,128)(2,1)S(1)} %collective-permute-done.2.early_other_ref, bf16[768,128]{1,0:T(8,128)(2,1)S(1)} %get-tuple-element.45.late_own_ref, ...), custom_call_target="tpu_custom_call" | custom-call | flops 300000000 | bytes 4000000 | tf_op jit(solution)/shard_map/block_state/pallas_call | solution.py:504
  21.9 0.6 %collective-permute-start.4 = (bf16[144,1024]{1,0:T(8,128)(2,1)S(1)}, bf16[144,1024]{1,0:T(8,128)(2,1)S(1)}, u32[]{:S(2)}, u32[]{:S(2)}) collective-permute-start(bf16[144,1024]{1,0:T(8,128)(2,1)S(1)} %get-tuple-element.51.own_ref), channel_id=1, source_target_pairs={{0,1},{1,0},{2,3},{3,2},{4,5},{5,4},{6,7},{7,6},{8,9},{9,8},{10,11... | collective-permute-start | bytes 884744 | tf_op jit(solution)/shard_map/ppermute | solution.py:815
  22.5 2.1 %collective-permute-start.7 = (bf16[1024,128]{1,0:T(8,128)(2,1)S(1)}, bf16[1024,128]{1,0:T(8,128)(2,1)S(1)}, u32[]{:S(2)}, u32[]{:S(2)}) collective-permute-start(bf16[1024,128]{1,0:T(8,128)(2,1)S(1)} %get-tuple-element.56.c_ref), channel_id=1, source_target_pairs={{0,2},{2,0},{1,3},{3,1},{4,6},{6,4},{5,7},{7,5},{8,10},{10,8},{9,1... | collective-permute-start | bytes 786440 | tf_op jit(solution)/shard_map/ppermute | solution.py:815
  24.6 0.0 collective-permute-done.4.other_ref.near_ref
  24.6 0.6 %join_runs.2.own_ref = bf16[144,512]{1,0:T(8,128)(2,1)S(1)} custom-call(s32[4]{0:T(128)S(1)} %pad_add_fusion.place_ref, bf16[144,1024]{1,0:T(8,128)(2,1)S(1)} %get-tuple-element.51.own_ref, bf16[144,1024]{1,0:T(8,128)(2,1)S(1)} %collective-permute-done.4.other_ref.near_ref), custom_call_target="tpu_custom_call" | custom-call | flops 1000000 | bytes 100000 | tf_op jit(solution)/shard_map/join_runs/pallas_call | solution.py:536
  25.2 1.6 %collective-permute-start.5 = (bf16[144,512]{1,0:T(8,128)(2,1)S(1)}, bf16[144,512]{1,0:T(8,128)(2,1)S(1)}, u32[]{:S(2)}, u32[]{:S(2)}) collective-permute-start(bf16[144,512]{1,0:T(8,128)(2,1)S(1)} %join_runs.2.own_ref), channel_id=1, source_target_pairs={{0,4},{4,0},{8,12},{12,8},{1,5},{5,1},{9,13},{13,9},{2,6},{6,2},{1... | collective-permute-start | bytes 442376 | tf_op jit(solution)/shard_map/ppermute | solution.py:815
  26.8 0.0 copy-done.1
  26.8 0.0 copy-start.3
  26.8 1.4 %widen_codes.1.codes_ref = bf16[1024,2304]{1,0:T(8,128)(2,1)S(1)} custom-call(s32[18,1024]{1,0:T(8,128)S(1)} %bitcast.8), custom_call_target="tpu_custom_call" | custom-call | flops 1000000000 | bytes 1000000 | tf_op jit(solution)/shard_map/widen_codes/pallas_call | solution.py:562
  28.3 2.9 %collective-permute-done.5.other_ref.refs_0_ = bf16[144,512]{1,0:T(8,128)(2,1)S(1)} collective-permute-done((bf16[144,512]{1,0:T(8,128)(2,1)S(1)}, bf16[144,512]{1,0:T(8,128)(2,1)S(1)}, u32[]{:S(2)}, u32[]{:S(2)}) %collective-permute-start.5) | collective-permute-done | bytes 147488 | tf_op jit(solution)/shard_map/ppermute | solution.py:815
  31.2 0.0 collective-permute-start.8
  31.2 0.6 %join_runs.3 = bf16[144,512]{1,0:T(8,128)(2,1)S(1)} custom-call(s32[4]{0:T(128)S(1)} %pad_add_fusion.place_ref, bf16[144,512]{1,0:T(8,128)(2,1)S(1)} %join_runs.2.own_ref, bf16[144,512]{1,0:T(8,128)(2,1)S(1)} %collective-permute-done.5.other_ref.refs_0_), custom_call_target="tpu_custom_call" | custom-call | flops 1000000 | bytes 100000 | tf_op jit(solution)/shard_map/join_runs/pallas_call | solution.py:536
  31.8 2.6 %collective-permute-start.6 = (bf16[144,512]{1,0:T(8,128)(2,1)S(1)}, bf16[144,512]{1,0:T(8,128)(2,1)S(1)}, u32[]{:S(2)}, u32[]{:S(2)}) collective-permute-start(bf16[144,512]{1,0:T(8,128)(2,1)S(1)} %join_runs.3), channel_id=1, source_target_pairs={{0,8},{4,12},{8,0},{12,4},{1,9},{5,13},{9,1},{13,5},{2,10},{6,14},... | collective-permute-start | bytes 442376 | tf_op jit(solution)/shard_map/ppermute | solution.py:815
  34.4 0.0 collective-permute-done.7.c_other_ref
  34.4 0.0 copy-done.3
  34.4 3.1 %level_products.1 = (bf16[1024,512]{1,0:T(8,128)(2,1)S(1)}, bf16[1024,256]{1,0:T(8,128)(2,1)S(1)}, bf16[1024,128]{1,0:T(8,128)(2,1)S(1)}) custom-call(f32[18]{0:T(128)S(1)} %copy-done.3, bf16[128,1024]{1,0:T(8,128)(2,1)} %get-tuple-element.54.turned_far_ref, bf16[1024,128]{1,0:T(8,128)(2,1)} %get-tuple-element.55.c_far_ref, ...), custom_call_target="tpu_custom_call" | custom-call | flops 1000000000 | bytes 10000000 | tf_op jit(solution)/shard_map/level_products/pallas_call | solution.py:632
  37.4 0.0 collective-permute-done.8.refs_1_
  37.5 0.0 copy-start.2
  37.5 4.0 %local_terms.1 = (bf16[1024,1024]{1,0:T(8,128)(2,1)S(1)}, bf16[1024,1024]{1,0:T(8,128)(2,1)S(1)}, f32[8,1024]{1,0:T(8,128)S(1)}) custom-call(s32[4]{0:T(128)S(1)} %pad_add_fusion.place_ref, bf16[1024,1024]{1,0:T(8,128)(2,1)} %get-tuple-element.53.hidden_far_ref, bf16[1024,512]{1,0:T(8,128)(2,1)S(1)} %get-tuple-element.58.left_ref, ...), custom_call_target="tpu_custom_call" | custom-call | flops 3000000000 | bytes 10000000 | tf_op jit(solution)/shard_map/local_terms/pallas_call | solution.py:723
  41.4 0.8 %collective-permute-done.6.message_ref = bf16[144,512]{1,0:T(8,128)(2,1)S(1)} collective-permute-done((bf16[144,512]{1,0:T(8,128)(2,1)S(1)}, bf16[144,512]{1,0:T(8,128)(2,1)S(1)}, u32[]{:S(2)}, u32[]{:S(2)}) %collective-permute-start.6) | collective-permute-done | bytes 147488 | tf_op jit(solution)/shard_map/ppermute | solution.py:815
  42.2 0.0 collective-permute-start.9
  42.2 0.0 copy-done.2
  42.2 1.6 %carried_and_norm.2.refs_0_ = bf16[1024,512]{1,0:T(8,128)(2,1)S(1)} custom-call(s32[4]{0:T(128)S(1)} %pad_add_fusion.place_ref, bf16[144,512]{1,0:T(8,128)(2,1)S(1)} %collective-permute-done.6.message_ref, f32[8,1024]{1,0:T(8,128)S(1)} %get-tuple-element.65.before_ref, bf16[1024,1024]{1,0:T(8,128)(2,1)S(1)} %get-tuple-element.66.hidden_ref, ...), custom_call_target="tpu_custom_call" | custom-call | flops 2000000000 | bytes 8000000 | tf_op jit(solution)/shard_map/carried_and_norm/pallas_call | solution.py:792
  43.8 0.0 collective-permute-done.9.message_ref
  43.8 2.5 %carried_and_norm.3 = bf16[1024,1024]{1,0:T(8,128)(2,1)} custom-call(s32[4]{0:T(128)S(1)} %pad_add_fusion.place_ref, bf16[144,512]{1,0:T(8,128)(2,1)S(1)} %collective-permute-done.9.message_ref, f32[8,1024]{1,0:T(8,128)S(1)} %get-tuple-element.65.before_ref, bf16[1024,1024]{1,0:T(8,128)(2,1)S(1)} %get-tuple-element.66.hidden_ref, ...), custom_call_target="tpu_custom_call" | custom-call | flops 2000000000 | bytes 8000000 | tf_op jit(solution)/shard_map/carried_and_norm/pallas_call | solution.py:792
Async XLA Ops:
  0.0 3.9 %copy-start.4 = (bf16[512,256]{1,0:T(8,128)(2,1)S(1)}, bf16[512,256]{1,0:T(8,128)(2,1)}, u32[]{:S(2)}) copy-start(bf16[512,256]{1,0:T(8,128)(2,1)} %own_weight_ref.1) | copy-start | bytes 786436
  0.0 3.9 %copy-start = (bf16[1024,1024]{1,0:T(8,128)(2,1)S(1)}, bf16[1024,1024]{1,0:T(8,128)(2,1)}, u32[]{:S(2)}) copy-start(bf16[1024,1024]{1,0:T(8,128)(2,1)} %key_ref.3) | copy-start | bytes 6291460
  0.0 3.9 %copy-start.6 = (s32[1024]{0:T(1024)S(1)}, s32[1024]{0:T(1024)}, u32[]{:S(2)}) copy-start(s32[1024]{0:T(1024)} %param.18) | copy-start | bytes 12292
  0.0 3.9 %collective-permute-start.1 = (bf16[512,256]{1,0:T(8,128)(2,1)}, bf16[512,256]{1,0:T(8,128)(2,1)}, u32[]{:S(2)}, u32[]{:S(2)}) collective-permute-start(bf16[512,256]{1,0:T(8,128)(2,1)} %own_weight_ref.1), channel_id=1, source_target_pairs={{0,1},{1,0},{2,3},{3,2},{4,5},{5,4},{6,7},{7,6},{8,9},{9,8},{10,11... | collective-permute-start | bytes 786440 | tf_op jit(solution)/shard_map/ppermute | solution.py:815
  1.9 11.7 %collective-permute-start = (bf16[256,1024]{1,0:T(8,128)(2,1)S(1)}, bf16[256,1024]{1,0:T(8,128)(2,1)S(1)}, u32[]{:S(2)}, u32[]{:S(2)}) collective-permute-start(bf16[256,1024]{1,0:T(8,128)(2,1)S(1)} %edge_rows.1), channel_id=1, source_target_pairs={{0,1},{1,4},{4,5},{5,8},{8,9},{9,12},{12,13},{2,3},{3,6},{6,7},{7,... | collective-permute-start | bytes 1572872 | tf_op jit(solution)/shard_map/ppermute | solution.py:811
  10.7 7.9 %collective-permute-start.3 = (bf16[768,128]{1,0:T(8,128)(2,1)S(1)}, bf16[768,128]{1,0:T(8,128)(2,1)S(1)}, u32[]{:S(2)}, u32[]{:S(2)}) collective-permute-start(bf16[768,128]{1,0:T(8,128)(2,1)S(1)} %get-tuple-element.45.late_own_ref), channel_id=1, source_target_pairs={{0,2},{2,0},{1,3},{3,1},{4,6},{6,4},{5,7},{7,5},{8,10},{10,8},{9,1... | collective-permute-start | bytes 589832 | tf_op jit(solution)/shard_map/ppermute | solution.py:815
  13.6 1.3 %copy-start.5 = (f32[1024,16]{0,1:T(8,128)S(1)}, f32[1024,16]{0,1:T(8,128)}, u32[]{:S(2)}) copy-start(f32[1024,16]{0,1:T(8,128)} %param.15) | copy-start | bytes 196612
  14.8 5.2 %collective-permute-start.2 = (bf16[256,128]{1,0:T(8,128)(2,1)S(1)}, bf16[256,128]{1,0:T(8,128)(2,1)S(1)}, u32[]{:S(2)}, u32[]{:S(2)}) collective-permute-start(bf16[256,128]{1,0:T(8,128)(2,1)S(1)} %get-tuple-element.44.early_own_ref), channel_id=1, source_target_pairs={{0,2},{2,0},{1,3},{3,1},{4,6},{6,4},{5,7},{7,5},{8,10},{10,8},{9,1... | collective-permute-start | bytes 196616 | tf_op jit(solution)/shard_map/ppermute | solution.py:815
  17.9 9.0 %copy-start.1 = (s32[1024,18]{0,1:T(8,128)S(1)}, s32[1024,18]{0,1:T(8,128)}, u32[]{:S(2)}) copy-start(s32[1024,18]{0,1:T(8,128)} %param.16) | copy-start | bytes 221188
  21.9 2.7 %collective-permute-start.4 = (bf16[144,1024]{1,0:T(8,128)(2,1)S(1)}, bf16[144,1024]{1,0:T(8,128)(2,1)S(1)}, u32[]{:S(2)}, u32[]{:S(2)}) collective-permute-start(bf16[144,1024]{1,0:T(8,128)(2,1)S(1)} %get-tuple-element.51.own_ref), channel_id=1, source_target_pairs={{0,1},{1,0},{2,3},{3,2},{4,5},{5,4},{6,7},{7,6},{8,9},{9,8},{10,11... | collective-permute-start | bytes 884744 | tf_op jit(solution)/shard_map/ppermute | solution.py:815
  22.5 11.8 %collective-permute-start.7 = (bf16[1024,128]{1,0:T(8,128)(2,1)S(1)}, bf16[1024,128]{1,0:T(8,128)(2,1)S(1)}, u32[]{:S(2)}, u32[]{:S(2)}) collective-permute-start(bf16[1024,128]{1,0:T(8,128)(2,1)S(1)} %get-tuple-element.56.c_ref), channel_id=1, source_target_pairs={{0,2},{2,0},{1,3},{3,1},{4,6},{6,4},{5,7},{7,5},{8,10},{10,8},{9,1... | collective-permute-start | bytes 786440 | tf_op jit(solution)/shard_map/ppermute | solution.py:815
  25.2 6.0 %collective-permute-start.5 = (bf16[144,512]{1,0:T(8,128)(2,1)S(1)}, bf16[144,512]{1,0:T(8,128)(2,1)S(1)}, u32[]{:S(2)}, u32[]{:S(2)}) collective-permute-start(bf16[144,512]{1,0:T(8,128)(2,1)S(1)} %join_runs.2.own_ref), channel_id=1, source_target_pairs={{0,4},{4,0},{8,12},{12,8},{1,5},{5,1},{9,13},{13,9},{2,6},{6,2},{1... | collective-permute-start | bytes 442376 | tf_op jit(solution)/shard_map/ppermute | solution.py:815
  26.8 7.5 %copy-start.3 = (f32[18]{0:T(128)S(1)}, f32[18]{0:T(128)}, u32[]{:S(2)}) copy-start(f32[18]{0:T(128)} %scale_ref.1) | copy-start | bytes 220
  31.2 6.3 %collective-permute-start.8 = (bf16[144,512]{1,0:T(8,128)(2,1)S(1)}, bf16[144,512]{1,0:T(8,128)(2,1)S(1)}, u32[]{:S(2)}, u32[]{:S(2)}) collective-permute-start(bf16[144,512]{1,0:T(8,128)(2,1)S(1)} %collective-permute-done.5.other_ref.refs_0_), channel_id=1, source_target_pairs={{0,1},{1,0},{2,3},{3,2},{4,5},{5,4},{6,7},{7,6},{8,9},{9,8},{10,11... | collective-permute-start | bytes 442376 | tf_op jit(solution)/shard_map/ppermute | solution.py:815
  31.8 10.4 %collective-permute-start.6 = (bf16[144,512]{1,0:T(8,128)(2,1)S(1)}, bf16[144,512]{1,0:T(8,128)(2,1)S(1)}, u32[]{:S(2)}, u32[]{:S(2)}) collective-permute-start(bf16[144,512]{1,0:T(8,128)(2,1)S(1)} %join_runs.3), channel_id=1, source_target_pairs={{0,8},{4,12},{8,0},{12,4},{1,9},{5,13},{9,1},{13,5},{2,10},{6,14},... | collective-permute-start | bytes 442376 | tf_op jit(solution)/shard_map/ppermute | solution.py:815
  37.5 4.7 %copy-start.2 = (f32[1024]{0:T(1024)S(1)}, f32[1024]{0:T(1024)}, u32[]{:S(2)}) copy-start(f32[1024]{0:T(1024)} %param.19) | copy-start | bytes 12292
  42.2 1.6 %collective-permute-start.9 = (bf16[144,512]{1,0:T(8,128)(2,1)S(1)}, bf16[144,512]{1,0:T(8,128)(2,1)S(1)}, u32[]{:S(2)}, u32[]{:S(2)}) collective-permute-start(bf16[144,512]{1,0:T(8,128)(2,1)S(1)} %collective-permute-done.6.message_ref), channel_id=1, source_target_pairs={{0,1},{1,0},{2,3},{3,2},{4,5},{5,4},{6,7},{7,6},{8,9},{9,8},{10,11... | collective-permute-start | bytes 442376 | tf_op jit(solution)/shard_map/ppermute | solution.py:815

commit v4 on v3

--- a/solution.py
+++ b/solution.py
@@ -75,6 +75,15 @@
 def split_rows(rows):
     high = rows.astype(BF16)
     return high, (rows - high.astype(F32)).astype(BF16)
+
+
+def half_index():
+    return lax.axis_index("fsdp")
+
+
+def shard_bit(level):
+    shard = lax.axis_index("seq") * lax.axis_size("fsdp") + lax.axis_index("fsdp")
+    return jnp.bitwise_and(jnp.right_shift(shard, level), 1)
 
 
 def edge_kernel(key_ref, value_ref, edge_ref, sems):
@@ -107,6 +116,36 @@
         cost_estimate=cost(0, 2**20),
         name="edge_rows",
     )(*far_off(key_rows, value_rows))
+
+
+def lower_ones():
+    row = lax.broadcasted_iota(jnp.int32, (CHUNK, CHUNK), 0)
+    lane = lax.broadcasted_iota(jnp.int32, (CHUNK, CHUNK), 1)
+    lower = (lane <= row).astype(F32).astype(BF16)
+    return jnp.concatenate([lower] * 3, axis=1)
+
+
+def chunk_sums(lower, rate):
+    first = rate.astype(BF16)
+    second, third = split_rows(rate - first.astype(F32))
+    return dot_turned(lower, jnp.concatenate([first, second, third], axis=1))
+
+
+def fade_wide(rate_ref, fall, carry, fall_ref, carry_ref):
+    heads, row_count = rate_ref.shape
+    width = fall_ref.shape[1]
+    lower = lower_ones()
+    spread = spread_matrix(heads, width)
+    prefix = jnp.zeros((1, heads), F32)
+    for at in range(0, row_count, CHUNK):
+        rows = slice(at, at + CHUNK)
+        total = chunk_sums(lower, rate_ref[:, rows])
+        fall[rows, :] = jnp.exp(total[CHUNK // 2 - 1 : CHUNK // 2] - total).astype(BF16)
+        carry[rows, :] = jnp.exp(-(total + prefix)).astype(BF16)
+        prefix = prefix + total[CHUNK - 1 :]
+    for lanes in lane_tiles(width):
+        fall_ref[:, lanes] = dot(fall[...], spread[:, lanes]).astype(BF16)
+        carry_ref[:, lanes] = dot(carry[...], spread[:, lanes]).astype(BF16)
 
 
 def chunk_masks(doc_pos):
@@ -155,14 +194,16 @@
 
 def late_kernel(
     split,
-    place_ref,
     pos_ref,
+    rate_ref,
     query_ref,
     key_ref,
     value_ref,
     residual_ref,
     own_weight_ref,
     other_weight_ref,
+    fall_ref,
+    carry_ref,
     hidden_ref,
     c_ref,
     weight_ref,
@@ -174,6 +215,8 @@
     query_buf,
     value_buf,
     residual_buf,
+    fall,
+    carry,
     sems,
 ):
     row_count, width = query_ref.shape
@@ -205,11 +248,12 @@
     for chunk in range(split - 1):
         for which in range(3):
             copy_early(which, chunk).start()
-    is_low = place_ref[0] == 0
+    is_low = half_index() == 0
     own_weight, other_weight = own_weight_ref[...], other_weight_ref[...]
     weight_ref[:half_width, :] = jnp.where(is_low, own_weight, other_weight)
     weight_ref[half_width:, :] = jnp.where(is_low, other_weight, own_weight)
     key_early_ref[...] = key_ref[: split * CHUNK, :]
+    fade_wide(rate_ref, fall, carry, fall_ref, carry_ref)
 
     def attend_one(chunk, value_before):
         for which in range(3):
@@ -245,28 +289,31 @@
             copy_early(which, chunk).wait()
 
 
-def attend_late(split, place, positions, query, key, value, residual, weights):
+def attend_late(split, positions, rate_turned, query, key, value, residual, weights):
     row_count, width = query.shape
     chunks = row_count // CHUNK
     late = row_count - split * CHUNK
     return pl.pallas_call(
         functools.partial(late_kernel, split),
-        in_specs=[SMEM, VMEM, HBM, VMEM, HBM, HBM, VMEM, VMEM],
-        out_specs=[VMEM] * 8,
+        in_specs=[VMEM, VMEM, HBM, VMEM, HBM, HBM, VMEM, VMEM],
+        out_specs=[VMEM] * 10,
         out_shape=[
+            shaped((row_count, width), BF16),
+            shaped((row_count, width), BF16),
             shaped((row_count, width), BF16),
             shaped((row_count, STATES), BF16),
             shaped((width, 2 * STATES), BF16),
             shaped((late, STATES), BF16),
         ]
         + [shaped((split * CHUNK, width), BF16)] * 4,
-        scratch_shapes=[pltpu.VMEM((late, width), BF16)] * 3 + [pltpu.SemaphoreType.DMA((3, chunks))],
+        scratch_shapes=[pltpu.VMEM((late, width), BF16)] * 3
+        + [pltpu.VMEM((row_count, rate_turned.shape[0]), BF16)] * 2
+        + [pltpu.SemaphoreType.DMA((3, chunks))],
         compiler_params=params(),
         cost_estimate=cost(6 * 10**9, 10**7),
         name="attention_late",
     )(
-        place,
-        *near_by(positions),
+        *near_by(positions, rate_turned),
         *far_off(query),
         *near_by(key),
         *far_off(value, residual),
@@ -335,32 +382,15 @@
     )(*near_by(positions, edges, *parts, weight, hidden, c_mat))
 
 
-def lower_ones():
-    row = lax.broadcasted_iota(jnp.int32, (CHUNK, CHUNK), 0)
-    lane = lax.broadcasted_iota(jnp.int32, (CHUNK, CHUNK), 1)
-    lower = (lane <= row).astype(F32).astype(BF16)
-    return jnp.concatenate([lower] * 3, axis=1)
-
-
-def chunk_sums(lower, rate):
-    first = rate.astype(BF16)
-    second, third = split_rows(rate - first.astype(F32))
-    return dot_turned(lower, jnp.concatenate([first, second, third], axis=1))
-
-
 def scale_kernel(
     rate_ref,
     hidden_ref,
     c_ref,
     scaled_ref,
     rows_ref,
-    fall_ref,
-    carry_ref,
     hidden_far_ref,
     c_far_ref,
     rise,
-    fall,
-    carry,
     logs,
     sems,
 ):
@@ -376,28 +406,22 @@
     spread = spread_matrix(heads, width)
     lower = lower_ones()
     row_idx = lax.broadcasted_iota(jnp.int32, (8, heads), 0)
-    prefix = jnp.zeros((1, heads), F32)
     for chunk in range(chunks):
         rows = slice(chunk * CHUNK, (chunk + 1) * CHUNK)
         total = chunk_sums(lower, rate_ref[:, rows])
         middle = total[CHUNK // 2 - 1 : CHUNK // 2]
         last = total[CHUNK - 1 :]
         rise[rows, :] = jnp.exp(total - middle).astype(BF16)
-        fall[rows, :] = jnp.exp(middle - total).astype(BF16)
-        carry[rows, :] = jnp.exp(-(total + prefix)).astype(BF16)
         logs[chunk * 8 : (chunk + 1) * 8, :] = jnp.where(
             row_idx == 0,
             middle - last,
             jnp.where(row_idx == 1, -last, jnp.where(row_idx == 2, -middle, 0.0)),
         )
-        prefix = prefix + last
     high, low = split_rows(jnp.exp(logs[...]))
     for lanes in lane_tiles(width):
         wide = dot(rise[...], spread[:, lanes])
         scaled_ref[:, lanes] = (wide * hidden_ref[:, lanes].astype(F32)).astype(BF16)
         rows_ref[:, lanes] = dot(high, spread[:, lanes]) + dot(low, spread[:, lanes])
-        fall_ref[:, lanes] = dot(fall[...], spread[:, lanes]).astype(BF16)
-        carry_ref[:, lanes] = dot(carry[...], spread[:, lanes]).astype(BF16)
     for copy in copies:
         copy.wait()
 
@@ -409,16 +433,14 @@
     return pl.pallas_call(
         scale_kernel,
         in_specs=[VMEM] * 3,
-        out_specs=[VMEM] * 4 + [HBM] * 2,
+        out_specs=[VMEM] * 2 + [HBM] * 2,
         out_shape=[
             shaped((row_count, width), BF16),
             shaped((chunks * 8, width), F32),
-            shaped((row_count, width), BF16),
-            shaped((row_count, width), BF16),
             far_shaped(hidden.shape, BF16),
             far_shaped(c_mat.shape, BF16),
         ],
-        scratch_shapes=[pltpu.VMEM((row_count, heads), BF16)] * 3
+        scratch_shapes=[pltpu.VMEM((row_count, heads), BF16)]
         + [pltpu.VMEM((chunks * 8, heads), F32), pltpu.SemaphoreType.DMA((chunks + 1,))],
         compiler_params=params(),
         cost_estimate=cost(10**9, 4 * 10**6),
@@ -427,7 +449,6 @@
 
 
 def state_kernel(
-    local_levels,
     early_own_ref,
     early_other_ref,
     late_own_ref,
@@ -435,7 +456,6 @@
     scaled_ref,
     rows_ref,
     state_ref,
-    runs_ref,
     turned_far_ref,
     turned,
     sems,
@@ -458,28 +478,14 @@
 
     def step(at, carry):
         lanes = pl.ds(pl.multiple_of(at * tile, tile), tile)
-        held = {}
-        fade = None
+        total = fade = None
         for chunk in range(chunks):
+            span = slice(chunk * CHUNK, (chunk + 1) * CHUNK)
             factor = rows_ref[chunk * 8 : (chunk + 1) * 8, lanes]
-            fades = factor[1:2]
-            for level in range(local_levels):
-                start = (chunk * local_levels + level) * STATES
-                if level in held:
-                    run = (held[level] * factor[2:3]).astype(BF16)
-                else:
-                    run = jnp.zeros((STATES, tile), BF16)
-                runs_ref[start : start + STATES, lanes] = run
-            span = slice(chunk * CHUNK, (chunk + 1) * CHUNK)
-            joined = dot(turned[:, span], scaled_ref[span, lanes]) * factor[0:1]
-            held = {level: state * fades for level, state in held.items()}
-            level = 0
-            while level in held:
-                joined = joined + held.pop(level)
-                level += 1
-            held[level] = joined
-            fade = fades if fade is None else fade * fades
-        state_ref[:STATES, lanes] = held[local_levels].astype(BF16)
+            added = dot(turned[:, span], scaled_ref[span, lanes]) * factor[0:1]
+            total = added if total is None else total * factor[1:2] + added
+            fade = factor[1:2] if fade is None else fade * factor[1:2]
+        state_ref[:STATES, lanes] = total.astype(BF16)
         state_ref[STATES:, lanes] = fade_rows(fade)
         return carry
 
@@ -499,17 +505,11 @@
 
 def block_state(early_own, early_other, late_own, late_other, scaled, factor_rows):
     row_count, width = scaled.shape
-    chunks = row_count // CHUNK
-    local_levels = chunks.bit_length() - 1
     return pl.pallas_call(
-        functools.partial(state_kernel, local_levels),
+        state_kernel,
         in_specs=[VMEM] * 6,
-        out_specs=[VMEM, VMEM, HBM],
-        out_shape=[
-            shaped((STATES + EXTRA, width), BF16),
-            shaped((chunks * local_levels * STATES, width), BF16),
-            far_shaped((STATES, row_count), BF16),
-        ],
+        out_specs=[VMEM, HBM],
+        out_shape=[shaped((STATES + EXTRA, width), BF16), far_shaped((STATES, row_count), BF16)],
         scratch_shapes=[pltpu.VMEM((STATES, row_count), BF16), pltpu.SemaphoreType.DMA((1,))],
         compiler_params=params(),
         cost_estimate=cost(3 * 10**8, 4 * 10**6),
@@ -517,34 +517,39 @@
     )(*near_by(early_own, early_other, late_own, late_other, scaled, factor_rows))
 
 
-def join_kernel(level, place_ref, own_ref, other_ref, joined_ref):
+def join_kernel(level, own_ref, other_ref, joined_ref):
     half_width = joined_ref.shape[1]
     own, other = own_ref[...], other_ref[...]
     if own.shape[1] != half_width:
-        is_low = place_ref[0] == 0
+        is_low = half_index() == 0
         own = jnp.where(is_low, own[:, :half_width], own[:, half_width:])
         other = jnp.where(is_low, other[:, :half_width], other[:, half_width:])
-    upper = place_ref[1 + level] == 1
+    upper = shard_bit(level) == 1
     own_fade, other_fade = fade_of(own), fade_of(other)
     lower, higher = jnp.where(upper, other, own), jnp.where(upper, own, other)
     fade = jnp.where(upper, own_fade, other_fade)
     joined_ref[:STATES, :] = (lower[:STATES].astype(F32) * fade + higher[:STATES].astype(F32)).astype(BF16)
-    joined_ref[STATES:, :] = fade_rows(own_fade * other_fade)
-
-
-def join(level, place, own, other, half_width):
+    if joined_ref.shape[0] > STATES:
+        joined_ref[STATES:, :] = fade_rows(own_fade * other_fade)
+
+
+def join(level, own, other, half_width, last):
     return pl.pallas_call(
         functools.partial(join_kernel, level),
-        in_specs=[SMEM, VMEM, VMEM],
+        in_specs=[VMEM, VMEM],
         out_specs=VMEM,
-        out_shape=shaped((own.shape[0], half_width), BF16),
+        out_shape=shaped((STATES if last else STATES + EXTRA, half_width), BF16),
         compiler_params=params(),
         cost_estimate=cost(10**6, 10**5),
         name="join_runs",
-    )(place, *near_by(own, other))
-
-
-def codes_kernel(codes_ref, wide_ref):
+    )(*near_by(own, other))
+
+
+def runs_kernel(local_levels, turned_far_ref, codes_ref, scaled_ref, rows_ref, wide_ref, runs_ref, turned, sems):
+    row_count, width = scaled_ref.shape
+    chunks = row_count // CHUNK
+    turned_copy = pltpu.make_async_copy(turned_far_ref, turned, sems.at[0])
+    turned_copy.start()
     codes = codes_ref[...].astype(F32).T.astype(BF16)
     levels = codes.shape[1]
     pair = 2 * CHUNK
@@ -554,20 +559,55 @@
         start = (level_of * CHUNK) - at
         pick = ((lane >= start) & (lane < start + CHUNK)).astype(F32).astype(BF16)
         wide_ref[:, at : at + pair] = dot(codes, pick).astype(BF16)
-
-
-def widen_codes(codes_turned):
-    levels, row_count = codes_turned.shape
+    turned_copy.wait()
+    tile = min(width, 256)
+
+    def step(at, token):
+        lanes = pl.ds(pl.multiple_of(at * tile, tile), tile)
+        held = {}
+        for chunk in range(chunks):
+            factor = rows_ref[chunk * 8 : (chunk + 1) * 8, lanes]
+            for level in range(local_levels):
+                start = (chunk * local_levels + level) * STATES
+                if level in held:
+                    run = (held[level] * factor[2:3]).astype(BF16)
+                else:
+                    run = jnp.zeros((STATES, tile), BF16)
+                runs_ref[start : start + STATES, lanes] = run
+            if chunk == chunks - 1:
+                break
+            span = slice(chunk * CHUNK, (chunk + 1) * CHUNK)
+            joined = dot(turned[:, span], scaled_ref[span, lanes]) * factor[0:1]
+            held = {level: state * factor[1:2] for level, state in held.items()}
+            level = 0
+            while level in held:
+                joined = joined + held.pop(level)
+                level += 1
+            held[level] = joined
+        return token
+
+    lax.fori_loop(0, width // tile, step, 0)
+
+
+def codes_and_runs(turned_far, codes_turned, scaled, factor_rows):
+    row_count, width = scaled.shape
+    levels = codes_turned.shape[0]
     levels += levels % 2
+    chunks = row_count // CHUNK
+    local_levels = chunks.bit_length() - 1
     return pl.pallas_call(
-        codes_kernel,
-        in_specs=[VMEM],
-        out_specs=VMEM,
-        out_shape=shaped((row_count, levels * CHUNK), BF16),
+        functools.partial(runs_kernel, local_levels),
+        in_specs=[HBM] + [VMEM] * 3,
+        out_specs=[VMEM] * 2,
+        out_shape=[
+            shaped((row_count, levels * CHUNK), BF16),
+            shaped((chunks * local_levels * STATES, width), BF16),
+        ],
+        scratch_shapes=[pltpu.VMEM((STATES, row_count), BF16), pltpu.SemaphoreType.DMA((1,))],
         compiler_params=params(),
-        cost_estimate=cost(10**9, 10**6),
-        name="widen_codes",
-    )(*near_by(codes_turned))
+        cost_estimate=cost(10**9, 10**7),
+        name="codes_and_runs",
+    )(*far_off(turned_far), *near_by(codes_turned, scaled, factor_rows))
 
 
 def weights_kernel(
@@ -656,7 +696,6 @@
 def local_kernel(
     local_levels,
     cross_levels,
-    place_ref,
     hidden_far_ref,
     left_ref,
     early_reads_ref,
@@ -681,10 +720,10 @@
     for copy in copies:
         copy.start()
 
-    is_low = place_ref[0] == 0
+    is_low = half_index() == 0
     before = jnp.ones((1, width), F32)
     for level in range(cross_levels - 1):
-        upper = place_ref[1 + level]
+        upper = shard_bit(level)
         if level == 0:
             message = near_ref[...]
         else:
@@ -716,13 +755,13 @@
         copy.wait()
 
 
-def local_terms(place, hidden_far, left, early_reads, scaled, fall, carry, runs, near, received, swapped):
+def local_terms(hidden_far, left, early_reads, scaled, fall, carry, runs, near, received, swapped):
     row_count, width = scaled.shape
     local_levels = (row_count // CHUNK).bit_length() - 1
     cross_levels = 2 + len(received)
     return pl.pallas_call(
         functools.partial(local_kernel, local_levels, cross_levels),
-        in_specs=[SMEM, HBM] + [VMEM] * (7 + 2 * len(received)),
+        in_specs=[HBM] + [VMEM] * (7 + 2 * len(received)),
         out_specs=[VMEM] * 3,
         out_shape=[shaped((row_count, width), BF16)] * 2 + [shaped((8, width), F32)],
         scratch_shapes=[
@@ -734,20 +773,19 @@
         cost_estimate=cost(3 * 10**9, 10**7),
         name="local_terms",
     )(
-        place,
         *far_off(hidden_far),
         *near_by(left, early_reads, scaled, fall, carry, runs, near, *received, *swapped),
     )
 
 
 def finish_kernel(
-    swap, place_ref, message_ref, before_ref, hidden_ref, reads_ref, local_ref, carry_ref, gain_ref, *refs
+    swap, cross_levels, message_ref, before_ref, hidden_ref, reads_ref, local_ref, carry_ref, gain_ref, *refs
 ):
     row_count, width = local_ref.shape
     half_width = width // 2
-    own_start = place_ref[0] * half_width
+    own_start = half_index() * half_width
     start = half_width - own_start if swap else own_start
-    upper = place_ref[place_ref.shape[0] - 1]
+    upper = shard_bit(cross_levels - 1)
     tile = min(half_width, 256)
     row = lax.broadcasted_iota(jnp.int32, (tile, tile), 0) // HEAD_VALUES
     lane = lax.broadcasted_iota(jnp.int32, (tile, tile), 1) // HEAD_VALUES
@@ -773,25 +811,25 @@
         lanes = pl.ds(pl.multiple_of(start + at * tile, tile), tile)
         here = slice(at * tile, (at + 1) * tile)
         carried = carried_state(message_ref[:, here], before_ref[0:1, lanes], upper)
-        cross = dot(reads_ref[...], carried)
-        mixed = local_ref[:, lanes].astype(F32) + cross * carry_ref[:, lanes].astype(F32)
-        mean = dot((mixed * mixed).astype(BF16), mean_mat)
-        normed = mixed * lax.rsqrt(mean + 1e-05) * gain_ref[:, lanes]
-        result[:, here] = (hidden_ref[:, lanes].astype(F32) + normed).astype(BF16)
+        cross = dot(reads_ref[...], carried).astype(BF16)
+        mixed = local_ref[:, lanes] + cross * carry_ref[:, lanes]
+        mean = dot(mixed * mixed, mean_mat)
+        normed = mixed * lax.rsqrt(mean + 1e-05).astype(BF16) * gain_ref[:, lanes].astype(BF16)
+        result[:, here] = hidden_ref[:, lanes] + normed
         if swap:
             copy_out(result, here, lanes, 1 + at)
     for copy in copies:
         copy.wait()
 
 
-def finish(place, message, before, hidden, reads, local, carry, gain, held):
+def finish(cross_levels, message, before, hidden, reads, local, carry, gain, held):
     row_count, width = local.shape
     half_width = width // 2
     swap = held is not None
     half_shape = (row_count, half_width)
     return pl.pallas_call(
-        functools.partial(finish_kernel, swap),
-        in_specs=[SMEM] + [VMEM] * (8 if swap else 7),
+        functools.partial(finish_kernel, swap, cross_levels),
+        in_specs=[VMEM] * (8 if swap else 7),
         out_specs=HBM if swap else VMEM,
         out_shape=far_shaped((row_count, width), BF16) if swap else shaped(half_shape, BF16),
         scratch_shapes=[
@@ -803,7 +841,7 @@
         compiler_params=params(),
         cost_estimate=cost(2 * 10**9, 8 * 10**6),
         name="carried_and_norm",
-    )(place, *near_by(message, before, hidden, reads, local, carry, gain, *([held] if swap else [])))
+    )(*near_by(message, before, hidden, reads, local, carry, gain, *([held] if swap else [])))
 
 
 def from_behind(x, axis, by):
@@ -841,53 +879,49 @@
     half_width = width // 2
     shard_axes = ("seq", "fsdp")
     cross_levels = lax.axis_size(shard_axes).bit_length() - 1
-    shard = lax.axis_index(shard_axes)
-    half_index = lax.axis_index("fsdp")
-    place = jnp.stack(
-        [half_index] + [jnp.bitwise_and(jnp.right_shift(shard, level), 1) for level in range(cross_levels)]
-    ).astype(jnp.int32)
 
     weights = (bc_weight, partner(bc_weight, "fsdp", 0))
     edges = from_behind(edge_rows(key_rows, value_rows), shard_axes, 1)
     pos_rows = positions.reshape(row_count // CHUNK, CHUNK)
     split = max(1, row_count // CHUNK // 4)
-    hidden, c_mat, weight, b_late, *parts = attend_late(
-        split, place, pos_rows, query_rows, key_rows, value_rows, residual_in, weights
+    rate_turned = decay_rate.T
+    fall, carry, hidden, c_mat, weight, b_late, *parts = attend_late(
+        split, pos_rows, rate_turned, query_rows, key_rows, value_rows, residual_in, weights
     )
     late_own, late_other = summed_over_heads(b_late)
     hidden, c_mat, b_early = attend_early(split, pos_rows, edges, parts, weight, hidden, c_mat)
     early_own, early_other = summed_over_heads(b_early)
-    scaled, factor_rows, fall, carry, hidden_far, c_far = scale_hidden(decay_rate.T, hidden, c_mat)
+    scaled, factor_rows, hidden_far, c_far = scale_hidden(rate_turned, hidden, c_mat)
     c_mat, scaled = lax.optimization_barrier((c_mat, scaled))
     c_sent, c_other = summed_over_heads(c_mat)
     if lax.axis_size("head") > 2:
         c_far = c_sent
-    state, runs, turned_far = block_state(
+    state, turned_far = block_state(
         early_own, early_other, late_own, late_other, scaled, factor_rows
     )
     near = partner(state, "fsdp", 0)
-    joined = join(0, place, state, near, half_width)
+    joined = join(0, state, near, half_width, cross_levels == 2)
     received, swapped = [], []
     for level in range(1, cross_levels):
         other = partner(joined, "seq", level - 1)
         if level == 1:
-            codes_wide = widen_codes(level_codes.T)
+            codes_wide, runs = codes_and_runs(turned_far, level_codes.T, scaled, factor_rows)
             other, codes_wide = lax.optimization_barrier((other, codes_wide))
         received.append(other)
         if level < cross_levels - 1:
-            joined = join(level, place, joined, other, half_width)
+            joined = join(level, joined, other, half_width, level == cross_levels - 2)
             swapped.append(partner(other, "fsdp", 0))
     left, early_reads, last_reads = level_products(
         level_scale, turned_far, c_far, c_other, codes_wide, cross_levels
     )
     local, hidden, before = local_terms(
-        place, hidden_far, left, early_reads, scaled, fall, carry, runs, near, received[:-1], swapped
+        hidden_far, left, early_reads, scaled, fall, carry, runs, near, received[:-1], swapped
     )
     last, local = lax.optimization_barrier((received[-1], local))
     last_swapped = partner(last, "fsdp", 0)
     gain = ssm_gain[None, :]
-    half = finish(place, last, before, hidden, last_reads, local, carry, gain, None)
-    return finish(place, last_swapped, before, hidden, last_reads, local, carry, gain, half)
+    half = finish(cross_levels, last, before, hidden, last_reads, local, carry, gain, None)
+    return finish(cross_levels, last_swapped, before, hidden, last_reads, local, carry, gain, half)
 
 
 def solution(mesh):

time: 46.6 us -> 42.4 us (0.910)
  Pallas kernels: 28 us -> 23.9 us
    pallas_call x8, Pallas kernels: 18.4 us -> 14.7 us  [the longest x1 6.18 us: attend_late(): pl.pallas_call(functools.partial(late_kernel, split), in_specs=[VMEM, VME...]
  transfers between devices with their start and end apart: 10 -> 10, of which waited for: 4 -> 5; matrix products, arithmetic and copies ran while one was open for 0% -> 0% of each run, Pallas kernels for 51% -> 49%
where the time goes in v4:
time: 42.4 us; the launch traced here: 42.2 us
  Pallas kernels  23.9 us (56%)
  starting transfers between devices  12.5 us (29%)
  waiting for transfers between devices  5.63 us (13%)
    ppermute x9, starting transfers between devices, partner(): lax.ppermute(x, axis, [(i, i ^ 1 << distance) for i in range(lax.axis_siz...  10.6 us
    pallas_call x1, Pallas kernels, attend_late(): pl.pallas_call(functools.partial(late_kernel, split), in_specs=[VMEM, VME...  6.18 us
    ppermute x9, waiting for transfers between devices, partner(): lax.ppermute(x, axis, [(i, i ^ 1 << distance) for i in range(lax.axis_siz...  5.63 us
    pallas_call x1, Pallas kernels, local_terms(): pl.pallas_call(functools.partial(local_kernel, local_levels, cross_levels...  3.5 us
    pallas_call x1, Pallas kernels, level_products(): pl.pallas_call(functools.partial(weights_kernel, local_levels, cross_leve...  3.07 us
    pallas_call x1, Pallas kernels, codes_and_runs(): pl.pallas_call(functools.partial(runs_kernel, local_levels), in_specs=[HB...  3.01 us
    pallas_call x2, Pallas kernels, finish(): pl.pallas_call(functools.partial(finish_kernel, swap, cross_levels), in_s...  2.55 us
    ppermute x1, starting transfers between devices, from_behind(): return lax.ppermute(x, axis, [(i, i + by) for i in range(length - by)])  1.92 us
  transfers between devices with their start and end apart: 10, of which 5 were waited for; matrix products, arithmetic and copies ran while one was open for 0% of the time, Pallas kernels for 49%

profile of v4, /device:TPU:0, one launch (start us, length us, event | category | flops | bytes accessed | tf_op | source)
XLA Modules:
  0.0 42.2 jit_solution(8965727337191638656)
XLA Ops:
  0.0 0.0 copy-start.3
  0.0 0.0 copy-start
  0.0 0.0 copy-start.6
  0.0 0.0 copy-start.5
  0.0 0.5 %collective-permute-start.1 = (bf16[512,256]{1,0:T(8,128)(2,1)}, bf16[512,256]{1,0:T(8,128)(2,1)S(1)}, u32[]{:S(2)}, u32[]{:S(2)}) collective-permute-start(bf16[512,256]{1,0:T(8,128)(2,1)} %own_weight_ref.1), channel_id=1, source_target_pairs={{0,1},{1,0},{2,3},{3,2},{4,5},{5,4},{6,7},{7,6},{8,9},{9,8},{10,11... | collective-permute-start | bytes 786440 | tf_op jit(solution)/shard_map/ppermute | solution.py:853
  0.5 1.3 %edge_rows.1 = bf16[256,1024]{1,0:T(8,128)(2,1)S(1)} custom-call(bf16[1024,1024]{1,0:T(8,128)(2,1)} %key_ref.3, bf16[1024,1024]{1,0:T(8,128)(2,1)} %value_ref.3), custom_call_target="tpu_custom_call" | custom-call | bytes 1048576 | tf_op jit(solution)/shard_map/edge_rows/pallas_call | solution.py:109
  1.9 1.9 %collective-permute-start = (bf16[256,1024]{1,0:T(8,128)(2,1)S(1)}, bf16[256,1024]{1,0:T(8,128)(2,1)S(1)}, u32[]{:S(2)}, u32[]{:S(2)}) collective-permute-start(bf16[256,1024]{1,0:T(8,128)(2,1)S(1)} %edge_rows.1), channel_id=1, source_target_pairs={{0,1},{1,4},{4,5},{5,8},{8,9},{9,12},{12,13},{2,3},{3,6},{6,7},{7,... | collective-permute-start | bytes 1572872 | tf_op jit(solution)/shard_map/ppermute | solution.py:849
  3.8 0.0 collective-permute-done.1.other_weight_ref
  3.8 0.0 copy-done.3
  3.8 0.0 copy-done
  3.8 0.0 copy-done.6
  3.8 0.0 copy-done.5
  3.9 6.2 %attention_late.1 = (bf16[1024,1024]{1,0:T(8,128)(2,1)S(1)}, bf16[1024,1024]{1,0:T(8,128)(2,1)S(1)}, bf16[1024,1024]{1,0:T(8,128)(2,1)S(1)}, bf16[1024,128]{1,0:...) custom-call(s32[8,128]{1,0:T(8,128)S(1)} %bitcast.9, ...), custom_call_target="tpu_custom_call" | custom-call | flops 6000000000 | bytes 10000000 | tf_op jit(solution)/shard_map/attention_late/pallas_call | solution.py:296
  10.0 2.9 %collective-permute-start.3 = (bf16[768,128]{1,0:T(8,128)(2,1)S(1)}, bf16[768,128]{1,0:T(8,128)(2,1)S(1)}, u32[]{:S(2)}, u32[]{:S(2)}) collective-permute-start(bf16[768,128]{1,0:T(8,128)(2,1)S(1)} %get-tuple-element.46.late_own_ref), channel_id=1, source_target_pairs={{0,2},{2,0},{1,3},{3,1},{4,6},{6,4},{5,7},{7,5},{8,10},{10,8},{9,1... | collective-permute-start | bytes 589832 | tf_op jit(solution)/shard_map/ppermute | solution.py:853
  12.9 0.0 collective-permute-done.edge_ref
  12.9 1.2 %attention_early.1 = (bf16[1024,1024]{1,0:T(8,128)(2,1)S(1)}, bf16[1024,128]{1,0:T(8,128)(2,1)S(1)}, bf16[256,128]{1,0:T(8,128)(2,1)S(1)}) custom-call(s32[8,128]{1,0:T(8,128)S(1)} %bitcast.10, bf16[256,1024]{1,0:T(8,128)(2,1)S(1)} %collective-permute-done.edge_ref, ...), custom_call_target="tpu_custom_call", output_to_operand_aliasing={{0}: (7, {}), {1}: (8, {})} | custom-call | flops 2000000000 | bytes 2000000 | tf_op jit(solution)/shard_map/attention_early/pallas_call | solution.py:369
  14.2 0.1 collective-permute-start.2
  14.2 1.5 %scale_hidden.1 = (bf16[1024,1024]{1,0:T(8,128)(2,1)S(1)}, f32[64,1024]{1,0:T(8,128)S(1)}, bf16[1024,1024]{1,0:T(8,128)(2,1)}, bf16[1024,128]{1,0:T(8,128)(2,1)}) custom-call(f32[16,1024]{1,0:T(8,128)S(1)} %bitcast.8, bf16[1024,1024]{1,0:T(8,128)(2,1)S(1)} %get-tuple-element.48.hidden_ref, bf16[1024,128]{1,0:T(8,128)(2,1)S(1)} %get-tuple-element.58.c_ref), custom_call_target="tpu_custom_call" | custom-call | flops 1000000000 | bytes 4000000 | tf_op jit(solution)/shard_map/scale_hidden/pallas_call | solution.py:433
  15.7 0.0 copy-start.4
  15.7 2.1 %collective-permute-done.3.late_other_ref = bf16[768,128]{1,0:T(8,128)(2,1)S(1)} collective-permute-done((bf16[768,128]{1,0:T(8,128)(2,1)S(1)}, bf16[768,128]{1,0:T(8,128)(2,1)S(1)}, u32[]{:S(2)}, u32[]{:S(2)}) %collective-permute-start.3) | collective-permute-done | bytes 196640 | tf_op jit(solution)/shard_map/ppermute | solution.py:853
  17.9 1.4 %collective-permute-done.2.early_other_ref = bf16[256,128]{1,0:T(8,128)(2,1)S(1)} collective-permute-done((bf16[256,128]{1,0:T(8,128)(2,1)S(1)}, bf16[256,128]{1,0:T(8,128)(2,1)S(1)}, u32[]{:S(2)}, u32[]{:S(2)}) %collective-permute-start.2) | collective-permute-done | bytes 65568 | tf_op jit(solution)/shard_map/ppermute | solution.py:853
  19.3 1.4 %block_state.1 = (bf16[144,1024]{1,0:T(8,128)(2,1)S(1)}, bf16[128,1024]{1,0:T(8,128)(2,1)}) custom-call(bf16[256,128]{1,0:T(8,128)(2,1)S(1)} %get-tuple-element.45.early_own_ref, bf16[256,128]{1,0:T(8,128)(2,1)S(1)} %collective-permute-done.2.early_other_ref, bf16[768,128]{1,0:T(8,128)(2,1)S(1)} %get-tuple-element.46.late_own_ref, ...), custom_call_target="tpu_custom_call" | custom-call | flops 300000000 | bytes 4000000 | tf_op jit(solution)/shard_map/block_state/pallas_call | solution.py:508
  20.7 0.7 %collective-permute-start.4 = (bf16[144,1024]{1,0:T(8,128)(2,1)S(1)}, bf16[144,1024]{1,0:T(8,128)(2,1)S(1)}, u32[]{:S(2)}, u32[]{:S(2)}) collective-permute-start(bf16[144,1024]{1,0:T(8,128)(2,1)S(1)} %get-tuple-element.52.own_ref), channel_id=1, source_target_pairs={{0,1},{1,0},{2,3},{3,2},{4,5},{5,4},{6,7},{7,6},{8,9},{9,8},{10,11... | collective-permute-start | bytes 884744 | tf_op jit(solution)/shard_map/ppermute | solution.py:853
  21.4 2.0 %collective-permute-start.7 = (bf16[1024,128]{1,0:T(8,128)(2,1)S(1)}, bf16[1024,128]{1,0:T(8,128)(2,1)S(1)}, u32[]{:S(2)}, u32[]{:S(2)}) collective-permute-start(bf16[1024,128]{1,0:T(8,128)(2,1)S(1)} %get-tuple-element.58.c_ref), channel_id=1, source_target_pairs={{0,2},{2,0},{1,3},{3,1},{4,6},{6,4},{5,7},{7,5},{8,10},{10,8},{9,1... | collective-permute-start | bytes 786440 | tf_op jit(solution)/shard_map/ppermute | solution.py:853
  23.4 0.0 collective-permute-done.4.other_ref.near_ref
  23.4 0.1 join_runs.2.own_ref
  23.5 0.0 copy-start.2
  23.5 1.7 %collective-permute-start.5 = (bf16[144,512]{1,0:T(8,128)(2,1)S(1)}, bf16[144,512]{1,0:T(8,128)(2,1)S(1)}, u32[]{:S(2)}, u32[]{:S(2)}) collective-permute-start(bf16[144,512]{1,0:T(8,128)(2,1)S(1)} %join_runs.2.own_ref), channel_id=1, source_target_pairs={{0,4},{4,0},{8,12},{12,8},{1,5},{5,1},{9,13},{13,9},{2,6},{6,2},{1... | collective-permute-start | bytes 442376 | tf_op jit(solution)/shard_map/ppermute | solution.py:853
  25.1 0.0 copy-done.4
  25.1 3.0 %codes_and_runs.1 = (bf16[1024,2304]{1,0:T(8,128)(2,1)S(1)}, bf16[3072,1024]{1,0:T(8,128)(2,1)S(1)}) custom-call(bf16[128,1024]{1,0:T(8,128)(2,1)} %get-tuple-element.53.turned_far_ref, s32[18,1024]{1,0:T(8,128)S(1)} %bitcast.6, bf16[1024,1024]{1,0:T(8,128)(2,1)S(1)} %get-tuple-element.50.scaled_ref, f32[64,1024]{1,0:T(8,128)S(1)} %get-tuple-element.51.rows_ref), custom_call_target="tpu_custom_call" | custom-call | flops 1000000000 | bytes 10000000 | tf_op jit(solution)/shard_map/codes_and_runs/pallas_call | solution.py:598
  28.2 1.2 %collective-permute-done.5.other_ref.refs_0_ = bf16[144,512]{1,0:T(8,128)(2,1)S(1)} collective-permute-done((bf16[144,512]{1,0:T(8,128)(2,1)S(1)}, bf16[144,512]{1,0:T(8,128)(2,1)S(1)}, u32[]{:S(2)}, u32[]{:S(2)}) %collective-permute-start.5) | collective-permute-done | bytes 147488 | tf_op jit(solution)/shard_map/ppermute | solution.py:853
  29.4 0.0 collective-permute-start.8
  29.4 0.1 join_runs.3
  29.4 2.7 %collective-permute-start.6 = (bf16[128,512]{1,0:T(8,128)(2,1)S(1)}, bf16[128,512]{1,0:T(8,128)(2,1)S(1)}, u32[]{:S(2)}, u32[]{:S(2)}) collective-permute-start(bf16[128,512]{1,0:T(8,128)(2,1)S(1)} %join_runs.3), channel_id=1, source_target_pairs={{0,8},{4,12},{8,0},{12,4},{1,9},{5,13},{9,1},{13,5},{2,10},{6,14},... | collective-permute-start | bytes 393224 | tf_op jit(solution)/shard_map/ppermute | solution.py:853
  32.2 0.0 collective-permute-done.7.c_other_ref
  32.2 0.0 copy-done.2
  32.2 3.1 %level_products.1 = (bf16[1024,512]{1,0:T(8,128)(2,1)S(1)}, bf16[1024,256]{1,0:T(8,128)(2,1)S(1)}, bf16[1024,128]{1,0:T(8,128)(2,1)S(1)}) custom-call(f32[18]{0:T(128)S(1)} %copy-done.2, bf16[128,1024]{1,0:T(8,128)(2,1)} %get-tuple-element.53.turned_far_ref, bf16[1024,128]{1,0:T(8,128)(2,1)} %get-tuple-element.57.c_far_ref, ...), custom_call_target="tpu_custom_call" | custom-call | flops 1000000000 | bytes 10000000 | tf_op jit(solution)/shard_map/level_products/pallas_call | solution.py:672
  35.2 0.0 collective-permute-done.8.refs_1_
  35.2 0.0 copy-start.1
  35.3 3.5 %local_terms.1 = (bf16[1024,1024]{1,0:T(8,128)(2,1)S(1)}, bf16[1024,1024]{1,0:T(8,128)(2,1)S(1)}, f32[8,1024]{1,0:T(8,128)S(1)}) custom-call(bf16[1024,1024]{1,0:T(8,128)(2,1)} %get-tuple-element.56.hidden_far_ref, bf16[1024,512]{1,0:T(8,128)(2,1)S(1)} %get-tuple-element.60.left_ref, bf16[1024,256]{1,0:T(8,128)(2,1)S(1)} %get-tuple-element.61.early_reads_ref, ...), custom_call_target="tpu_custom_call" | custom-call | flops 3000000000 | bytes 10000000 | tf_op jit(solution)/shard_map/local_terms/pallas_call | solution.py:762
  38.8 0.4 collective-permute-done.6.message_ref
  39.1 0.0 collective-permute-start.9
  39.1 0.0 copy-done.1
  39.1 0.8 %carried_and_norm.2.refs_0_ = bf16[1024,512]{1,0:T(8,128)(2,1)S(1)} custom-call(bf16[128,512]{1,0:T(8,128)(2,1)S(1)} %collective-permute-done.6.message_ref, f32[8,1024]{1,0:T(8,128)S(1)} %get-tuple-element.67.before_ref, bf16[1024,1024]{1,0:T(8,128)(2,1)S(1)} %get-tuple-element.68.hidden_ref, bf16[1024,128]{1,0:T(8,128)(2,1)S(1)} %get-tuple-element.69.reads_ref, ...), custom_call_target="tpu_custom_call" | custom-call | flops 2000000000 | bytes 8000000 | tf_op jit(solution)/shard_map/carried_and_norm/pallas_call | solution.py:830
  40.0 0.5 %collective-permute-done.9.message_ref = bf16[128,512]{1,0:T(8,128)(2,1)S(1)} collective-permute-done((bf16[128,512]{1,0:T(8,128)(2,1)S(1)}, bf16[128,512]{1,0:T(8,128)(2,1)S(1)}, u32[]{:S(2)}, u32[]{:S(2)}) %collective-permute-start.9) | collective-permute-done | bytes 131104 | tf_op jit(solution)/shard_map/ppermute | solution.py:853
  40.5 1.7 %carried_and_norm.3 = bf16[1024,1024]{1,0:T(8,128)(2,1)} custom-call(bf16[128,512]{1,0:T(8,128)(2,1)S(1)} %collective-permute-done.9.message_ref, f32[8,1024]{1,0:T(8,128)S(1)} %get-tuple-element.67.before_ref, bf16[1024,1024]{1,0:T(8,128)(2,1)S(1)} %get-tuple-element.68.hidden_ref, bf16[1024,128]{1,0:T(8,128)(2,1)S(1)} %get-tuple-element.69.reads_ref, ...), custom_call_target="tpu_custom_call" | custom-call | flops 2000000000 | bytes 8000000 | tf_op jit(solution)/shard_map/carried_and_norm/pallas_call | solution.py:830
Async XLA Ops:
  0.0 3.8 %copy-start.3 = (bf16[512,256]{1,0:T(8,128)(2,1)S(1)}, bf16[512,256]{1,0:T(8,128)(2,1)}, u32[]{:S(2)}) copy-start(bf16[512,256]{1,0:T(8,128)(2,1)} %own_weight_ref.1) | copy-start | bytes 786436
  0.0 3.8 %copy-start = (bf16[1024,1024]{1,0:T(8,128)(2,1)S(1)}, bf16[1024,1024]{1,0:T(8,128)(2,1)}, u32[]{:S(2)}) copy-start(bf16[1024,1024]{1,0:T(8,128)(2,1)} %key_ref.3) | copy-start | bytes 6291460
  0.0 3.8 %copy-start.6 = (s32[1024]{0:T(1024)S(1)}, s32[1024]{0:T(1024)}, u32[]{:S(2)}) copy-start(s32[1024]{0:T(1024)} %param.18) | copy-start | bytes 12292
  0.0 3.8 %copy-start.5 = (f32[1024,16]{0,1:T(8,128)S(1)}, f32[1024,16]{0,1:T(8,128)}, u32[]{:S(2)}) copy-start(f32[1024,16]{0,1:T(8,128)} %param.15) | copy-start | bytes 196612
  0.0 3.8 %collective-permute-start.1 = (bf16[512,256]{1,0:T(8,128)(2,1)}, bf16[512,256]{1,0:T(8,128)(2,1)S(1)}, u32[]{:S(2)}, u32[]{:S(2)}) collective-permute-start(bf16[512,256]{1,0:T(8,128)(2,1)} %own_weight_ref.1), channel_id=1, source_target_pairs={{0,1},{1,0},{2,3},{3,2},{4,5},{5,4},{6,7},{7,6},{8,9},{9,8},{10,11... | collective-permute-start | bytes 786440 | tf_op jit(solution)/shard_map/ppermute | solution.py:853
  1.9 11.0 %collective-permute-start = (bf16[256,1024]{1,0:T(8,128)(2,1)S(1)}, bf16[256,1024]{1,0:T(8,128)(2,1)S(1)}, u32[]{:S(2)}, u32[]{:S(2)}) collective-permute-start(bf16[256,1024]{1,0:T(8,128)(2,1)S(1)} %edge_rows.1), channel_id=1, source_target_pairs={{0,1},{1,4},{4,5},{5,8},{8,9},{9,12},{12,13},{2,3},{3,6},{6,7},{7,... | collective-permute-start | bytes 1572872 | tf_op jit(solution)/shard_map/ppermute | solution.py:849
  10.0 7.8 %collective-permute-start.3 = (bf16[768,128]{1,0:T(8,128)(2,1)S(1)}, bf16[768,128]{1,0:T(8,128)(2,1)S(1)}, u32[]{:S(2)}, u32[]{:S(2)}) collective-permute-start(bf16[768,128]{1,0:T(8,128)(2,1)S(1)} %get-tuple-element.46.late_own_ref), channel_id=1, source_target_pairs={{0,2},{2,0},{1,3},{3,1},{4,6},{6,4},{5,7},{7,5},{8,10},{10,8},{9,1... | collective-permute-start | bytes 589832 | tf_op jit(solution)/shard_map/ppermute | solution.py:853
  14.2 5.1 %collective-permute-start.2 = (bf16[256,128]{1,0:T(8,128)(2,1)S(1)}, bf16[256,128]{1,0:T(8,128)(2,1)S(1)}, u32[]{:S(2)}, u32[]{:S(2)}) collective-permute-start(bf16[256,128]{1,0:T(8,128)(2,1)S(1)} %get-tuple-element.45.early_own_ref), channel_id=1, source_target_pairs={{0,2},{2,0},{1,3},{3,1},{4,6},{6,4},{5,7},{7,5},{8,10},{10,8},{9,1... | collective-permute-start | bytes 196616 | tf_op jit(solution)/shard_map/ppermute | solution.py:853
  15.7 9.4 %copy-start.4 = (s32[1024,18]{0,1:T(8,128)S(1)}, s32[1024,18]{0,1:T(8,128)}, u32[]{:S(2)}) copy-start(s32[1024,18]{0,1:T(8,128)} %param.16) | copy-start | bytes 221188
  20.7 2.7 %collective-permute-start.4 = (bf16[144,1024]{1,0:T(8,128)(2,1)S(1)}, bf16[144,1024]{1,0:T(8,128)(2,1)S(1)}, u32[]{:S(2)}, u32[]{:S(2)}) collective-permute-start(bf16[144,1024]{1,0:T(8,128)(2,1)S(1)} %get-tuple-element.52.own_ref), channel_id=1, source_target_pairs={{0,1},{1,0},{2,3},{3,2},{4,5},{5,4},{6,7},{7,6},{8,9},{9,8},{10,11... | collective-permute-start | bytes 884744 | tf_op jit(solution)/shard_map/ppermute | solution.py:853
  21.4 10.8 %collective-permute-start.7 = (bf16[1024,128]{1,0:T(8,128)(2,1)S(1)}, bf16[1024,128]{1,0:T(8,128)(2,1)S(1)}, u32[]{:S(2)}, u32[]{:S(2)}) collective-permute-start(bf16[1024,128]{1,0:T(8,128)(2,1)S(1)} %get-tuple-element.58.c_ref), channel_id=1, source_target_pairs={{0,2},{2,0},{1,3},{3,1},{4,6},{6,4},{5,7},{7,5},{8,10},{10,8},{9,1... | collective-permute-start | bytes 786440 | tf_op jit(solution)/shard_map/ppermute | solution.py:853
  23.5 8.7 %copy-start.2 = (f32[18]{0:T(128)S(1)}, f32[18]{0:T(128)}, u32[]{:S(2)}) copy-start(f32[18]{0:T(128)} %scale_ref.1) | copy-start | bytes 220
  23.5 5.9 %collective-permute-start.5 = (bf16[144,512]{1,0:T(8,128)(2,1)S(1)}, bf16[144,512]{1,0:T(8,128)(2,1)S(1)}, u32[]{:S(2)}, u32[]{:S(2)}) collective-permute-start(bf16[144,512]{1,0:T(8,128)(2,1)S(1)} %join_runs.2.own_ref), channel_id=1, source_target_pairs={{0,4},{4,0},{8,12},{12,8},{1,5},{5,1},{9,13},{13,9},{2,6},{6,2},{1... | collective-permute-start | bytes 442376 | tf_op jit(solution)/shard_map/ppermute | solution.py:853
  29.4 5.9 %collective-permute-start.8 = (bf16[144,512]{1,0:T(8,128)(2,1)S(1)}, bf16[144,512]{1,0:T(8,128)(2,1)S(1)}, u32[]{:S(2)}, u32[]{:S(2)}) collective-permute-start(bf16[144,512]{1,0:T(8,128)(2,1)S(1)} %collective-permute-done.5.other_ref.refs_0_), channel_id=1, source_target_pairs={{0,1},{1,0},{2,3},{3,2},{4,5},{5,4},{6,7},{7,6},{8,9},{9,8},{10,11... | collective-permute-start | bytes 442376 | tf_op jit(solution)/shard_map/ppermute | solution.py:853
  29.4 9.7 %collective-permute-start.6 = (bf16[128,512]{1,0:T(8,128)(2,1)S(1)}, bf16[128,512]{1,0:T(8,128)(2,1)S(1)}, u32[]{:S(2)}, u32[]{:S(2)}) collective-permute-start(bf16[128,512]{1,0:T(8,128)(2,1)S(1)} %join_runs.3), channel_id=1, source_target_pairs={{0,8},{4,12},{8,0},{12,4},{1,9},{5,13},{9,1},{13,5},{2,10},{6,14},... | collective-permute-start | bytes 393224 | tf_op jit(solution)/shard_map/ppermute | solution.py:853
  35.2 3.9 %copy-start.1 = (f32[1024]{0:T(1024)S(1)}, f32[1024]{0:T(1024)}, u32[]{:S(2)}) copy-start(f32[1024]{0:T(1024)} %param.19) | copy-start | bytes 12292
  39.1 1.3 %collective-permute-start.9 = (bf16[128,512]{1,0:T(8,128)(2,1)S(1)}, bf16[128,512]{1,0:T(8,128)(2,1)S(1)}, u32[]{:S(2)}, u32[]{:S(2)}) collective-permute-start(bf16[128,512]{1,0:T(8,128)(2,1)S(1)} %collective-permute-done.6.message_ref), channel_id=1, source_target_pairs={{0,1},{1,0},{2,3},{3,2},{4,5},{5,4},{6,7},{7,6},{8,9},{9,8},{10,11... | collective-permute-start | bytes 393224 | tf_op jit(solution)/shard_map/ppermute | solution.py:853

commit v5 on v4

--- a/solution.py
+++ b/solution.py
@@ -86,17 +86,33 @@
     return jnp.bitwise_and(jnp.right_shift(shard, level), 1)
 
 
-def edge_kernel(key_ref, value_ref, edge_ref, sems):
+def edge_kernel(
+    split,
+    key_ref,
+    value_ref,
+    query_ref,
+    residual_ref,
+    edge_ref,
+    key_first_ref,
+    value_first_ref,
+    query_first_ref,
+    residual_first_ref,
+    sems,
+):
     row_count = key_ref.shape[0]
     part = WINDOW // 4
+    moves = []
+    for at, ref in enumerate((key_ref, value_ref)):
+        moves += [
+            (ref, row_count - WINDOW + piece * part, edge_ref, at * WINDOW + piece * part, part) for piece in range(4)
+        ]
+    for ref, first_ref in ((key_ref, key_first_ref), (value_ref, value_first_ref)):
+        moves += [(ref, (split - 1 + at) * CHUNK, first_ref, at * CHUNK, CHUNK) for at in range(2)]
+    moves += [(query_ref, split * CHUNK, query_first_ref, 0, CHUNK)]
+    moves += [(residual_ref, split * CHUNK, residual_first_ref, 0, CHUNK)]
     copies = [
-        pltpu.make_async_copy(
-            ref.at[pl.ds(row_count - WINDOW + piece * part, part)],
-            edge_ref.at[pl.ds(at * WINDOW + piece * part, part)],
-            sems.at[at, piece],
-        )
-        for at, ref in enumerate((key_ref, value_ref))
-        for piece in range(4)
+        pltpu.make_async_copy(ref.at[pl.ds(start, rows)], to.at[pl.ds(to_start, rows)], sems.at[at])
+        for at, (ref, start, to, to_start, rows) in enumerate(moves)
     ]
     for copy in copies:
         copy.start()
@@ -104,18 +120,20 @@
         copy.wait()
 
 
-def edge_rows(key_rows, value_rows):
+def edge_rows(split, key_rows, value_rows, query_rows, residual):
     width = key_rows.shape[1]
     return pl.pallas_call(
-        edge_kernel,
-        in_specs=[HBM, HBM],
-        out_specs=VMEM,
-        out_shape=shaped((2 * WINDOW, width), BF16),
-        scratch_shapes=[pltpu.SemaphoreType.DMA((2, 4))],
+        functools.partial(edge_kernel, split),
+        in_specs=[HBM] * 4,
+        out_specs=[VMEM] * 5,
+        out_shape=[shaped((2 * WINDOW, width), BF16)]
+        + [shaped((2 * CHUNK, width), BF16)] * 2
+        + [shaped((CHUNK, width), BF16)] * 2,
+        scratch_shapes=[pltpu.SemaphoreType.DMA((14,))],
         compiler_params=params(),
         cost_estimate=cost(0, 2**20),
         name="edge_rows",
-    )(*far_off(key_rows, value_rows))
+    )(*far_off(key_rows, value_rows, query_rows, residual))
 
 
 def lower_ones():
@@ -195,15 +213,16 @@
 def late_kernel(
     split,
     pos_ref,
-    rate_ref,
     query_ref,
     key_ref,
     value_ref,
     residual_ref,
+    key_first_ref,
+    value_first_ref,
+    query_first_ref,
+    residual_first_ref,
     own_weight_ref,
     other_weight_ref,
-    fall_ref,
-    carry_ref,
     hidden_ref,
     c_ref,
     weight_ref,
@@ -212,17 +231,17 @@
     query_early_ref,
     value_early_ref,
     residual_early_ref,
+    key_buf,
+    value_buf,
     query_buf,
-    value_buf,
     residual_buf,
-    fall,
-    carry,
     sems,
 ):
     row_count, width = query_ref.shape
     chunks = row_count // CHUNK
     half_width = width // 2
     arrays = (
+        (key_ref, key_buf, key_early_ref),
         (value_ref, value_buf, value_early_ref),
         (query_ref, query_buf, query_early_ref),
         (residual_ref, residual_buf, residual_early_ref),
@@ -239,85 +258,90 @@
         rows = chunk_rows(chunk)
         return pltpu.make_async_copy(source.at[rows], early.at[rows], sems.at[which, chunk + chunks - split])
 
-    copy_early(0, split - 1).start()
-    for chunk in range(split, chunks):
-        for which in range(3):
+    for chunk in range(split + 1, chunks):
+        for which in range(4):
             copy(which, chunk).start()
-    for which in range(1, 3):
-        copy_early(which, split - 1).start()
-    for chunk in range(split - 1):
-        for which in range(3):
+    for chunk in range(split):
+        for which in range(4):
             copy_early(which, chunk).start()
+
+    def attend_one(chunk, query, key_before, key, value_before, value, residual):
+        attend_heads(
+            chunk_masks(pos_ref[pl.ds(chunk, 1), :]),
+            width,
+            query,
+            key_before,
+            key,
+            value_before,
+            value,
+            residual,
+            (hidden_ref, chunk_rows(chunk)),
+        )
+
+    whole = chunk_rows(0)
+    attend_one(
+        split,
+        (query_first_ref, whole),
+        (key_first_ref, whole),
+        (key_first_ref, chunk_rows(1)),
+        (value_first_ref, whole),
+        (value_first_ref, chunk_rows(1)),
+        (residual_first_ref, whole),
+    )
+    key_buf[:CHUNK, :] = key_first_ref[CHUNK:, :]
+    value_buf[:CHUNK, :] = value_first_ref[CHUNK:, :]
     is_low = half_index() == 0
     own_weight, other_weight = own_weight_ref[...], other_weight_ref[...]
     weight_ref[:half_width, :] = jnp.where(is_low, own_weight, other_weight)
     weight_ref[half_width:, :] = jnp.where(is_low, other_weight, own_weight)
-    key_early_ref[...] = key_ref[: split * CHUNK, :]
-    fade_wide(rate_ref, fall, carry, fall_ref, carry_ref)
-
-    def attend_one(chunk, value_before):
-        for which in range(3):
+
+    def step(chunk, token):
+        for which in range(4):
             copy(which, chunk).wait()
-        rows = chunk_rows(chunk - split)
-        attend_heads(
-            chunk_masks(pos_ref[pl.ds(chunk, 1), :]),
-            width,
+        rows, before = chunk_rows(chunk - split), chunk_rows(chunk - split - 1)
+        attend_one(
+            chunk,
             (query_buf, rows),
-            (key_ref, chunk_rows(chunk - 1)),
-            (key_ref, chunk_rows(chunk)),
-            value_before,
+            (key_buf, before),
+            (key_buf, rows),
+            (value_buf, before),
             (value_buf, rows),
             (residual_buf, rows),
-            (hidden_ref, chunk_rows(chunk)),
         )
-
-    copy_early(0, split - 1).wait()
-    attend_one(split, (value_early_ref, chunk_rows(split - 1)))
-
-    def step(chunk, token):
-        attend_one(chunk, (value_buf, chunk_rows(chunk - split - 1)))
         return token
 
     lax.fori_loop(split + 1, chunks, step, 0)
     shared = dot(hidden_ref[split * CHUNK :, :], weight_ref[...])
     b_ref[...] = shared[:, :STATES].astype(BF16)
     c_ref[split * CHUNK :, :] = shared[:, STATES:].astype(BF16)
-    for which in range(1, 3):
-        copy_early(which, split - 1).wait()
-    for chunk in range(split - 1):
-        for which in range(3):
+    for chunk in range(split):
+        for which in range(4):
             copy_early(which, chunk).wait()
 
 
-def attend_late(split, positions, rate_turned, query, key, value, residual, weights):
+def attend_late(split, positions, query, key, value, residual, firsts, weights):
     row_count, width = query.shape
     chunks = row_count // CHUNK
     late = row_count - split * CHUNK
     return pl.pallas_call(
         functools.partial(late_kernel, split),
-        in_specs=[VMEM, VMEM, HBM, VMEM, HBM, HBM, VMEM, VMEM],
-        out_specs=[VMEM] * 10,
+        in_specs=[VMEM] + [HBM] * 4 + [VMEM] * 6,
+        out_specs=[VMEM] * 8,
         out_shape=[
-            shaped((row_count, width), BF16),
-            shaped((row_count, width), BF16),
             shaped((row_count, width), BF16),
             shaped((row_count, STATES), BF16),
             shaped((width, 2 * STATES), BF16),
             shaped((late, STATES), BF16),
         ]
         + [shaped((split * CHUNK, width), BF16)] * 4,
-        scratch_shapes=[pltpu.VMEM((late, width), BF16)] * 3
-        + [pltpu.VMEM((row_count, rate_turned.shape[0]), BF16)] * 2
-        + [pltpu.SemaphoreType.DMA((3, chunks))],
+        scratch_shapes=[pltpu.VMEM((late, width), BF16)] * 4 + [pltpu.SemaphoreType.DMA((4, chunks))],
         compiler_params=params(),
         cost_estimate=cost(6 * 10**9, 10**7),
         name="attention_late",
     )(
-        *near_by(positions, rate_turned),
-        *far_off(query),
-        *near_by(key),
-        *far_off(value, residual),
-        *near_by(*weights),
+        *near_by(positions),
+        *far_off(query, key, value, residual),
+        *near_by(*firsts, *weights),
     )
 
 
@@ -388,21 +412,20 @@
     c_ref,
     scaled_ref,
     rows_ref,
-    hidden_far_ref,
+    fall_ref,
+    carry_ref,
     c_far_ref,
     rise,
+    fall,
+    carry,
     logs,
     sems,
 ):
     heads, row_count = rate_ref.shape
     width = hidden_ref.shape[1]
     chunks = row_count // CHUNK
-    copies = [pltpu.make_async_copy(c_ref, c_far_ref, sems.at[chunks])]
-    for chunk in range(chunks):
-        rows = pl.ds(chunk * CHUNK, CHUNK)
-        copies.append(pltpu.make_async_copy(hidden_ref.at[rows], hidden_far_ref.at[rows], sems.at[chunk]))
-    for copy in copies:
-        copy.start()
+    copy = pltpu.make_async_copy(c_ref, c_far_ref, sems.at[0])
+    copy.start()
     spread = spread_matrix(heads, width)
     lower = lower_ones()
     row_idx = lax.broadcasted_iota(jnp.int32, (8, heads), 0)
@@ -422,8 +445,8 @@
         wide = dot(rise[...], spread[:, lanes])
         scaled_ref[:, lanes] = (wide * hidden_ref[:, lanes].astype(F32)).astype(BF16)
         rows_ref[:, lanes] = dot(high, spread[:, lanes]) + dot(low, spread[:, lanes])
-    for copy in copies:
-        copy.wait()
+    fade_wide(rate_ref, fall, carry, fall_ref, carry_ref)
+    copy.wait()
 
 
 def scale_hidden(rate_turned, hidden, c_mat):
@@ -433,15 +456,16 @@
     return pl.pallas_call(
         scale_kernel,
         in_specs=[VMEM] * 3,
-        out_specs=[VMEM] * 2 + [HBM] * 2,
+        out_specs=[VMEM] * 4 + [HBM],
         out_shape=[
             shaped((row_count, width), BF16),
             shaped((chunks * 8, width), F32),
-            far_shaped(hidden.shape, BF16),
+            shaped((row_count, width), BF16),
+            shaped((row_count, width), BF16),
             far_shaped(c_mat.shape, BF16),
         ],
-        scratch_shapes=[pltpu.VMEM((row_count, heads), BF16)]
-        + [pltpu.VMEM((chunks * 8, heads), F32), pltpu.SemaphoreType.DMA((chunks + 1,))],
+        scratch_shapes=[pltpu.VMEM((row_count, heads), BF16)] * 3
+        + [pltpu.VMEM((chunks * 8, heads), F32), pltpu.SemaphoreType.DMA((1,))],
         compiler_params=params(),
         cost_estimate=cost(10**9, 4 * 10**6),
         name="scale_hidden",
@@ -545,11 +569,28 @@
     )(*near_by(own, other))
 
 
-def runs_kernel(local_levels, turned_far_ref, codes_ref, scaled_ref, rows_ref, wide_ref, runs_ref, turned, sems):
+def runs_kernel(
+    local_levels,
+    turned_far_ref,
+    codes_ref,
+    hidden_ref,
+    scaled_ref,
+    rows_ref,
+    wide_ref,
+    runs_ref,
+    hidden_far_ref,
+    turned,
+    sems,
+):
     row_count, width = scaled_ref.shape
     chunks = row_count // CHUNK
-    turned_copy = pltpu.make_async_copy(turned_far_ref, turned, sems.at[0])
+    turned_copy = pltpu.make_async_copy(turned_far_ref, turned, sems.at[chunks])
     turned_copy.start()
+    copies = []
+    for chunk in range(chunks):
+        rows = pl.ds(chunk * CHUNK, CHUNK)
+        copies.append(pltpu.make_async_copy(hidden_ref.at[rows], hidden_far_ref.at[rows], sems.at[chunk]))
+        copies[-1].start()
     codes = codes_ref[...].astype(F32).T.astype(BF16)
     levels = codes.shape[1]
     pair = 2 * CHUNK
@@ -587,9 +628,11 @@
         return token
 
     lax.fori_loop(0, width // tile, step, 0)
-
-
-def codes_and_runs(turned_far, codes_turned, scaled, factor_rows):
+    for copy in copies:
+        copy.wait()
+
+
+def codes_and_runs(turned_far, codes_turned, hidden, scaled, factor_rows):
     row_count, width = scaled.shape
     levels = codes_turned.shape[0]
     levels += levels % 2
@@ -597,17 +640,18 @@
     local_levels = chunks.bit_length() - 1
     return pl.pallas_call(
         functools.partial(runs_kernel, local_levels),
-        in_specs=[HBM] + [VMEM] * 3,
-        out_specs=[VMEM] * 2,
+        in_specs=[HBM] + [VMEM] * 4,
+        out_specs=[VMEM, VMEM, HBM],
         out_shape=[
             shaped((row_count, levels * CHUNK), BF16),
             shaped((chunks * local_levels * STATES, width), BF16),
+            far_shaped(hidden.shape, BF16),
         ],
-        scratch_shapes=[pltpu.VMEM((STATES, row_count), BF16), pltpu.SemaphoreType.DMA((1,))],
+        scratch_shapes=[pltpu.VMEM((STATES, row_count), BF16), pltpu.SemaphoreType.DMA((chunks + 1,))],
         compiler_params=params(),
         cost_estimate=cost(10**9, 10**7),
         name="codes_and_runs",
-    )(*far_off(turned_far), *near_by(codes_turned, scaled, factor_rows))
+    )(*far_off(turned_far), *near_by(codes_turned, hidden, scaled, factor_rows))
 
 
 def weights_kernel(
@@ -644,7 +688,7 @@
         rows = chunk_rows(chunk)
 
         def lam_of(level):
-            return codes_ref[rows, level * CHUNK : (level + 1) * CHUNK].astype(F32) * scale_ref[level]
+            return codes_ref[rows, level * CHUNK : (level + 1) * CHUNK].astype(F32) * scale_ref[0:1, level : level + 1]
 
         c_wide = (c_buf[rows, :].astype(F32) + c_other_ref[rows, :].astype(F32)).astype(BF16).astype(F32)
         gram = dot(c_wide.astype(BF16), turned[:, rows])
@@ -671,7 +715,7 @@
     local_levels = (row_count // CHUNK).bit_length() - 1
     return pl.pallas_call(
         functools.partial(weights_kernel, local_levels, cross_levels),
-        in_specs=[SMEM] + [HBM] * 2 + [VMEM] * 2,
+        in_specs=[VMEM] + [HBM] * 2 + [VMEM] * 2,
         out_specs=[VMEM] * 3,
         out_shape=[
             shaped((row_count, (1 + local_levels) * STATES), BF16),
@@ -686,7 +730,7 @@
         compiler_params=params(),
         cost_estimate=cost(10**9, 10**7),
         name="level_products",
-    )(scale, *far_off(turned_far, c_far), *near_by(c_other, codes_wide))
+    )(*near_by(scale), *far_off(turned_far, c_far), *near_by(c_other, codes_wide))
 
 
 def carried_state(message, before, upper):
@@ -853,6 +897,11 @@
     return lax.ppermute(x, axis, [(i, i ^ 1 << distance) for i in range(lax.axis_size(axis))])
 
 
+def mirrored(x):
+    length = lax.axis_size("seq")
+    return lax.ppermute(x, "seq", [(i, length - 1 - i) for i in range(length)])
+
+
 def summed_over_heads(share):
     rounds = lax.axis_size("head").bit_length() - 1
     if rounds == 0:
@@ -881,17 +930,18 @@
     cross_levels = lax.axis_size(shard_axes).bit_length() - 1
 
     weights = (bc_weight, partner(bc_weight, "fsdp", 0))
-    edges = from_behind(edge_rows(key_rows, value_rows), shard_axes, 1)
+    split = max(1, row_count // CHUNK // 4)
+    edge, *firsts = edge_rows(split, key_rows, value_rows, query_rows, residual_in)
+    edges = from_behind(edge, shard_axes, 1)
     pos_rows = positions.reshape(row_count // CHUNK, CHUNK)
-    split = max(1, row_count // CHUNK // 4)
     rate_turned = decay_rate.T
-    fall, carry, hidden, c_mat, weight, b_late, *parts = attend_late(
-        split, pos_rows, rate_turned, query_rows, key_rows, value_rows, residual_in, weights
+    hidden, c_mat, weight, b_late, *parts = attend_late(
+        split, pos_rows, query_rows, key_rows, value_rows, residual_in, firsts, weights
     )
     late_own, late_other = summed_over_heads(b_late)
     hidden, c_mat, b_early = attend_early(split, pos_rows, edges, parts, weight, hidden, c_mat)
     early_own, early_other = summed_over_heads(b_early)
-    scaled, factor_rows, hidden_far, c_far = scale_hidden(rate_turned, hidden, c_mat)
+    scaled, factor_rows, fall, carry, c_far = scale_hidden(rate_turned, hidden, c_mat)
     c_mat, scaled = lax.optimization_barrier((c_mat, scaled))
     c_sent, c_other = summed_over_heads(c_mat)
     if lax.axis_size("head") > 2:
@@ -903,16 +953,18 @@
     joined = join(0, state, near, half_width, cross_levels == 2)
     received, swapped = [], []
     for level in range(1, cross_levels):
-        other = partner(joined, "seq", level - 1)
+        other = mirrored(joined) if level == cross_levels - 1 else partner(joined, "seq", level - 1)
         if level == 1:
-            codes_wide, runs = codes_and_runs(turned_far, level_codes.T, scaled, factor_rows)
+            codes_wide, runs, hidden_far = codes_and_runs(
+                turned_far, level_codes.T, hidden, scaled, factor_rows
+            )
             other, codes_wide = lax.optimization_barrier((other, codes_wide))
         received.append(other)
         if level < cross_levels - 1:
             joined = join(level, joined, other, half_width, level == cross_levels - 2)
             swapped.append(partner(other, "fsdp", 0))
     left, early_reads, last_reads = level_products(
-        level_scale, turned_far, c_far, c_other, codes_wide, cross_levels
+        level_scale[None, :], turned_far, c_far, c_other, codes_wide, cross_levels
     )
     local, hidden, before = local_terms(
         hidden_far, left, early_reads, scaled, fall, carry, runs, near, received[:-1], swapped

time: 42.4 us -> 41.6 us (0.981)
  waiting for transfers between devices: 5.63 us -> 4.25 us
    ppermute x0 -> x1, starting transfers between devices: none -> 2.83 us  [mirrored(): return lax.ppermute(x, 'seq', [(i, length - 1 - i) for i in range(length)])]
    ppermute x9 -> x8, starting transfers between devices: 10.6 us -> 8.06 us  [partner(): lax.ppermute(x, axis, [(i, i ^ 1 << distance) for i in range(lax.axis_siz...]
    ppermute x9 -> x8, waiting for transfers between devices: 5.63 us -> 4.24 us  [partner(): lax.ppermute(x, axis, [(i, i ^ 1 << distance) for i in range(lax.axis_siz...]
    pallas_call x3, Pallas kernels: 8.98 us -> 9.6 us  [the longest x1 5.46 us: attend_late(): pl.pallas_call(functools.partial(late_kernel, split), in_specs=[VMEM] + [...]
    pallas_call x1, Pallas kernels: 3.07 us -> 2.62 us  [level_products(): pl.pallas_call(functools.partial(weights_kernel, local_levels, cross_leve...]
  transfers between devices with their start and end apart: 10 -> 10, of which waited for: 5 -> 4; matrix products, arithmetic and copies ran while one was open for 0% -> 0% of each run, Pallas kernels for 49% -> 51%
where the time goes in v5:
time: 41.6 us; the launch traced here: 41.5 us
  Pallas kernels  24.1 us (58%)
  starting transfers between devices  12.9 us (31%)
  waiting for transfers between devices  4.25 us (10%)
    ppermute x8, starting transfers between devices, partner(): lax.ppermute(x, axis, [(i, i ^ 1 << distance) for i in range(lax.axis_siz...  8.06 us
    pallas_call x1, Pallas kernels, attend_late(): pl.pallas_call(functools.partial(late_kernel, split), in_specs=[VMEM] + [...  5.46 us
    ppermute x8, waiting for transfers between devices, partner(): lax.ppermute(x, axis, [(i, i ^ 1 << distance) for i in range(lax.axis_siz...  4.24 us
    pallas_call x1, Pallas kernels, local_terms(): pl.pallas_call(functools.partial(local_kernel, local_levels, cross_levels...  3.5 us
    pallas_call x1, Pallas kernels, codes_and_runs(): pl.pallas_call(functools.partial(runs_kernel, local_levels), in_specs=[HB...  3.1 us
    ppermute x1, starting transfers between devices, mirrored(): return lax.ppermute(x, 'seq', [(i, length - 1 - i) for i in range(length)])  2.83 us
    pallas_call x1, Pallas kernels, level_products(): pl.pallas_call(functools.partial(weights_kernel, local_levels, cross_leve...  2.62 us
    pallas_call x2, Pallas kernels, finish(): pl.pallas_call(functools.partial(finish_kernel, swap, cross_levels), in_s...  2.55 us
  transfers between devices with their start and end apart: 10, of which 4 were waited for; matrix products, arithmetic and copies ran while one was open for 0% of the time, Pallas kernels for 51%

profile of v5, /device:TPU:0, one launch (start us, length us, event | category | flops | bytes accessed | tf_op | source)
XLA Modules:
  0.0 41.5 jit_solution(8756992945945802782)
XLA Ops:
  0.0 0.0 copy-start.3
  0.0 0.0 copy-start.5
  0.0 0.5 %collective-permute-start.1 = (bf16[512,256]{1,0:T(8,128)(2,1)}, bf16[512,256]{1,0:T(8,128)(2,1)S(1)}, u32[]{:S(2)}, u32[]{:S(2)}) collective-permute-start(bf16[512,256]{1,0:T(8,128)(2,1)} %own_weight_ref.1), channel_id=1, source_target_pairs={{0,1},{1,0},{2,3},{3,2},{4,5},{5,4},{6,7},{7,6},{8,9},{9,8},{10,11... | collective-permute-start | bytes 786440 | tf_op jit(solution)/shard_map/ppermute | solution.py:897
  0.5 1.7 %edge_rows.1 = (bf16[256,1024]{1,0:T(8,128)(2,1)S(1)}, bf16[256,1024]{1,0:T(8,128)(2,1)S(1)}, bf16[256,1024]{1,0:T(8,128)(2,1)S(1)}, bf16[128,1024]{1,0:T(8,128)(2,1)S(1)}, bf16[128,1024]{1,0:T(8,128)(2,1)S(1)}) custom-call(bf16[1024,1024]{1,0:T(8,128)(2,1)} %key_ref.3, bf16[1024,1024]{1,0:T(8,128)(2,1)} %value_ref.3, bf16[1024,1024]{1,0:T(8,128)(2,1)} %query_ref.3, ...), custom_call_target="tpu_custom_call" | custom-call | bytes 1048576 | tf_op jit(solution)/shard_map/edge_rows/pallas_call | solution.py:125
  2.2 2.0 %collective-permute-start = (bf16[256,1024]{1,0:T(8,128)(2,1)S(1)}, bf16[256,1024]{1,0:T(8,128)(2,1)S(1)}, u32[]{:S(2)}, u32[]{:S(2)}) collective-permute-start(bf16[256,1024]{1,0:T(8,128)(2,1)S(1)} %get-tuple-element.43), channel_id=1, source_target_pairs={{0,1},{1,4},{4,5},{5,8},{8,9},{9,12},{12,13},{2,3},{3,6},{6,7},{7,... | collective-permute-start | bytes 1572872 | tf_op jit(solution)/shard_map/ppermute | solution.py:893
  4.2 0.0 collective-permute-done.1.other_weight_ref
  4.2 0.0 copy-done.3
  4.2 0.0 copy-done.5
  4.3 5.5 %attention_late.1 = (bf16[1024,1024]{1,0:T(8,128)(2,1)S(1)}, bf16[1024,128]{1,0:T(8,128)(2,1)S(1)}, bf16[1024,256]{1,0:T(8,128)(2,1)S(1)}, bf16[768,128]{1,0:T(8...) custom-call(s32[8,128]{1,0:T(8,128)S(1)} %bitcast.10, ...), custom_call_target="tpu_custom_call" | custom-call | flops 6000000000 | bytes 10000000 | tf_op jit(solution)/shard_map/attention_late/pallas_call | solution.py:326
  9.7 3.0 %collective-permute-start.3 = (bf16[768,128]{1,0:T(8,128)(2,1)S(1)}, bf16[768,128]{1,0:T(8,128)(2,1)S(1)}, u32[]{:S(2)}, u32[]{:S(2)}) collective-permute-start(bf16[768,128]{1,0:T(8,128)(2,1)S(1)} %get-tuple-element.56.late_own_ref), channel_id=1, source_target_pairs={{0,2},{2,0},{1,3},{3,1},{4,6},{6,4},{5,7},{7,5},{8,10},{10,8},{9,1... | collective-permute-start | bytes 589832 | tf_op jit(solution)/shard_map/ppermute | solution.py:897
  12.7 0.0 collective-permute-done.edge_ref
  12.7 0.0 copy-start.4
  12.7 1.2 %attention_early.1 = (bf16[1024,1024]{1,0:T(8,128)(2,1)S(1)}, bf16[1024,128]{1,0:T(8,128)(2,1)S(1)}, bf16[256,128]{1,0:T(8,128)(2,1)S(1)}) custom-call(s32[8,128]{1,0:T(8,128)S(1)} %bitcast.11, bf16[256,1024]{1,0:T(8,128)(2,1)S(1)} %collective-permute-done.edge_ref, ...), custom_call_target="tpu_custom_call", output_to_operand_aliasing={{0}: (7, {}), {1}: (8, {})} | custom-call | flops 2000000000 | bytes 2000000 | tf_op jit(solution)/shard_map/attention_early/pallas_call | solution.py:393
  13.9 0.1 collective-permute-start.2
  14.0 0.0 copy-done.4
  14.0 2.4 %scale_hidden.1 = (bf16[1024,1024]{1,0:T(8,128)(2,1)S(1)}, f32[64,1024]{1,0:T(8,128)S(1)}, bf16[1024,1024]{1,0:T(8,128)(2,1)S(1)}, bf16[1024,1024]{1,0:T(8,128)(2,1)S(1)}, bf16[1024,128]{1,0:T(8,128)(2,1)}) custom-call(f32[16,1024]{1,0:T(8,128)S(1)} %bitcast.9, bf16[1024,1024]{1,0:T(8,128)(2,1)S(1)} %get-tuple-element.58.hidden_ref, ...), custom_call_target="tpu_custom_call" | custom-call | flops 1000000000 | bytes 4000000 | tf_op jit(solution)/shard_map/scale_hidden/pallas_call | solution.py:456
  16.5 0.0 copy-start
  16.5 1.3 %collective-permute-done.3.late_other_ref = bf16[768,128]{1,0:T(8,128)(2,1)S(1)} collective-permute-done((bf16[768,128]{1,0:T(8,128)(2,1)S(1)}, bf16[768,128]{1,0:T(8,128)(2,1)S(1)}, u32[]{:S(2)}, u32[]{:S(2)}) %collective-permute-start.3) | collective-permute-done | bytes 196640 | tf_op jit(solution)/shard_map/ppermute | solution.py:897
  17.8 1.4 %collective-permute-done.2.early_other_ref = bf16[256,128]{1,0:T(8,128)(2,1)S(1)} collective-permute-done((bf16[256,128]{1,0:T(8,128)(2,1)S(1)}, bf16[256,128]{1,0:T(8,128)(2,1)S(1)}, u32[]{:S(2)}, u32[]{:S(2)}) %collective-permute-start.2) | collective-permute-done | bytes 65568 | tf_op jit(solution)/shard_map/ppermute | solution.py:897
  19.2 1.4 %block_state.1 = (bf16[144,1024]{1,0:T(8,128)(2,1)S(1)}, bf16[128,1024]{1,0:T(8,128)(2,1)}) custom-call(bf16[256,128]{1,0:T(8,128)(2,1)S(1)} %get-tuple-element.55.early_own_ref, bf16[256,128]{1,0:T(8,128)(2,1)S(1)} %collective-permute-done.2.early_other_ref, bf16[768,128]{1,0:T(8,128)(2,1)S(1)} %get-tuple-element.56.late_own_ref, ...), custom_call_target="tpu_custom_call" | custom-call | flops 300000000 | bytes 4000000 | tf_op jit(solution)/shard_map/block_state/pallas_call | solution.py:532
  20.6 0.6 %collective-permute-start.4 = (bf16[144,1024]{1,0:T(8,128)(2,1)S(1)}, bf16[144,1024]{1,0:T(8,128)(2,1)S(1)}, u32[]{:S(2)}, u32[]{:S(2)}) collective-permute-start(bf16[144,1024]{1,0:T(8,128)(2,1)S(1)} %get-tuple-element.62.own_ref), channel_id=1, source_target_pairs={{0,1},{1,0},{2,3},{3,2},{4,5},{5,4},{6,7},{7,6},{8,9},{9,8},{10,11... | collective-permute-start | bytes 884744 | tf_op jit(solution)/shard_map/ppermute | solution.py:897
  21.1 2.1 %collective-permute-start.7 = (bf16[1024,128]{1,0:T(8,128)(2,1)S(1)}, bf16[1024,128]{1,0:T(8,128)(2,1)S(1)}, u32[]{:S(2)}, u32[]{:S(2)}) collective-permute-start(bf16[1024,128]{1,0:T(8,128)(2,1)S(1)} %get-tuple-element.68.c_ref), channel_id=1, source_target_pairs={{0,2},{2,0},{1,3},{3,1},{4,6},{6,4},{5,7},{7,5},{8,10},{10,8},{9,1... | collective-permute-start | bytes 786440 | tf_op jit(solution)/shard_map/ppermute | solution.py:897
  23.3 0.0 collective-permute-done.4.other_ref.near_ref
  23.3 0.1 join_runs.2.own_ref
  23.3 1.5 %collective-permute-start.5 = (bf16[144,512]{1,0:T(8,128)(2,1)S(1)}, bf16[144,512]{1,0:T(8,128)(2,1)S(1)}, u32[]{:S(2)}, u32[]{:S(2)}) collective-permute-start(bf16[144,512]{1,0:T(8,128)(2,1)S(1)} %join_runs.2.own_ref), channel_id=1, source_target_pairs={{0,4},{4,0},{8,12},{12,8},{1,5},{5,1},{9,13},{13,9},{2,6},{6,2},{1... | collective-permute-start | bytes 442376 | tf_op jit(solution)/shard_map/ppermute | solution.py:897
  24.9 0.0 copy-done
  24.9 0.0 copy-start.2
  24.9 3.1 %codes_and_runs.1 = (bf16[1024,2304]{1,0:T(8,128)(2,1)S(1)}, bf16[3072,1024]{1,0:T(8,128)(2,1)S(1)}, bf16[1024,1024]{1,0:T(8,128)(2,1)}) custom-call(bf16[128,1024]{1,0:T(8,128)(2,1)} %get-tuple-element.63.turned_far_ref, s32[18,1024]{1,0:T(8,128)S(1)} %bitcast.5, bf16[1024,1024]{1,0:T(8,128)(2,1)S(1)} %get-tuple-element.58.hidden_ref, ...), custom_call_target="tpu_custom_call" | custom-call | flops 1000000000 | bytes 10000000 | tf_op jit(solution)/shard_map/codes_and_runs/pallas_call | solution.py:641
  28.0 1.2 %collective-permute-done.5.other_ref.refs_0_ = bf16[144,512]{1,0:T(8,128)(2,1)S(1)} collective-permute-done((bf16[144,512]{1,0:T(8,128)(2,1)S(1)}, bf16[144,512]{1,0:T(8,128)(2,1)S(1)}, u32[]{:S(2)}, u32[]{:S(2)}) %collective-permute-start.5) | collective-permute-done | bytes 147488 | tf_op jit(solution)/shard_map/ppermute | solution.py:897
  29.2 0.0 collective-permute-start.8
  29.2 0.1 join_runs.3
  29.3 2.8 %collective-permute-start.6 = (bf16[128,512]{1,0:T(8,128)(2,1)S(1)}, bf16[128,512]{1,0:T(8,128)(2,1)S(1)}, u32[]{:S(2)}, u32[]{:S(2)}) collective-permute-start(bf16[128,512]{1,0:T(8,128)(2,1)S(1)} %join_runs.3), channel_id=1, source_target_pairs={{0,12},{4,8},{8,4},{12,0},{1,13},{5,9},{9,5},{13,1},{2,14},{6,10},... | collective-permute-start | bytes 393224 | tf_op jit(solution)/shard_map/ppermute | solution.py:902
  32.1 0.0 collective-permute-done.7.c_other_ref
  32.1 0.0 copy-done.2
  32.1 2.6 %level_products.1 = (bf16[1024,512]{1,0:T(8,128)(2,1)S(1)}, bf16[1024,256]{1,0:T(8,128)(2,1)S(1)}, bf16[1024,128]{1,0:T(8,128)(2,1)S(1)}) custom-call(f32[1,18]{1,0:T(1,128)S(1)} %bitcast.8, bf16[128,1024]{1,0:T(8,128)(2,1)} %get-tuple-element.63.turned_far_ref, bf16[1024,128]{1,0:T(8,128)(2,1)} %get-tuple-element.67.c_far_ref, ...), custom_call_target="tpu_custom_call" | custom-call | flops 1000000000 | bytes 10000000 | tf_op jit(solution)/shard_map/level_products/pallas_call | solution.py:716
  34.8 0.0 collective-permute-done.8.refs_1_
  34.8 0.0 copy-start.1
  34.8 3.5 %local_terms.1 = (bf16[1024,1024]{1,0:T(8,128)(2,1)S(1)}, bf16[1024,1024]{1,0:T(8,128)(2,1)S(1)}, f32[8,1024]{1,0:T(8,128)S(1)}) custom-call(bf16[1024,1024]{1,0:T(8,128)(2,1)} %get-tuple-element.66.hidden_far_ref, bf16[1024,512]{1,0:T(8,128)(2,1)S(1)} %get-tuple-element.70.left_ref, bf16[1024,256]{1,0:T(8,128)(2,1)S(1)} %get-tuple-element.71.early_reads_ref, ...), custom_call_target="tpu_custom_call" | custom-call | flops 3000000000 | bytes 10000000 | tf_op jit(solution)/shard_map/local_terms/pallas_call | solution.py:806
  38.3 0.0 collective-permute-done.6.message_ref
  38.3 0.3 collective-permute-start.9
  38.6 0.0 copy-done.1
  38.6 0.8 %carried_and_norm.2.refs_0_ = bf16[1024,512]{1,0:T(8,128)(2,1)S(1)} custom-call(bf16[128,512]{1,0:T(8,128)(2,1)S(1)} %collective-permute-done.6.message_ref, f32[8,1024]{1,0:T(8,128)S(1)} %get-tuple-element.77.before_ref, bf16[1024,1024]{1,0:T(8,128)(2,1)S(1)} %get-tuple-element.78.hidden_ref, bf16[1024,128]{1,0:T(8,128)(2,1)S(1)} %get-tuple-element.79.reads_ref, ...), custom_call_target="tpu_custom_call" | custom-call | flops 2000000000 | bytes 8000000 | tf_op jit(solution)/shard_map/carried_and_norm/pallas_call | solution.py:874
  39.4 0.3 collective-permute-done.9.message_ref
  39.7 1.7 %carried_and_norm.3 = bf16[1024,1024]{1,0:T(8,128)(2,1)} custom-call(bf16[128,512]{1,0:T(8,128)(2,1)S(1)} %collective-permute-done.9.message_ref, f32[8,1024]{1,0:T(8,128)S(1)} %get-tuple-element.77.before_ref, bf16[1024,1024]{1,0:T(8,128)(2,1)S(1)} %get-tuple-element.78.hidden_ref, bf16[1024,128]{1,0:T(8,128)(2,1)S(1)} %get-tuple-element.79.reads_ref, ...), custom_call_target="tpu_custom_call" | custom-call | flops 2000000000 | bytes 8000000 | tf_op jit(solution)/shard_map/carried_and_norm/pallas_call | solution.py:874
Async XLA Ops:
  0.0 4.2 %copy-start.3 = (bf16[512,256]{1,0:T(8,128)(2,1)S(1)}, bf16[512,256]{1,0:T(8,128)(2,1)}, u32[]{:S(2)}) copy-start(bf16[512,256]{1,0:T(8,128)(2,1)} %own_weight_ref.1) | copy-start | bytes 786436
  0.0 4.2 %copy-start.5 = (s32[1024]{0:T(1024)S(1)}, s32[1024]{0:T(1024)}, u32[]{:S(2)}) copy-start(s32[1024]{0:T(1024)} %param.18) | copy-start | bytes 12292
  0.0 4.2 %collective-permute-start.1 = (bf16[512,256]{1,0:T(8,128)(2,1)}, bf16[512,256]{1,0:T(8,128)(2,1)S(1)}, u32[]{:S(2)}, u32[]{:S(2)}) collective-permute-start(bf16[512,256]{1,0:T(8,128)(2,1)} %own_weight_ref.1), channel_id=1, source_target_pairs={{0,1},{1,0},{2,3},{3,2},{4,5},{5,4},{6,7},{7,6},{8,9},{9,8},{10,11... | collective-permute-start | bytes 786440 | tf_op jit(solution)/shard_map/ppermute | solution.py:897
  2.2 10.5 %collective-permute-start = (bf16[256,1024]{1,0:T(8,128)(2,1)S(1)}, bf16[256,1024]{1,0:T(8,128)(2,1)S(1)}, u32[]{:S(2)}, u32[]{:S(2)}) collective-permute-start(bf16[256,1024]{1,0:T(8,128)(2,1)S(1)} %get-tuple-element.43), channel_id=1, source_target_pairs={{0,1},{1,4},{4,5},{5,8},{8,9},{9,12},{12,13},{2,3},{3,6},{6,7},{7,... | collective-permute-start | bytes 1572872 | tf_op jit(solution)/shard_map/ppermute | solution.py:893
  9.7 8.0 %collective-permute-start.3 = (bf16[768,128]{1,0:T(8,128)(2,1)S(1)}, bf16[768,128]{1,0:T(8,128)(2,1)S(1)}, u32[]{:S(2)}, u32[]{:S(2)}) collective-permute-start(bf16[768,128]{1,0:T(8,128)(2,1)S(1)} %get-tuple-element.56.late_own_ref), channel_id=1, source_target_pairs={{0,2},{2,0},{1,3},{3,1},{4,6},{6,4},{5,7},{7,5},{8,10},{10,8},{9,1... | collective-permute-start | bytes 589832 | tf_op jit(solution)/shard_map/ppermute | solution.py:897
  12.7 1.3 %copy-start.4 = (f32[1024,16]{0,1:T(8,128)S(1)}, f32[1024,16]{0,1:T(8,128)}, u32[]{:S(2)}) copy-start(f32[1024,16]{0,1:T(8,128)} %param.15) | copy-start | bytes 196612
  13.9 5.2 %collective-permute-start.2 = (bf16[256,128]{1,0:T(8,128)(2,1)S(1)}, bf16[256,128]{1,0:T(8,128)(2,1)S(1)}, u32[]{:S(2)}, u32[]{:S(2)}) collective-permute-start(bf16[256,128]{1,0:T(8,128)(2,1)S(1)} %get-tuple-element.55.early_own_ref), channel_id=1, source_target_pairs={{0,2},{2,0},{1,3},{3,1},{4,6},{6,4},{5,7},{7,5},{8,10},{10,8},{9,1... | collective-permute-start | bytes 196616 | tf_op jit(solution)/shard_map/ppermute | solution.py:897
  16.5 8.4 %copy-start = (s32[1024,18]{0,1:T(8,128)S(1)}, s32[1024,18]{0,1:T(8,128)}, u32[]{:S(2)}) copy-start(s32[1024,18]{0,1:T(8,128)} %param.16) | copy-start | bytes 221188
  20.6 2.7 %collective-permute-start.4 = (bf16[144,1024]{1,0:T(8,128)(2,1)S(1)}, bf16[144,1024]{1,0:T(8,128)(2,1)S(1)}, u32[]{:S(2)}, u32[]{:S(2)}) collective-permute-start(bf16[144,1024]{1,0:T(8,128)(2,1)S(1)} %get-tuple-element.62.own_ref), channel_id=1, source_target_pairs={{0,1},{1,0},{2,3},{3,2},{4,5},{5,4},{6,7},{7,6},{8,9},{9,8},{10,11... | collective-permute-start | bytes 884744 | tf_op jit(solution)/shard_map/ppermute | solution.py:897
  21.1 11.0 %collective-permute-start.7 = (bf16[1024,128]{1,0:T(8,128)(2,1)S(1)}, bf16[1024,128]{1,0:T(8,128)(2,1)S(1)}, u32[]{:S(2)}, u32[]{:S(2)}) collective-permute-start(bf16[1024,128]{1,0:T(8,128)(2,1)S(1)} %get-tuple-element.68.c_ref), channel_id=1, source_target_pairs={{0,2},{2,0},{1,3},{3,1},{4,6},{6,4},{5,7},{7,5},{8,10},{10,8},{9,1... | collective-permute-start | bytes 786440 | tf_op jit(solution)/shard_map/ppermute | solution.py:897
  23.3 5.9 %collective-permute-start.5 = (bf16[144,512]{1,0:T(8,128)(2,1)S(1)}, bf16[144,512]{1,0:T(8,128)(2,1)S(1)}, u32[]{:S(2)}, u32[]{:S(2)}) collective-permute-start(bf16[144,512]{1,0:T(8,128)(2,1)S(1)} %join_runs.2.own_ref), channel_id=1, source_target_pairs={{0,4},{4,0},{8,12},{12,8},{1,5},{5,1},{9,13},{13,9},{2,6},{6,2},{1... | collective-permute-start | bytes 442376 | tf_op jit(solution)/shard_map/ppermute | solution.py:897
  24.9 7.2 %copy-start.2 = (f32[18]{0:T(128)S(1)}, f32[18]{0:T(128)}, u32[]{:S(2)}) copy-start(f32[18]{0:T(128)} %param.17) | copy-start | bytes 220
  29.2 5.5 %collective-permute-start.8 = (bf16[144,512]{1,0:T(8,128)(2,1)S(1)}, bf16[144,512]{1,0:T(8,128)(2,1)S(1)}, u32[]{:S(2)}, u32[]{:S(2)}) collective-permute-start(bf16[144,512]{1,0:T(8,128)(2,1)S(1)} %collective-permute-done.5.other_ref.refs_0_), channel_id=1, source_target_pairs={{0,1},{1,0},{2,3},{3,2},{4,5},{5,4},{6,7},{7,6},{8,9},{9,8},{10,11... | collective-permute-start | bytes 442376 | tf_op jit(solution)/shard_map/ppermute | solution.py:897
  29.3 9.0 %collective-permute-start.6 = (bf16[128,512]{1,0:T(8,128)(2,1)S(1)}, bf16[128,512]{1,0:T(8,128)(2,1)S(1)}, u32[]{:S(2)}, u32[]{:S(2)}) collective-permute-start(bf16[128,512]{1,0:T(8,128)(2,1)S(1)} %join_runs.3), channel_id=1, source_target_pairs={{0,12},{4,8},{8,4},{12,0},{1,13},{5,9},{9,5},{13,1},{2,14},{6,10},... | collective-permute-start | bytes 393224 | tf_op jit(solution)/shard_map/ppermute | solution.py:902
  34.8 3.8 %copy-start.1 = (f32[1024]{0:T(1024)S(1)}, f32[1024]{0:T(1024)}, u32[]{:S(2)}) copy-start(f32[1024]{0:T(1024)} %param.19) | copy-start | bytes 12292
  38.3 1.4 %collective-permute-start.9 = (bf16[128,512]{1,0:T(8,128)(2,1)S(1)}, bf16[128,512]{1,0:T(8,128)(2,1)S(1)}, u32[]{:S(2)}, u32[]{:S(2)}) collective-permute-start(bf16[128,512]{1,0:T(8,128)(2,1)S(1)} %collective-permute-done.6.message_ref), channel_id=1, source_target_pairs={{0,1},{1,0},{2,3},{3,2},{4,5},{5,4},{6,7},{7,6},{8,9},{9,8},{10,11... | collective-permute-start | bytes 393224 | tf_op jit(solution)/shard_map/ppermute | solution.py:897

commit v6 on v5

--- a/solution.py
+++ b/solution.py
@@ -86,33 +86,17 @@
     return jnp.bitwise_and(jnp.right_shift(shard, level), 1)
 
 
-def edge_kernel(
-    split,
-    key_ref,
-    value_ref,
-    query_ref,
-    residual_ref,
-    edge_ref,
-    key_first_ref,
-    value_first_ref,
-    query_first_ref,
-    residual_first_ref,
-    sems,
-):
+def edge_kernel(key_ref, value_ref, edge_ref, sems):
     row_count = key_ref.shape[0]
     part = WINDOW // 4
-    moves = []
-    for at, ref in enumerate((key_ref, value_ref)):
-        moves += [
-            (ref, row_count - WINDOW + piece * part, edge_ref, at * WINDOW + piece * part, part) for piece in range(4)
-        ]
-    for ref, first_ref in ((key_ref, key_first_ref), (value_ref, value_first_ref)):
-        moves += [(ref, (split - 1 + at) * CHUNK, first_ref, at * CHUNK, CHUNK) for at in range(2)]
-    moves += [(query_ref, split * CHUNK, query_first_ref, 0, CHUNK)]
-    moves += [(residual_ref, split * CHUNK, residual_first_ref, 0, CHUNK)]
     copies = [
-        pltpu.make_async_copy(ref.at[pl.ds(start, rows)], to.at[pl.ds(to_start, rows)], sems.at[at])
-        for at, (ref, start, to, to_start, rows) in enumerate(moves)
+        pltpu.make_async_copy(
+            ref.at[pl.ds(row_count - WINDOW + piece * part, part)],
+            edge_ref.at[pl.ds(at * WINDOW + piece * part, part)],
+            sems.at[at, piece],
+        )
+        for at, ref in enumerate((key_ref, value_ref))
+        for piece in range(4)
     ]
     for copy in copies:
         copy.start()
@@ -120,20 +104,18 @@
         copy.wait()
 
 
-def edge_rows(split, key_rows, value_rows, query_rows, residual):
+def edge_rows(key_rows, value_rows):
     width = key_rows.shape[1]
     return pl.pallas_call(
-        functools.partial(edge_kernel, split),
-        in_specs=[HBM] * 4,
-        out_specs=[VMEM] * 5,
-        out_shape=[shaped((2 * WINDOW, width), BF16)]
-        + [shaped((2 * CHUNK, width), BF16)] * 2
-        + [shaped((CHUNK, width), BF16)] * 2,
-        scratch_shapes=[pltpu.SemaphoreType.DMA((14,))],
+        edge_kernel,
+        in_specs=[HBM] * 2,
+        out_specs=VMEM,
+        out_shape=shaped((2 * WINDOW, width), BF16),
+        scratch_shapes=[pltpu.SemaphoreType.DMA((2, 4))],
         compiler_params=params(),
         cost_estimate=cost(0, 2**20),
         name="edge_rows",
-    )(*far_off(key_rows, value_rows, query_rows, residual))
+    )(*far_off(key_rows, value_rows))
 
 
 def lower_ones():
@@ -217,10 +199,6 @@
     key_ref,
     value_ref,
     residual_ref,
-    key_first_ref,
-    value_first_ref,
-    query_first_ref,
-    residual_first_ref,
     own_weight_ref,
     other_weight_ref,
     hidden_ref,
@@ -258,74 +236,65 @@
         rows = chunk_rows(chunk)
         return pltpu.make_async_copy(source.at[rows], early.at[rows], sems.at[which, chunk + chunks - split])
 
-    for chunk in range(split + 1, chunks):
+    for which in range(2):
+        copy_early(which, split - 1).start()
+    for chunk in range(split, chunks):
         for which in range(4):
             copy(which, chunk).start()
-    for chunk in range(split):
+    for which in range(2, 4):
+        copy_early(which, split - 1).start()
+    for chunk in range(split - 1):
         for which in range(4):
             copy_early(which, chunk).start()
-
-    def attend_one(chunk, query, key_before, key, value_before, value, residual):
-        attend_heads(
-            chunk_masks(pos_ref[pl.ds(chunk, 1), :]),
-            width,
-            query,
-            key_before,
-            key,
-            value_before,
-            value,
-            residual,
-            (hidden_ref, chunk_rows(chunk)),
-        )
-
-    whole = chunk_rows(0)
-    attend_one(
-        split,
-        (query_first_ref, whole),
-        (key_first_ref, whole),
-        (key_first_ref, chunk_rows(1)),
-        (value_first_ref, whole),
-        (value_first_ref, chunk_rows(1)),
-        (residual_first_ref, whole),
-    )
-    key_buf[:CHUNK, :] = key_first_ref[CHUNK:, :]
-    value_buf[:CHUNK, :] = value_first_ref[CHUNK:, :]
     is_low = half_index() == 0
     own_weight, other_weight = own_weight_ref[...], other_weight_ref[...]
     weight_ref[:half_width, :] = jnp.where(is_low, own_weight, other_weight)
     weight_ref[half_width:, :] = jnp.where(is_low, other_weight, own_weight)
 
-    def step(chunk, token):
+    def attend_one(chunk, key_before, value_before):
         for which in range(4):
             copy(which, chunk).wait()
-        rows, before = chunk_rows(chunk - split), chunk_rows(chunk - split - 1)
-        attend_one(
-            chunk,
+        rows = chunk_rows(chunk - split)
+        attend_heads(
+            chunk_masks(pos_ref[pl.ds(chunk, 1), :]),
+            width,
             (query_buf, rows),
-            (key_buf, before),
+            key_before,
             (key_buf, rows),
-            (value_buf, before),
+            value_before,
             (value_buf, rows),
             (residual_buf, rows),
+            (hidden_ref, chunk_rows(chunk)),
         )
+
+    for which in range(2):
+        copy_early(which, split - 1).wait()
+    last = chunk_rows(split - 1)
+    attend_one(split, (key_early_ref, last), (value_early_ref, last))
+
+    def step(chunk, token):
+        before = chunk_rows(chunk - split - 1)
+        attend_one(chunk, (key_buf, before), (value_buf, before))
         return token
 
     lax.fori_loop(split + 1, chunks, step, 0)
     shared = dot(hidden_ref[split * CHUNK :, :], weight_ref[...])
     b_ref[...] = shared[:, :STATES].astype(BF16)
     c_ref[split * CHUNK :, :] = shared[:, STATES:].astype(BF16)
-    for chunk in range(split):
+    for which in range(2, 4):
+        copy_early(which, split - 1).wait()
+    for chunk in range(split - 1):
         for which in range(4):
             copy_early(which, chunk).wait()
 
 
-def attend_late(split, positions, query, key, value, residual, firsts, weights):
+def attend_late(split, positions, query, key, value, residual, weights):
     row_count, width = query.shape
     chunks = row_count // CHUNK
     late = row_count - split * CHUNK
     return pl.pallas_call(
         functools.partial(late_kernel, split),
-        in_specs=[VMEM] + [HBM] * 4 + [VMEM] * 6,
+        in_specs=[VMEM] + [HBM] * 4 + [VMEM] * 2,
         out_specs=[VMEM] * 8,
         out_shape=[
             shaped((row_count, width), BF16),
@@ -341,7 +310,7 @@
     )(
         *near_by(positions),
         *far_off(query, key, value, residual),
-        *near_by(*firsts, *weights),
+        *near_by(*weights),
     )
 
 
@@ -569,24 +538,31 @@
     )(*near_by(own, other))
 
 
+def run_place(chunk, level=0):
+    return sum(bin(at).count("1") for at in range(chunk)) + bin(chunk & ((1 << level) - 1)).count("1")
+
+
 def runs_kernel(
     local_levels,
     turned_far_ref,
+    c_far_ref,
     codes_ref,
     hidden_ref,
     scaled_ref,
     rows_ref,
     wide_ref,
     runs_ref,
+    turned,
+    c_ref,
     hidden_far_ref,
-    turned,
     sems,
 ):
     row_count, width = scaled_ref.shape
     chunks = row_count // CHUNK
     turned_copy = pltpu.make_async_copy(turned_far_ref, turned, sems.at[chunks])
     turned_copy.start()
-    copies = []
+    copies = [pltpu.make_async_copy(c_far_ref, c_ref, sems.at[chunks + 1])]
+    copies[0].start()
     for chunk in range(chunks):
         rows = pl.ds(chunk * CHUNK, CHUNK)
         copies.append(pltpu.make_async_copy(hidden_ref.at[rows], hidden_far_ref.at[rows], sems.at[chunk]))
@@ -608,13 +584,9 @@
         held = {}
         for chunk in range(chunks):
             factor = rows_ref[chunk * 8 : (chunk + 1) * 8, lanes]
-            for level in range(local_levels):
-                start = (chunk * local_levels + level) * STATES
-                if level in held:
-                    run = (held[level] * factor[2:3]).astype(BF16)
-                else:
-                    run = jnp.zeros((STATES, tile), BF16)
-                runs_ref[start : start + STATES, lanes] = run
+            for level in sorted(held):
+                start = run_place(chunk, level) * STATES
+                runs_ref[start : start + STATES, lanes] = (held[level] * factor[2:3]).astype(BF16)
             if chunk == chunks - 1:
                 break
             span = slice(chunk * CHUNK, (chunk + 1) * CHUNK)
@@ -632,7 +604,7 @@
         copy.wait()
 
 
-def codes_and_runs(turned_far, codes_turned, hidden, scaled, factor_rows):
+def codes_and_runs(turned_far, c_far, codes_turned, hidden, scaled, factor_rows):
     row_count, width = scaled.shape
     levels = codes_turned.shape[0]
     levels += levels % 2
@@ -640,44 +612,35 @@
     local_levels = chunks.bit_length() - 1
     return pl.pallas_call(
         functools.partial(runs_kernel, local_levels),
-        in_specs=[HBM] + [VMEM] * 4,
-        out_specs=[VMEM, VMEM, HBM],
+        in_specs=[HBM] * 2 + [VMEM] * 4,
+        out_specs=[VMEM] * 4 + [HBM],
         out_shape=[
             shaped((row_count, levels * CHUNK), BF16),
-            shaped((chunks * local_levels * STATES, width), BF16),
+            shaped((max(1, run_place(chunks)) * STATES, width), BF16),
+            shaped(turned_far.shape, BF16),
+            shaped(c_far.shape, BF16),
             far_shaped(hidden.shape, BF16),
         ],
-        scratch_shapes=[pltpu.VMEM((STATES, row_count), BF16), pltpu.SemaphoreType.DMA((chunks + 1,))],
+        scratch_shapes=[pltpu.SemaphoreType.DMA((chunks + 2,))],
         compiler_params=params(),
         cost_estimate=cost(10**9, 10**7),
         name="codes_and_runs",
-    )(*far_off(turned_far), *near_by(codes_turned, hidden, scaled, factor_rows))
+    )(*far_off(turned_far, c_far), *near_by(codes_turned, hidden, scaled, factor_rows))
 
 
 def weights_kernel(
     local_levels,
     cross_levels,
     scale_ref,
-    turned_far_ref,
-    c_far_ref,
+    turned,
+    c_buf,
     c_other_ref,
     codes_ref,
     left_ref,
     early_reads_ref,
     last_reads_ref,
-    turned,
-    c_buf,
-    sems,
 ):
     row_count = c_other_ref.shape[0]
-    copies = [
-        pltpu.make_async_copy(turned_far_ref, turned, sems.at[0]),
-        pltpu.make_async_copy(c_far_ref, c_buf, sems.at[1]),
-    ]
-    for copy in copies:
-        copy.start()
-    for copy in copies:
-        copy.wait()
 
     query_row = lax.broadcasted_iota(jnp.int32, (CHUNK, CHUNK), 0)
     key_lane = lax.broadcasted_iota(jnp.int32, (CHUNK, CHUNK), 1)
@@ -710,27 +673,22 @@
     lax.fori_loop(0, row_count // CHUNK, step, 0)
 
 
-def level_products(scale, turned_far, c_far, c_other, codes_wide, cross_levels):
+def level_products(scale, b_turned, c_own, c_other, codes_wide, cross_levels):
     row_count = c_other.shape[0]
     local_levels = (row_count // CHUNK).bit_length() - 1
     return pl.pallas_call(
         functools.partial(weights_kernel, local_levels, cross_levels),
-        in_specs=[VMEM] + [HBM] * 2 + [VMEM] * 2,
+        in_specs=[VMEM] * 5,
         out_specs=[VMEM] * 3,
         out_shape=[
             shaped((row_count, (1 + local_levels) * STATES), BF16),
             shaped((row_count, (cross_levels - 1) * STATES), BF16),
             shaped((row_count, STATES), BF16),
         ],
-        scratch_shapes=[
-            pltpu.VMEM((STATES, row_count), BF16),
-            pltpu.VMEM((row_count, STATES), BF16),
-            pltpu.SemaphoreType.DMA((2,)),
-        ],
         compiler_params=params(),
         cost_estimate=cost(10**9, 10**7),
         name="level_products",
-    )(*near_by(scale), *far_off(turned_far, c_far), *near_by(c_other, codes_wide))
+    )(*near_by(scale, b_turned, c_own, c_other, codes_wide))
 
 
 def carried_state(message, before, upper):
@@ -782,19 +740,20 @@
     for lanes in tiles:
         crossed[:, lanes] = dot(early_reads_ref[...], carried[:, lanes]) * carry_ref[:, lanes].astype(F32)
 
-    def step(chunk, token):
-        rows = chunk_rows(chunk)
-        left = left_ref[rows, :]
-        run_rows = local_levels * STATES
-        runs = pl.ds(pl.multiple_of(chunk * run_rows, run_rows), run_rows)
+    for chunk in range(chunks):
+        rows = slice(chunk * CHUNK, (chunk + 1) * CHUNK)
+        levels = [level for level in range(local_levels) if chunk >> level & 1]
+        left = [left_ref[rows, :CHUNK]]
+        left += [left_ref[rows, (level + 1) * CHUNK : (level + 2) * CHUNK] for level in levels]
+        left = jnp.concatenate(left, axis=1)
+        runs = slice(run_place(chunk) * STATES, run_place(chunk + 1) * STATES)
         for lanes in tiles:
-            summed = dot(left, jnp.concatenate([scaled_ref[rows, lanes], runs_ref[runs, lanes]], axis=0))
+            right = scaled_ref[rows, lanes]
+            if levels:
+                right = jnp.concatenate([right, runs_ref[runs, lanes]], axis=0)
             local_ref[rows, lanes] = (
-                summed * fall_ref[rows, lanes].astype(F32) + crossed[rows, lanes]
+                dot(left, right) * fall_ref[rows, lanes].astype(F32) + crossed[rows, lanes]
             ).astype(BF16)
-        return token
-
-    lax.fori_loop(0, chunks, step, 0)
     for copy in copies:
         copy.wait()
 
@@ -931,12 +890,11 @@
 
     weights = (bc_weight, partner(bc_weight, "fsdp", 0))
     split = max(1, row_count // CHUNK // 4)
-    edge, *firsts = edge_rows(split, key_rows, value_rows, query_rows, residual_in)
-    edges = from_behind(edge, shard_axes, 1)
+    edges = from_behind(edge_rows(key_rows, value_rows), shard_axes, 1)
     pos_rows = positions.reshape(row_count // CHUNK, CHUNK)
     rate_turned = decay_rate.T
     hidden, c_mat, weight, b_late, *parts = attend_late(
-        split, pos_rows, query_rows, key_rows, value_rows, residual_in, firsts, weights
+        split, pos_rows, query_rows, key_rows, value_rows, residual_in, weights
     )
     late_own, late_other = summed_over_heads(b_late)
     hidden, c_mat, b_early = attend_early(split, pos_rows, edges, parts, weight, hidden, c_mat)
@@ -955,8 +913,8 @@
     for level in range(1, cross_levels):
         other = mirrored(joined) if level == cross_levels - 1 else partner(joined, "seq", level - 1)
         if level == 1:
-            codes_wide, runs, hidden_far = codes_and_runs(
-                turned_far, level_codes.T, hidden, scaled, factor_rows
+            codes_wide, runs, b_turned, c_own, hidden_far = codes_and_runs(
+                turned_far, c_far, level_codes.T, hidden, scaled, factor_rows
             )
             other, codes_wide = lax.optimization_barrier((other, codes_wide))
         received.append(other)
@@ -964,7 +922,7 @@
             joined = join(level, joined, other, half_width, level == cross_levels - 2)
             swapped.append(partner(other, "fsdp", 0))
     left, early_reads, last_reads = level_products(
-        level_scale[None, :], turned_far, c_far, c_other, codes_wide, cross_levels
+        level_scale[None, :], b_turned, c_own, c_other, codes_wide, cross_levels
     )
     local, hidden, before = local_terms(
         hidden_far, left, early_reads, scaled, fall, carry, runs, near, received[:-1], swapped

time: 41.6 us -> 40.5 us (0.974)
  Pallas kernels: 24.1 us -> 22.6 us
  waiting for transfers between devices: 4.25 us -> 5.3 us
  starting transfers between devices: 12.9 us -> 12.2 us
    pallas_call x1, Pallas kernels: 2.62 us -> 1.55 us  [level_products(): pl.pallas_call(functools.partial(weights_kernel, local_levels, cross_leve...]
    ppermute x1, waiting for transfers between devices: 0.01 us -> 0.72 us  [mirrored(): return lax.ppermute(x, 'seq', [(i, length - 1 - i) for i in range(length)])]
    pallas_call x1, Pallas kernels: 5.46 us -> 6.08 us  [attend_late(): pl.pallas_call(functools.partial(late_kernel, split), in_specs=[VMEM] + [...]
    pallas_call x1, Pallas kernels: 1.73 us -> 1.13 us  [edge_rows(): pl.pallas_call(edge_kernel, in_specs=[HBM] * 2, out_specs=VMEM, out_shape...]
    ppermute x1, starting transfers between devices: 2.83 us -> 2.32 us  [mirrored(): return lax.ppermute(x, 'seq', [(i, length - 1 - i) for i in range(length)])]
  transfers between devices with their start and end apart: 10 -> 10, of which waited for: 4 -> 5; matrix products, arithmetic and copies ran while one was open for 0% -> 0% of each run, Pallas kernels for 51% -> 48%
where the time goes in v6:
time: 40.5 us; the launch traced here: 40.3 us
  Pallas kernels  22.6 us (56%)
  starting transfers between devices  12.2 us (30%)
  waiting for transfers between devices  5.3 us (13%)
    ppermute x8, starting transfers between devices, partner(): lax.ppermute(x, axis, [(i, i ^ 1 << distance) for i in range(lax.axis_siz...  7.81 us
    pallas_call x1, Pallas kernels, attend_late(): pl.pallas_call(functools.partial(late_kernel, split), in_specs=[VMEM] + [...  6.08 us
    ppermute x8, waiting for transfers between devices, partner(): lax.ppermute(x, axis, [(i, i ^ 1 << distance) for i in range(lax.axis_siz...  4.57 us
    pallas_call x1, Pallas kernels, local_terms(): pl.pallas_call(functools.partial(local_kernel, local_levels, cross_levels...  3.23 us
    pallas_call x1, Pallas kernels, codes_and_runs(): pl.pallas_call(functools.partial(runs_kernel, local_levels), in_specs=[HB...  2.93 us
    pallas_call x2, Pallas kernels, finish(): pl.pallas_call(functools.partial(finish_kernel, swap, cross_levels), in_s...  2.56 us
    pallas_call x1, Pallas kernels, scale_hidden(): pl.pallas_call(scale_kernel, in_specs=[VMEM] * 3, out_specs=[VMEM] * 4 +...  2.4 us
    ppermute x1, starting transfers between devices, mirrored(): return lax.ppermute(x, 'seq', [(i, length - 1 - i) for i in range(length)])  2.32 us
  transfers between devices with their start and end apart: 10, of which 5 were waited for; matrix products, arithmetic and copies ran while one was open for 0% of the time, Pallas kernels for 48%

profile of v6, /device:TPU:0, one launch (start us, length us, event | category | flops | bytes accessed | tf_op | source)
XLA Modules:
  0.0 40.3 jit_solution(6892149914074247818)
XLA Ops:
  0.0 0.0 copy-start.3
  0.0 0.0 copy-start.5
  0.0 0.5 %collective-permute-start.1 = (bf16[512,256]{1,0:T(8,128)(2,1)}, bf16[512,256]{1,0:T(8,128)(2,1)S(1)}, u32[]{:S(2)}, u32[]{:S(2)}) collective-permute-start(bf16[512,256]{1,0:T(8,128)(2,1)} %own_weight_ref.1), channel_id=1, source_target_pairs={{0,1},{1,0},{2,3},{3,2},{4,5},{5,4},{6,7},{7,6},{8,9},{9,8},{10,11... | collective-permute-start | bytes 786440 | tf_op jit(solution)/shard_map/ppermute | solution.py:856
  0.5 1.1 %edge_rows.1 = bf16[256,1024]{1,0:T(8,128)(2,1)S(1)} custom-call(bf16[1024,1024]{1,0:T(8,128)(2,1)} %key_ref.3, bf16[1024,1024]{1,0:T(8,128)(2,1)} %value_ref.3), custom_call_target="tpu_custom_call" | custom-call | bytes 1048576 | tf_op jit(solution)/shard_map/edge_rows/pallas_call | solution.py:109
  1.6 2.0 %collective-permute-start = (bf16[256,1024]{1,0:T(8,128)(2,1)S(1)}, bf16[256,1024]{1,0:T(8,128)(2,1)S(1)}, u32[]{:S(2)}, u32[]{:S(2)}) collective-permute-start(bf16[256,1024]{1,0:T(8,128)(2,1)S(1)} %edge_rows.1), channel_id=1, source_target_pairs={{0,1},{1,4},{4,5},{5,8},{8,9},{9,12},{12,13},{2,3},{3,6},{6,7},{7,... | collective-permute-start | bytes 1572872 | tf_op jit(solution)/shard_map/ppermute | solution.py:852
  3.6 0.0 collective-permute-done.1.other_weight_ref
  3.6 0.0 copy-done.3
  3.6 0.0 copy-done.5
  3.7 6.1 %attention_late.1 = (bf16[1024,1024]{1,0:T(8,128)(2,1)S(1)}, bf16[1024,128]{1,0:T(8,128)(2,1)S(1)}, bf16[1024,256]{1,0:T(8,128)(2,1)S(1)}, bf16[768,128]{1,0:T(8...) custom-call(s32[8,128]{1,0:T(8,128)S(1)} %bitcast.10, ...), custom_call_target="tpu_custom_call" | custom-call | flops 6000000000 | bytes 10000000 | tf_op jit(solution)/shard_map/attention_late/pallas_call | solution.py:295
  9.7 3.0 %collective-permute-start.3 = (bf16[768,128]{1,0:T(8,128)(2,1)S(1)}, bf16[768,128]{1,0:T(8,128)(2,1)S(1)}, u32[]{:S(2)}, u32[]{:S(2)}) collective-permute-start(bf16[768,128]{1,0:T(8,128)(2,1)S(1)} %get-tuple-element.48.late_own_ref), channel_id=1, source_target_pairs={{0,2},{2,0},{1,3},{3,1},{4,6},{6,4},{5,7},{7,5},{8,10},{10,8},{9,1... | collective-permute-start | bytes 589832 | tf_op jit(solution)/shard_map/ppermute | solution.py:856
  12.7 0.0 collective-permute-done.edge_ref
  12.7 0.0 copy-start.4
  12.7 1.2 %attention_early.1 = (bf16[1024,1024]{1,0:T(8,128)(2,1)S(1)}, bf16[1024,128]{1,0:T(8,128)(2,1)S(1)}, bf16[256,128]{1,0:T(8,128)(2,1)S(1)}) custom-call(s32[8,128]{1,0:T(8,128)S(1)} %bitcast.11, bf16[256,1024]{1,0:T(8,128)(2,1)S(1)} %collective-permute-done.edge_ref, ...), custom_call_target="tpu_custom_call", output_to_operand_aliasing={{0}: (7, {}), {1}: (8, {})} | custom-call | flops 2000000000 | bytes 2000000 | tf_op jit(solution)/shard_map/attention_early/pallas_call | solution.py:362
  14.0 0.1 collective-permute-start.2
  14.1 0.0 copy-done.4
  14.1 2.4 %scale_hidden.1 = (bf16[1024,1024]{1,0:T(8,128)(2,1)S(1)}, f32[64,1024]{1,0:T(8,128)S(1)}, bf16[1024,1024]{1,0:T(8,128)(2,1)S(1)}, bf16[1024,1024]{1,0:T(8,128)(2,1)S(1)}, bf16[1024,128]{1,0:T(8,128)(2,1)}) custom-call(f32[16,1024]{1,0:T(8,128)S(1)} %bitcast.9, bf16[1024,1024]{1,0:T(8,128)(2,1)S(1)} %get-tuple-element.50.hidden_ref, ...), custom_call_target="tpu_custom_call" | custom-call | flops 1000000000 | bytes 4000000 | tf_op jit(solution)/shard_map/scale_hidden/pallas_call | solution.py:425
  16.5 0.0 copy-start
  16.5 1.3 %collective-permute-done.3.late_other_ref = bf16[768,128]{1,0:T(8,128)(2,1)S(1)} collective-permute-done((bf16[768,128]{1,0:T(8,128)(2,1)S(1)}, bf16[768,128]{1,0:T(8,128)(2,1)S(1)}, u32[]{:S(2)}, u32[]{:S(2)}) %collective-permute-start.3) | collective-permute-done | bytes 196640 | tf_op jit(solution)/shard_map/ppermute | solution.py:856
  17.8 1.4 %collective-permute-done.2.early_other_ref = bf16[256,128]{1,0:T(8,128)(2,1)S(1)} collective-permute-done((bf16[256,128]{1,0:T(8,128)(2,1)S(1)}, bf16[256,128]{1,0:T(8,128)(2,1)S(1)}, u32[]{:S(2)}, u32[]{:S(2)}) %collective-permute-start.2) | collective-permute-done | bytes 65568 | tf_op jit(solution)/shard_map/ppermute | solution.py:856
  19.2 1.4 %block_state.1 = (bf16[144,1024]{1,0:T(8,128)(2,1)S(1)}, bf16[128,1024]{1,0:T(8,128)(2,1)}) custom-call(bf16[256,128]{1,0:T(8,128)(2,1)S(1)} %get-tuple-element.47.early_own_ref, bf16[256,128]{1,0:T(8,128)(2,1)S(1)} %collective-permute-done.2.early_other_ref, bf16[768,128]{1,0:T(8,128)(2,1)S(1)} %get-tuple-element.48.late_own_ref, ...), custom_call_target="tpu_custom_call" | custom-call | flops 300000000 | bytes 4000000 | tf_op jit(solution)/shard_map/block_state/pallas_call | solution.py:501
  20.6 0.6 %collective-permute-start.4 = (bf16[144,1024]{1,0:T(8,128)(2,1)S(1)}, bf16[144,1024]{1,0:T(8,128)(2,1)S(1)}, u32[]{:S(2)}, u32[]{:S(2)}) collective-permute-start(bf16[144,1024]{1,0:T(8,128)(2,1)S(1)} %get-tuple-element.54.own_ref), channel_id=1, source_target_pairs={{0,1},{1,0},{2,3},{3,2},{4,5},{5,4},{6,7},{7,6},{8,9},{9,8},{10,11... | collective-permute-start | bytes 884744 | tf_op jit(solution)/shard_map/ppermute | solution.py:856
  21.2 2.1 %collective-permute-start.7 = (bf16[1024,128]{1,0:T(8,128)(2,1)S(1)}, bf16[1024,128]{1,0:T(8,128)(2,1)S(1)}, u32[]{:S(2)}, u32[]{:S(2)}) collective-permute-start(bf16[1024,128]{1,0:T(8,128)(2,1)S(1)} %get-tuple-element.62.c_ref), channel_id=1, source_target_pairs={{0,2},{2,0},{1,3},{3,1},{4,6},{6,4},{5,7},{7,5},{8,10},{10,8},{9,1... | collective-permute-start | bytes 786440 | tf_op jit(solution)/shard_map/ppermute | solution.py:856
  23.3 0.0 collective-permute-done.4.other_ref.near_ref
  23.3 0.1 join_runs.2.own_ref
  23.3 1.6 %collective-permute-start.5 = (bf16[144,512]{1,0:T(8,128)(2,1)S(1)}, bf16[144,512]{1,0:T(8,128)(2,1)S(1)}, u32[]{:S(2)}, u32[]{:S(2)}) collective-permute-start(bf16[144,512]{1,0:T(8,128)(2,1)S(1)} %join_runs.2.own_ref), channel_id=1, source_target_pairs={{0,4},{4,0},{8,12},{12,8},{1,5},{5,1},{9,13},{13,9},{2,6},{6,2},{1... | collective-permute-start | bytes 442376 | tf_op jit(solution)/shard_map/ppermute | solution.py:856
  24.9 0.0 copy-done
  24.9 0.0 copy-start.2
  24.9 2.9 %codes_and_runs.1 = (bf16[1024,2304]{1,0:T(8,128)(2,1)S(1)}, bf16[1536,1024]{1,0:T(8,128)(2,1)S(1)}, bf16[128,1024]{1,0:T(8,128)(2,1)S(1)}, bf16[1024,128]{1,0:T(8,128)(2,1)S(1)}, bf16[1024,1024]{1,0:T(8,128)(2,1)}) custom-call(bf16[128,1024]{1,0:T(8,128)(2,1)} %get-tuple-element.55.turned_far_ref, bf16[1024,128]{1,0:T(8,128)(2,1)} %get-tuple-element.56.c_far_ref, ...), custom_call_target="tpu_custom_call" | custom-call | flops 1000000000 | bytes 10000000 | tf_op jit(solution)/shard_map/codes_and_runs/pallas_call | solution.py:613
  27.9 1.4 %collective-permute-done.5.other_ref.refs_0_ = bf16[144,512]{1,0:T(8,128)(2,1)S(1)} collective-permute-done((bf16[144,512]{1,0:T(8,128)(2,1)S(1)}, bf16[144,512]{1,0:T(8,128)(2,1)S(1)}, u32[]{:S(2)}, u32[]{:S(2)}) %collective-permute-start.5) | collective-permute-done | bytes 147488 | tf_op jit(solution)/shard_map/ppermute | solution.py:856
  29.2 0.0 collective-permute-start.8
  29.3 0.1 join_runs.3
  29.3 2.3 %collective-permute-start.6 = (bf16[128,512]{1,0:T(8,128)(2,1)S(1)}, bf16[128,512]{1,0:T(8,128)(2,1)S(1)}, u32[]{:S(2)}, u32[]{:S(2)}) collective-permute-start(bf16[128,512]{1,0:T(8,128)(2,1)S(1)} %join_runs.3), channel_id=1, source_target_pairs={{0,12},{4,8},{8,4},{12,0},{1,13},{5,9},{9,5},{13,1},{2,14},{6,10},... | collective-permute-start | bytes 393224 | tf_op jit(solution)/shard_map/ppermute | solution.py:861
  31.6 0.0 collective-permute-done.7.c_other_ref
  31.6 0.0 copy-done.2
  31.6 1.6 %level_products.1 = (bf16[1024,512]{1,0:T(8,128)(2,1)S(1)}, bf16[1024,256]{1,0:T(8,128)(2,1)S(1)}, bf16[1024,128]{1,0:T(8,128)(2,1)S(1)}) custom-call(f32[1,18]{1,0:T(1,128)S(1)} %bitcast.8, bf16[128,1024]{1,0:T(8,128)(2,1)S(1)} %get-tuple-element.60.turned, bf16[1024,128]{1,0:T(8,128)(2,1)S(1)} %get-tuple-element.61.c_buf, ...), custom_call_target="tpu_custom_call" | custom-call | flops 1000000000 | bytes 10000000 | tf_op jit(solution)/shard_map/level_products/pallas_call | solution.py:679
  33.2 0.0 collective-permute-done.8.refs_1_
  33.2 0.0 copy-start.1
  33.2 3.2 %local_terms.1 = (bf16[1024,1024]{1,0:T(8,128)(2,1)S(1)}, bf16[1024,1024]{1,0:T(8,128)(2,1)S(1)}, f32[8,1024]{1,0:T(8,128)S(1)}) custom-call(bf16[1024,1024]{1,0:T(8,128)(2,1)} %get-tuple-element.59.hidden_far_ref, bf16[1024,512]{1,0:T(8,128)(2,1)S(1)} %get-tuple-element.64.left_ref, bf16[1024,256]{1,0:T(8,128)(2,1)S(1)} %get-tuple-element.65.early_reads_ref, ...), custom_call_target="tpu_custom_call" | custom-call | flops 3000000000 | bytes 10000000 | tf_op jit(solution)/shard_map/local_terms/pallas_call | solution.py:765
  36.5 0.7 %collective-permute-done.6.message_ref = bf16[128,512]{1,0:T(8,128)(2,1)S(1)} collective-permute-done((bf16[128,512]{1,0:T(8,128)(2,1)S(1)}, bf16[128,512]{1,0:T(8,128)(2,1)S(1)}, u32[]{:S(2)}, u32[]{:S(2)}) %collective-permute-start.6) | collective-permute-done | bytes 131104 | tf_op jit(solution)/shard_map/ppermute | solution.py:861
  37.2 0.0 collective-permute-start.9
  37.2 0.0 copy-done.1
  37.2 0.8 %carried_and_norm.2.refs_0_ = bf16[1024,512]{1,0:T(8,128)(2,1)S(1)} custom-call(bf16[128,512]{1,0:T(8,128)(2,1)S(1)} %collective-permute-done.6.message_ref, f32[8,1024]{1,0:T(8,128)S(1)} %get-tuple-element.71.before_ref, bf16[1024,1024]{1,0:T(8,128)(2,1)S(1)} %get-tuple-element.72.hidden_ref, bf16[1024,128]{1,0:T(8,128)(2,1)S(1)} %get-tuple-element.73.reads_ref, ...), custom_call_target="tpu_custom_call" | custom-call | flops 2000000000 | bytes 8000000 | tf_op jit(solution)/shard_map/carried_and_norm/pallas_call | solution.py:833
  38.0 0.5 %collective-permute-done.9.message_ref = bf16[128,512]{1,0:T(8,128)(2,1)S(1)} collective-permute-done((bf16[128,512]{1,0:T(8,128)(2,1)S(1)}, bf16[128,512]{1,0:T(8,128)(2,1)S(1)}, u32[]{:S(2)}, u32[]{:S(2)}) %collective-permute-start.9) | collective-permute-done | bytes 131104 | tf_op jit(solution)/shard_map/ppermute | solution.py:856
  38.5 1.7 %carried_and_norm.3 = bf16[1024,1024]{1,0:T(8,128)(2,1)} custom-call(bf16[128,512]{1,0:T(8,128)(2,1)S(1)} %collective-permute-done.9.message_ref, f32[8,1024]{1,0:T(8,128)S(1)} %get-tuple-element.71.before_ref, bf16[1024,1024]{1,0:T(8,128)(2,1)S(1)} %get-tuple-element.72.hidden_ref, bf16[1024,128]{1,0:T(8,128)(2,1)S(1)} %get-tuple-element.73.reads_ref, ...), custom_call_target="tpu_custom_call" | custom-call | flops 2000000000 | bytes 8000000 | tf_op jit(solution)/shard_map/carried_and_norm/pallas_call | solution.py:833
Async XLA Ops:
  0.0 3.6 %copy-start.3 = (bf16[512,256]{1,0:T(8,128)(2,1)S(1)}, bf16[512,256]{1,0:T(8,128)(2,1)}, u32[]{:S(2)}) copy-start(bf16[512,256]{1,0:T(8,128)(2,1)} %own_weight_ref.1) | copy-start | bytes 786436
  0.0 3.6 %copy-start.5 = (s32[1024]{0:T(1024)S(1)}, s32[1024]{0:T(1024)}, u32[]{:S(2)}) copy-start(s32[1024]{0:T(1024)} %param.18) | copy-start | bytes 12292
  0.0 3.6 %collective-permute-start.1 = (bf16[512,256]{1,0:T(8,128)(2,1)}, bf16[512,256]{1,0:T(8,128)(2,1)S(1)}, u32[]{:S(2)}, u32[]{:S(2)}) collective-permute-start(bf16[512,256]{1,0:T(8,128)(2,1)} %own_weight_ref.1), channel_id=1, source_target_pairs={{0,1},{1,0},{2,3},{3,2},{4,5},{5,4},{6,7},{7,6},{8,9},{9,8},{10,11... | collective-permute-start | bytes 786440 | tf_op jit(solution)/shard_map/ppermute | solution.py:856
  1.6 11.1 %collective-permute-start = (bf16[256,1024]{1,0:T(8,128)(2,1)S(1)}, bf16[256,1024]{1,0:T(8,128)(2,1)S(1)}, u32[]{:S(2)}, u32[]{:S(2)}) collective-permute-start(bf16[256,1024]{1,0:T(8,128)(2,1)S(1)} %edge_rows.1), channel_id=1, source_target_pairs={{0,1},{1,4},{4,5},{5,8},{8,9},{9,12},{12,13},{2,3},{3,6},{6,7},{7,... | collective-permute-start | bytes 1572872 | tf_op jit(solution)/shard_map/ppermute | solution.py:852
  9.7 8.0 %collective-permute-start.3 = (bf16[768,128]{1,0:T(8,128)(2,1)S(1)}, bf16[768,128]{1,0:T(8,128)(2,1)S(1)}, u32[]{:S(2)}, u32[]{:S(2)}) collective-permute-start(bf16[768,128]{1,0:T(8,128)(2,1)S(1)} %get-tuple-element.48.late_own_ref), channel_id=1, source_target_pairs={{0,2},{2,0},{1,3},{3,1},{4,6},{6,4},{5,7},{7,5},{8,10},{10,8},{9,1... | collective-permute-start | bytes 589832 | tf_op jit(solution)/shard_map/ppermute | solution.py:856
  12.7 1.3 %copy-start.4 = (f32[1024,16]{0,1:T(8,128)S(1)}, f32[1024,16]{0,1:T(8,128)}, u32[]{:S(2)}) copy-start(f32[1024,16]{0,1:T(8,128)} %param.15) | copy-start | bytes 196612
  14.0 5.2 %collective-permute-start.2 = (bf16[256,128]{1,0:T(8,128)(2,1)S(1)}, bf16[256,128]{1,0:T(8,128)(2,1)S(1)}, u32[]{:S(2)}, u32[]{:S(2)}) collective-permute-start(bf16[256,128]{1,0:T(8,128)(2,1)S(1)} %get-tuple-element.47.early_own_ref), channel_id=1, source_target_pairs={{0,2},{2,0},{1,3},{3,1},{4,6},{6,4},{5,7},{7,5},{8,10},{10,8},{9,1... | collective-permute-start | bytes 196616 | tf_op jit(solution)/shard_map/ppermute | solution.py:856
  16.5 8.5 %copy-start = (s32[1024,18]{0,1:T(8,128)S(1)}, s32[1024,18]{0,1:T(8,128)}, u32[]{:S(2)}) copy-start(s32[1024,18]{0,1:T(8,128)} %param.16) | copy-start | bytes 221188
  20.6 2.7 %collective-permute-start.4 = (bf16[144,1024]{1,0:T(8,128)(2,1)S(1)}, bf16[144,1024]{1,0:T(8,128)(2,1)S(1)}, u32[]{:S(2)}, u32[]{:S(2)}) collective-permute-start(bf16[144,1024]{1,0:T(8,128)(2,1)S(1)} %get-tuple-element.54.own_ref), channel_id=1, source_target_pairs={{0,1},{1,0},{2,3},{3,2},{4,5},{5,4},{6,7},{7,6},{8,9},{9,8},{10,11... | collective-permute-start | bytes 884744 | tf_op jit(solution)/shard_map/ppermute | solution.py:856
  21.2 10.5 %collective-permute-start.7 = (bf16[1024,128]{1,0:T(8,128)(2,1)S(1)}, bf16[1024,128]{1,0:T(8,128)(2,1)S(1)}, u32[]{:S(2)}, u32[]{:S(2)}) collective-permute-start(bf16[1024,128]{1,0:T(8,128)(2,1)S(1)} %get-tuple-element.62.c_ref), channel_id=1, source_target_pairs={{0,2},{2,0},{1,3},{3,1},{4,6},{6,4},{5,7},{7,5},{8,10},{10,8},{9,1... | collective-permute-start | bytes 786440 | tf_op jit(solution)/shard_map/ppermute | solution.py:856
  23.3 5.9 %collective-permute-start.5 = (bf16[144,512]{1,0:T(8,128)(2,1)S(1)}, bf16[144,512]{1,0:T(8,128)(2,1)S(1)}, u32[]{:S(2)}, u32[]{:S(2)}) collective-permute-start(bf16[144,512]{1,0:T(8,128)(2,1)S(1)} %join_runs.2.own_ref), channel_id=1, source_target_pairs={{0,4},{4,0},{8,12},{12,8},{1,5},{5,1},{9,13},{13,9},{2,6},{6,2},{1... | collective-permute-start | bytes 442376 | tf_op jit(solution)/shard_map/ppermute | solution.py:856
  24.9 6.7 %copy-start.2 = (f32[18]{0:T(128)S(1)}, f32[18]{0:T(128)}, u32[]{:S(2)}) copy-start(f32[18]{0:T(128)} %param.17) | copy-start | bytes 220
  29.2 4.0 %collective-permute-start.8 = (bf16[144,512]{1,0:T(8,128)(2,1)S(1)}, bf16[144,512]{1,0:T(8,128)(2,1)S(1)}, u32[]{:S(2)}, u32[]{:S(2)}) collective-permute-start(bf16[144,512]{1,0:T(8,128)(2,1)S(1)} %collective-permute-done.5.other_ref.refs_0_), channel_id=1, source_target_pairs={{0,1},{1,0},{2,3},{3,2},{4,5},{5,4},{6,7},{7,6},{8,9},{9,8},{10,11... | collective-permute-start | bytes 442376 | tf_op jit(solution)/shard_map/ppermute | solution.py:856
  29.3 7.9 %collective-permute-start.6 = (bf16[128,512]{1,0:T(8,128)(2,1)S(1)}, bf16[128,512]{1,0:T(8,128)(2,1)S(1)}, u32[]{:S(2)}, u32[]{:S(2)}) collective-permute-start(bf16[128,512]{1,0:T(8,128)(2,1)S(1)} %join_runs.3), channel_id=1, source_target_pairs={{0,12},{4,8},{8,4},{12,0},{1,13},{5,9},{9,5},{13,1},{2,14},{6,10},... | collective-permute-start | bytes 393224 | tf_op jit(solution)/shard_map/ppermute | solution.py:861
  33.2 4.0 %copy-start.1 = (f32[1024]{0:T(1024)S(1)}, f32[1024]{0:T(1024)}, u32[]{:S(2)}) copy-start(f32[1024]{0:T(1024)} %param.19) | copy-start | bytes 12292
  37.2 1.3 %collective-permute-start.9 = (bf16[128,512]{1,0:T(8,128)(2,1)S(1)}, bf16[128,512]{1,0:T(8,128)(2,1)S(1)}, u32[]{:S(2)}, u32[]{:S(2)}) collective-permute-start(bf16[128,512]{1,0:T(8,128)(2,1)S(1)} %collective-permute-done.6.message_ref), channel_id=1, source_target_pairs={{0,1},{1,0},{2,3},{3,2},{4,5},{5,4},{6,7},{7,6},{8,9},{9,8},{10,11... | collective-permute-start | bytes 393224 | tf_op jit(solution)/shard_map/ppermute | solution.py:856

commit v7 on v6

--- a/solution.py
+++ b/solution.py
@@ -738,7 +738,7 @@
     before_ref[...] = jnp.broadcast_to(before, before_ref.shape)
     tiles = lane_tiles(width)
     for lanes in tiles:
-        crossed[:, lanes] = dot(early_reads_ref[...], carried[:, lanes]) * carry_ref[:, lanes].astype(F32)
+        crossed[:, lanes] = dot(early_reads_ref[...], carried[:, lanes]).astype(BF16) * carry_ref[:, lanes]
 
     for chunk in range(chunks):
         rows = slice(chunk * CHUNK, (chunk + 1) * CHUNK)
@@ -752,7 +752,7 @@
             if levels:
                 right = jnp.concatenate([right, runs_ref[runs, lanes]], axis=0)
             local_ref[rows, lanes] = (
-                dot(left, right) * fall_ref[rows, lanes].astype(F32) + crossed[rows, lanes]
+                dot(left, right) * fall_ref[rows, lanes].astype(F32) + crossed[rows, lanes].astype(F32)
             ).astype(BF16)
     for copy in copies:
         copy.wait()
@@ -769,7 +769,7 @@
         out_shape=[shaped((row_count, width), BF16)] * 2 + [shaped((8, width), F32)],
         scratch_shapes=[
             pltpu.VMEM(((cross_levels - 1) * STATES, width), BF16),
-            pltpu.VMEM((row_count, width), F32),
+            pltpu.VMEM((row_count, width), BF16),
             pltpu.SemaphoreType.DMA((row_count // CHUNK,)),
         ],
         compiler_params=params(),
@@ -814,13 +814,22 @@
         lanes = pl.ds(pl.multiple_of(start + at * tile, tile), tile)
         here = slice(at * tile, (at + 1) * tile)
         carried = carried_state(message_ref[:, here], before_ref[0:1, lanes], upper)
-        cross = dot(reads_ref[...], carried).astype(BF16)
-        mixed = local_ref[:, lanes] + cross * carry_ref[:, lanes]
-        mean = dot(mixed * mixed, mean_mat)
-        normed = mixed * lax.rsqrt(mean + 1e-05).astype(BF16) * gain_ref[:, lanes].astype(BF16)
-        result[:, here] = hidden_ref[:, lanes] + normed
-        if swap:
-            copy_out(result, here, lanes, 1 + at)
+        blocks = 2 if swap else 1
+        for block in range(blocks):
+            rows = slice(block * (row_count // blocks), (block + 1) * (row_count // blocks))
+            cross = dot(reads_ref[rows, :], carried).astype(BF16)
+            mixed = local_ref[rows, lanes] + cross * carry_ref[rows, lanes]
+            mean = dot(mixed * mixed, mean_mat)
+            normed = mixed * lax.rsqrt(mean + 1e-05).astype(BF16) * gain_ref[:, lanes].astype(BF16)
+            result[rows, here] = hidden_ref[rows, lanes] + normed
+            if swap:
+                span = pl.ds(block * (row_count // blocks), row_count // blocks)
+                copies.append(
+                    pltpu.make_async_copy(
+                        result.at[span, here], out_ref.at[span, lanes], sems.at[1 + at, block]
+                    )
+                )
+                copies[-1].start()
     for copy in copies:
         copy.wait()
 

time: 40.5 us -> 40.4 us (level)
  no operation moved by 1% of the time
where the time goes in v7:
time: 40.4 us; the launch traced here: 40.2 us
  Pallas kernels  22.5 us (56%)
  starting transfers between devices  12.2 us (30%)
  waiting for transfers between devices  5.39 us (13%)
    ppermute x8, starting transfers between devices, partner(): lax.ppermute(x, axis, [(i, i ^ 1 << distance) for i in range(lax.axis_siz...  7.81 us
    pallas_call x1, Pallas kernels, attend_late(): pl.pallas_call(functools.partial(late_kernel, split), in_specs=[VMEM] + [...  6.08 us
    ppermute x8, waiting for transfers between devices, partner(): lax.ppermute(x, axis, [(i, i ^ 1 << distance) for i in range(lax.axis_siz...  4.57 us
    pallas_call x1, Pallas kernels, local_terms(): pl.pallas_call(functools.partial(local_kernel, local_levels, cross_levels...  3.14 us
    pallas_call x1, Pallas kernels, codes_and_runs(): pl.pallas_call(functools.partial(runs_kernel, local_levels), in_specs=[HB...  2.93 us
    pallas_call x2, Pallas kernels, finish(): pl.pallas_call(functools.partial(finish_kernel, swap, cross_levels), in_s...  2.48 us
    pallas_call x1, Pallas kernels, scale_hidden(): pl.pallas_call(scale_kernel, in_specs=[VMEM] * 3, out_specs=[VMEM] * 4 +...  2.4 us
    ppermute x1, starting transfers between devices, mirrored(): return lax.ppermute(x, 'seq', [(i, length - 1 - i) for i in range(length)])  2.32 us
  transfers between devices with their start and end apart: 10, of which 5 were waited for; matrix products, arithmetic and copies ran while one was open for 0% of the time, Pallas kernels for 48%

profile of v7, /device:TPU:0, one launch (start us, length us, event | category | flops | bytes accessed | tf_op | source)
XLA Modules:
  0.0 40.2 jit_solution(7888132393243776775)
XLA Ops:
  0.0 0.0 copy-start.3
  0.0 0.0 copy-start.5
  0.0 0.5 %collective-permute-start.1 = (bf16[512,256]{1,0:T(8,128)(2,1)}, bf16[512,256]{1,0:T(8,128)(2,1)S(1)}, u32[]{:S(2)}, u32[]{:S(2)}) collective-permute-start(bf16[512,256]{1,0:T(8,128)(2,1)} %own_weight_ref.1), channel_id=1, source_target_pairs={{0,1},{1,0},{2,3},{3,2},{4,5},{5,4},{6,7},{7,6},{8,9},{9,8},{10,11... | collective-permute-start | bytes 786440 | tf_op jit(solution)/shard_map/ppermute | solution.py:865
  0.5 1.1 %edge_rows.1 = bf16[256,1024]{1,0:T(8,128)(2,1)S(1)} custom-call(bf16[1024,1024]{1,0:T(8,128)(2,1)} %key_ref.3, bf16[1024,1024]{1,0:T(8,128)(2,1)} %value_ref.3), custom_call_target="tpu_custom_call" | custom-call | bytes 1048576 | tf_op jit(solution)/shard_map/edge_rows/pallas_call | solution.py:109
  1.6 2.0 %collective-permute-start = (bf16[256,1024]{1,0:T(8,128)(2,1)S(1)}, bf16[256,1024]{1,0:T(8,128)(2,1)S(1)}, u32[]{:S(2)}, u32[]{:S(2)}) collective-permute-start(bf16[256,1024]{1,0:T(8,128)(2,1)S(1)} %edge_rows.1), channel_id=1, source_target_pairs={{0,1},{1,4},{4,5},{5,8},{8,9},{9,12},{12,13},{2,3},{3,6},{6,7},{7,... | collective-permute-start | bytes 1572872 | tf_op jit(solution)/shard_map/ppermute | solution.py:861
  3.6 0.0 collective-permute-done.1.other_weight_ref
  3.6 0.0 copy-done.3
  3.6 0.0 copy-done.5
  3.7 6.1 %attention_late.1 = (bf16[1024,1024]{1,0:T(8,128)(2,1)S(1)}, bf16[1024,128]{1,0:T(8,128)(2,1)S(1)}, bf16[1024,256]{1,0:T(8,128)(2,1)S(1)}, bf16[768,128]{1,0:T(8...) custom-call(s32[8,128]{1,0:T(8,128)S(1)} %bitcast.10, ...), custom_call_target="tpu_custom_call" | custom-call | flops 6000000000 | bytes 10000000 | tf_op jit(solution)/shard_map/attention_late/pallas_call | solution.py:295
  9.7 3.0 %collective-permute-start.3 = (bf16[768,128]{1,0:T(8,128)(2,1)S(1)}, bf16[768,128]{1,0:T(8,128)(2,1)S(1)}, u32[]{:S(2)}, u32[]{:S(2)}) collective-permute-start(bf16[768,128]{1,0:T(8,128)(2,1)S(1)} %get-tuple-element.48.late_own_ref), channel_id=1, source_target_pairs={{0,2},{2,0},{1,3},{3,1},{4,6},{6,4},{5,7},{7,5},{8,10},{10,8},{9,1... | collective-permute-start | bytes 589832 | tf_op jit(solution)/shard_map/ppermute | solution.py:865
  12.7 0.0 collective-permute-done.edge_ref
  12.7 0.0 copy-start.4
  12.7 1.2 %attention_early.1 = (bf16[1024,1024]{1,0:T(8,128)(2,1)S(1)}, bf16[1024,128]{1,0:T(8,128)(2,1)S(1)}, bf16[256,128]{1,0:T(8,128)(2,1)S(1)}) custom-call(s32[8,128]{1,0:T(8,128)S(1)} %bitcast.11, bf16[256,1024]{1,0:T(8,128)(2,1)S(1)} %collective-permute-done.edge_ref, ...), custom_call_target="tpu_custom_call", output_to_operand_aliasing={{0}: (7, {}), {1}: (8, {})} | custom-call | flops 2000000000 | bytes 2000000 | tf_op jit(solution)/shard_map/attention_early/pallas_call | solution.py:362
  14.0 0.1 collective-permute-start.2
  14.1 0.0 copy-done.4
  14.1 2.4 %scale_hidden.1 = (bf16[1024,1024]{1,0:T(8,128)(2,1)S(1)}, f32[64,1024]{1,0:T(8,128)S(1)}, bf16[1024,1024]{1,0:T(8,128)(2,1)S(1)}, bf16[1024,1024]{1,0:T(8,128)(2,1)S(1)}, bf16[1024,128]{1,0:T(8,128)(2,1)}) custom-call(f32[16,1024]{1,0:T(8,128)S(1)} %bitcast.9, bf16[1024,1024]{1,0:T(8,128)(2,1)S(1)} %get-tuple-element.50.hidden_ref, ...), custom_call_target="tpu_custom_call" | custom-call | flops 1000000000 | bytes 4000000 | tf_op jit(solution)/shard_map/scale_hidden/pallas_call | solution.py:425
  16.5 0.0 copy-start
  16.5 1.3 %collective-permute-done.3.late_other_ref = bf16[768,128]{1,0:T(8,128)(2,1)S(1)} collective-permute-done((bf16[768,128]{1,0:T(8,128)(2,1)S(1)}, bf16[768,128]{1,0:T(8,128)(2,1)S(1)}, u32[]{:S(2)}, u32[]{:S(2)}) %collective-permute-start.3) | collective-permute-done | bytes 196640 | tf_op jit(solution)/shard_map/ppermute | solution.py:865
  17.8 1.4 %collective-permute-done.2.early_other_ref = bf16[256,128]{1,0:T(8,128)(2,1)S(1)} collective-permute-done((bf16[256,128]{1,0:T(8,128)(2,1)S(1)}, bf16[256,128]{1,0:T(8,128)(2,1)S(1)}, u32[]{:S(2)}, u32[]{:S(2)}) %collective-permute-start.2) | collective-permute-done | bytes 65568 | tf_op jit(solution)/shard_map/ppermute | solution.py:865
  19.2 1.4 %block_state.1 = (bf16[144,1024]{1,0:T(8,128)(2,1)S(1)}, bf16[128,1024]{1,0:T(8,128)(2,1)}) custom-call(bf16[256,128]{1,0:T(8,128)(2,1)S(1)} %get-tuple-element.47.early_own_ref, bf16[256,128]{1,0:T(8,128)(2,1)S(1)} %collective-permute-done.2.early_other_ref, bf16[768,128]{1,0:T(8,128)(2,1)S(1)} %get-tuple-element.48.late_own_ref, ...), custom_call_target="tpu_custom_call" | custom-call | flops 300000000 | bytes 4000000 | tf_op jit(solution)/shard_map/block_state/pallas_call | solution.py:501
  20.6 0.6 %collective-permute-start.4 = (bf16[144,1024]{1,0:T(8,128)(2,1)S(1)}, bf16[144,1024]{1,0:T(8,128)(2,1)S(1)}, u32[]{:S(2)}, u32[]{:S(2)}) collective-permute-start(bf16[144,1024]{1,0:T(8,128)(2,1)S(1)} %get-tuple-element.54.own_ref), channel_id=1, source_target_pairs={{0,1},{1,0},{2,3},{3,2},{4,5},{5,4},{6,7},{7,6},{8,9},{9,8},{10,11... | collective-permute-start | bytes 884744 | tf_op jit(solution)/shard_map/ppermute | solution.py:865
  21.2 2.1 %collective-permute-start.7 = (bf16[1024,128]{1,0:T(8,128)(2,1)S(1)}, bf16[1024,128]{1,0:T(8,128)(2,1)S(1)}, u32[]{:S(2)}, u32[]{:S(2)}) collective-permute-start(bf16[1024,128]{1,0:T(8,128)(2,1)S(1)} %get-tuple-element.62.c_ref), channel_id=1, source_target_pairs={{0,2},{2,0},{1,3},{3,1},{4,6},{6,4},{5,7},{7,5},{8,10},{10,8},{9,1... | collective-permute-start | bytes 786440 | tf_op jit(solution)/shard_map/ppermute | solution.py:865
  23.3 0.0 collective-permute-done.4.other_ref.near_ref
  23.3 0.1 join_runs.2.own_ref
  23.3 1.6 %collective-permute-start.5 = (bf16[144,512]{1,0:T(8,128)(2,1)S(1)}, bf16[144,512]{1,0:T(8,128)(2,1)S(1)}, u32[]{:S(2)}, u32[]{:S(2)}) collective-permute-start(bf16[144,512]{1,0:T(8,128)(2,1)S(1)} %join_runs.2.own_ref), channel_id=1, source_target_pairs={{0,4},{4,0},{8,12},{12,8},{1,5},{5,1},{9,13},{13,9},{2,6},{6,2},{1... | collective-permute-start | bytes 442376 | tf_op jit(solution)/shard_map/ppermute | solution.py:865
  24.9 0.0 copy-done
  24.9 0.0 copy-start.2
  24.9 2.9 %codes_and_runs.1 = (bf16[1024,2304]{1,0:T(8,128)(2,1)S(1)}, bf16[1536,1024]{1,0:T(8,128)(2,1)S(1)}, bf16[128,1024]{1,0:T(8,128)(2,1)S(1)}, bf16[1024,128]{1,0:T(8,128)(2,1)S(1)}, bf16[1024,1024]{1,0:T(8,128)(2,1)}) custom-call(bf16[128,1024]{1,0:T(8,128)(2,1)} %get-tuple-element.55.turned_far_ref, bf16[1024,128]{1,0:T(8,128)(2,1)} %get-tuple-element.56.c_far_ref, ...), custom_call_target="tpu_custom_call" | custom-call | flops 1000000000 | bytes 10000000 | tf_op jit(solution)/shard_map/codes_and_runs/pallas_call | solution.py:613
  27.9 1.4 %collective-permute-done.5.other_ref.refs_0_ = bf16[144,512]{1,0:T(8,128)(2,1)S(1)} collective-permute-done((bf16[144,512]{1,0:T(8,128)(2,1)S(1)}, bf16[144,512]{1,0:T(8,128)(2,1)S(1)}, u32[]{:S(2)}, u32[]{:S(2)}) %collective-permute-start.5) | collective-permute-done | bytes 147488 | tf_op jit(solution)/shard_map/ppermute | solution.py:865
  29.2 0.0 collective-permute-start.8
  29.3 0.1 join_runs.3
  29.3 2.3 %collective-permute-start.6 = (bf16[128,512]{1,0:T(8,128)(2,1)S(1)}, bf16[128,512]{1,0:T(8,128)(2,1)S(1)}, u32[]{:S(2)}, u32[]{:S(2)}) collective-permute-start(bf16[128,512]{1,0:T(8,128)(2,1)S(1)} %join_runs.3), channel_id=1, source_target_pairs={{0,12},{4,8},{8,4},{12,0},{1,13},{5,9},{9,5},{13,1},{2,14},{6,10},... | collective-permute-start | bytes 393224 | tf_op jit(solution)/shard_map/ppermute | solution.py:870
  31.6 0.0 collective-permute-done.7.c_other_ref
  31.6 0.0 copy-done.2
  31.6 1.6 %level_products.1 = (bf16[1024,512]{1,0:T(8,128)(2,1)S(1)}, bf16[1024,256]{1,0:T(8,128)(2,1)S(1)}, bf16[1024,128]{1,0:T(8,128)(2,1)S(1)}) custom-call(f32[1,18]{1,0:T(1,128)S(1)} %bitcast.8, bf16[128,1024]{1,0:T(8,128)(2,1)S(1)} %get-tuple-element.60.turned, bf16[1024,128]{1,0:T(8,128)(2,1)S(1)} %get-tuple-element.61.c_buf, ...), custom_call_target="tpu_custom_call" | custom-call | flops 1000000000 | bytes 10000000 | tf_op jit(solution)/shard_map/level_products/pallas_call | solution.py:679
  33.2 0.0 collective-permute-done.8.refs_1_
  33.2 0.0 copy-start.1
  33.2 3.1 %local_terms.1 = (bf16[1024,1024]{1,0:T(8,128)(2,1)S(1)}, bf16[1024,1024]{1,0:T(8,128)(2,1)S(1)}, f32[8,1024]{1,0:T(8,128)S(1)}) custom-call(bf16[1024,1024]{1,0:T(8,128)(2,1)} %get-tuple-element.59.hidden_far_ref, bf16[1024,512]{1,0:T(8,128)(2,1)S(1)} %get-tuple-element.64.left_ref, bf16[1024,256]{1,0:T(8,128)(2,1)S(1)} %get-tuple-element.65.early_reads_ref, ...), custom_call_target="tpu_custom_call" | custom-call | flops 3000000000 | bytes 10000000 | tf_op jit(solution)/shard_map/local_terms/pallas_call | solution.py:765
  36.4 0.8 %collective-permute-done.6.message_ref = bf16[128,512]{1,0:T(8,128)(2,1)S(1)} collective-permute-done((bf16[128,512]{1,0:T(8,128)(2,1)S(1)}, bf16[128,512]{1,0:T(8,128)(2,1)S(1)}, u32[]{:S(2)}, u32[]{:S(2)}) %collective-permute-start.6) | collective-permute-done | bytes 131104 | tf_op jit(solution)/shard_map/ppermute | solution.py:870
  37.2 0.0 collective-permute-start.9
  37.2 0.0 copy-done.1
  37.2 0.8 %carried_and_norm.2.refs_0_ = bf16[1024,512]{1,0:T(8,128)(2,1)S(1)} custom-call(bf16[128,512]{1,0:T(8,128)(2,1)S(1)} %collective-permute-done.6.message_ref, f32[8,1024]{1,0:T(8,128)S(1)} %get-tuple-element.71.before_ref, bf16[1024,1024]{1,0:T(8,128)(2,1)S(1)} %get-tuple-element.72.hidden_ref, bf16[1024,128]{1,0:T(8,128)(2,1)S(1)} %get-tuple-element.73.reads_ref, ...), custom_call_target="tpu_custom_call" | custom-call | flops 2000000000 | bytes 8000000 | tf_op jit(solution)/shard_map/carried_and_norm/pallas_call | solution.py:842
  38.0 0.5 %collective-permute-done.9.message_ref = bf16[128,512]{1,0:T(8,128)(2,1)S(1)} collective-permute-done((bf16[128,512]{1,0:T(8,128)(2,1)S(1)}, bf16[128,512]{1,0:T(8,128)(2,1)S(1)}, u32[]{:S(2)}, u32[]{:S(2)}) %collective-permute-start.9) | collective-permute-done | bytes 131104 | tf_op jit(solution)/shard_map/ppermute | solution.py:865
  38.5 1.6 %carried_and_norm.3 = bf16[1024,1024]{1,0:T(8,128)(2,1)} custom-call(bf16[128,512]{1,0:T(8,128)(2,1)S(1)} %collective-permute-done.9.message_ref, f32[8,1024]{1,0:T(8,128)S(1)} %get-tuple-element.71.before_ref, bf16[1024,1024]{1,0:T(8,128)(2,1)S(1)} %get-tuple-element.72.hidden_ref, bf16[1024,128]{1,0:T(8,128)(2,1)S(1)} %get-tuple-element.73.reads_ref, ...), custom_call_target="tpu_custom_call" | custom-call | flops 2000000000 | bytes 8000000 | tf_op jit(solution)/shard_map/carried_and_norm/pallas_call | solution.py:842
Async XLA Ops:
  0.0 3.6 %copy-start.3 = (bf16[512,256]{1,0:T(8,128)(2,1)S(1)}, bf16[512,256]{1,0:T(8,128)(2,1)}, u32[]{:S(2)}) copy-start(bf16[512,256]{1,0:T(8,128)(2,1)} %own_weight_ref.1) | copy-start | bytes 786436
  0.0 3.6 %copy-start.5 = (s32[1024]{0:T(1024)S(1)}, s32[1024]{0:T(1024)}, u32[]{:S(2)}) copy-start(s32[1024]{0:T(1024)} %param.18) | copy-start | bytes 12292
  0.0 3.6 %collective-permute-start.1 = (bf16[512,256]{1,0:T(8,128)(2,1)}, bf16[512,256]{1,0:T(8,128)(2,1)S(1)}, u32[]{:S(2)}, u32[]{:S(2)}) collective-permute-start(bf16[512,256]{1,0:T(8,128)(2,1)} %own_weight_ref.1), channel_id=1, source_target_pairs={{0,1},{1,0},{2,3},{3,2},{4,5},{5,4},{6,7},{7,6},{8,9},{9,8},{10,11... | collective-permute-start | bytes 786440 | tf_op jit(solution)/shard_map/ppermute | solution.py:865
  1.6 11.1 %collective-permute-start = (bf16[256,1024]{1,0:T(8,128)(2,1)S(1)}, bf16[256,1024]{1,0:T(8,128)(2,1)S(1)}, u32[]{:S(2)}, u32[]{:S(2)}) collective-permute-start(bf16[256,1024]{1,0:T(8,128)(2,1)S(1)} %edge_rows.1), channel_id=1, source_target_pairs={{0,1},{1,4},{4,5},{5,8},{8,9},{9,12},{12,13},{2,3},{3,6},{6,7},{7,... | collective-permute-start | bytes 1572872 | tf_op jit(solution)/shard_map/ppermute | solution.py:861
  9.7 8.0 %collective-permute-start.3 = (bf16[768,128]{1,0:T(8,128)(2,1)S(1)}, bf16[768,128]{1,0:T(8,128)(2,1)S(1)}, u32[]{:S(2)}, u32[]{:S(2)}) collective-permute-start(bf16[768,128]{1,0:T(8,128)(2,1)S(1)} %get-tuple-element.48.late_own_ref), channel_id=1, source_target_pairs={{0,2},{2,0},{1,3},{3,1},{4,6},{6,4},{5,7},{7,5},{8,10},{10,8},{9,1... | collective-permute-start | bytes 589832 | tf_op jit(solution)/shard_map/ppermute | solution.py:865
  12.7 1.3 %copy-start.4 = (f32[1024,16]{0,1:T(8,128)S(1)}, f32[1024,16]{0,1:T(8,128)}, u32[]{:S(2)}) copy-start(f32[1024,16]{0,1:T(8,128)} %param.15) | copy-start | bytes 196612
  14.0 5.2 %collective-permute-start.2 = (bf16[256,128]{1,0:T(8,128)(2,1)S(1)}, bf16[256,128]{1,0:T(8,128)(2,1)S(1)}, u32[]{:S(2)}, u32[]{:S(2)}) collective-permute-start(bf16[256,128]{1,0:T(8,128)(2,1)S(1)} %get-tuple-element.47.early_own_ref), channel_id=1, source_target_pairs={{0,2},{2,0},{1,3},{3,1},{4,6},{6,4},{5,7},{7,5},{8,10},{10,8},{9,1... | collective-permute-start | bytes 196616 | tf_op jit(solution)/shard_map/ppermute | solution.py:865
  16.5 8.5 %copy-start = (s32[1024,18]{0,1:T(8,128)S(1)}, s32[1024,18]{0,1:T(8,128)}, u32[]{:S(2)}) copy-start(s32[1024,18]{0,1:T(8,128)} %param.16) | copy-start | bytes 221188
  20.6 2.7 %collective-permute-start.4 = (bf16[144,1024]{1,0:T(8,128)(2,1)S(1)}, bf16[144,1024]{1,0:T(8,128)(2,1)S(1)}, u32[]{:S(2)}, u32[]{:S(2)}) collective-permute-start(bf16[144,1024]{1,0:T(8,128)(2,1)S(1)} %get-tuple-element.54.own_ref), channel_id=1, source_target_pairs={{0,1},{1,0},{2,3},{3,2},{4,5},{5,4},{6,7},{7,6},{8,9},{9,8},{10,11... | collective-permute-start | bytes 884744 | tf_op jit(solution)/shard_map/ppermute | solution.py:865
  21.2 10.5 %collective-permute-start.7 = (bf16[1024,128]{1,0:T(8,128)(2,1)S(1)}, bf16[1024,128]{1,0:T(8,128)(2,1)S(1)}, u32[]{:S(2)}, u32[]{:S(2)}) collective-permute-start(bf16[1024,128]{1,0:T(8,128)(2,1)S(1)} %get-tuple-element.62.c_ref), channel_id=1, source_target_pairs={{0,2},{2,0},{1,3},{3,1},{4,6},{6,4},{5,7},{7,5},{8,10},{10,8},{9,1... | collective-permute-start | bytes 786440 | tf_op jit(solution)/shard_map/ppermute | solution.py:865
  23.3 5.9 %collective-permute-start.5 = (bf16[144,512]{1,0:T(8,128)(2,1)S(1)}, bf16[144,512]{1,0:T(8,128)(2,1)S(1)}, u32[]{:S(2)}, u32[]{:S(2)}) collective-permute-start(bf16[144,512]{1,0:T(8,128)(2,1)S(1)} %join_runs.2.own_ref), channel_id=1, source_target_pairs={{0,4},{4,0},{8,12},{12,8},{1,5},{5,1},{9,13},{13,9},{2,6},{6,2},{1... | collective-permute-start | bytes 442376 | tf_op jit(solution)/shard_map/ppermute | solution.py:865
  24.9 6.7 %copy-start.2 = (f32[18]{0:T(128)S(1)}, f32[18]{0:T(128)}, u32[]{:S(2)}) copy-start(f32[18]{0:T(128)} %param.17) | copy-start | bytes 220
  29.2 4.0 %collective-permute-start.8 = (bf16[144,512]{1,0:T(8,128)(2,1)S(1)}, bf16[144,512]{1,0:T(8,128)(2,1)S(1)}, u32[]{:S(2)}, u32[]{:S(2)}) collective-permute-start(bf16[144,512]{1,0:T(8,128)(2,1)S(1)} %collective-permute-done.5.other_ref.refs_0_), channel_id=1, source_target_pairs={{0,1},{1,0},{2,3},{3,2},{4,5},{5,4},{6,7},{7,6},{8,9},{9,8},{10,11... | collective-permute-start | bytes 442376 | tf_op jit(solution)/shard_map/ppermute | solution.py:865
  29.3 7.9 %collective-permute-start.6 = (bf16[128,512]{1,0:T(8,128)(2,1)S(1)}, bf16[128,512]{1,0:T(8,128)(2,1)S(1)}, u32[]{:S(2)}, u32[]{:S(2)}) collective-permute-start(bf16[128,512]{1,0:T(8,128)(2,1)S(1)} %join_runs.3), channel_id=1, source_target_pairs={{0,12},{4,8},{8,4},{12,0},{1,13},{5,9},{9,5},{13,1},{2,14},{6,10},... | collective-permute-start | bytes 393224 | tf_op jit(solution)/shard_map/ppermute | solution.py:870
  33.2 4.0 %copy-start.1 = (f32[1024]{0:T(1024)S(1)}, f32[1024]{0:T(1024)}, u32[]{:S(2)}) copy-start(f32[1024]{0:T(1024)} %param.19) | copy-start | bytes 12292
  37.2 1.3 %collective-permute-start.9 = (bf16[128,512]{1,0:T(8,128)(2,1)S(1)}, bf16[128,512]{1,0:T(8,128)(2,1)S(1)}, u32[]{:S(2)}, u32[]{:S(2)}) collective-permute-start(bf16[128,512]{1,0:T(8,128)(2,1)S(1)} %collective-permute-done.6.message_ref), channel_id=1, source_target_pairs={{0,1},{1,0},{2,3},{3,2},{4,5},{5,4},{6,7},{7,6},{8,9},{9,8},{10,11... | collective-permute-start | bytes 393224 | tf_op jit(solution)/shard_map/ppermute | solution.py:865
